TPU v7x, 32 devices: a whole 2x2x4 slice. The times are simulated.
32 devices in a mesh: tok: 4 (over x, core), exp: 8 (over z, y).
Axes of the slice: x: 2, y: 2, z: 4, core: 2. Of those that a mesh axis runs over, the one named last changes fastest.
Arguments:
- tokens: float32 [3072, 1280], P('tok', 'exp'), may hold values from -6 to 6
- out_grad: float32 [3072, 1280], P('tok', 'exp'), may hold values from -6 to 6
- slot_proj: bfloat16 [1280, 2048], P(None, 'exp'), may hold values from -2 to 2
- weight_in: bfloat16 [8, 1280, 5120], P('exp', None, 'tok'), may hold values from -0.15625 to 0.15625
- weight_out: bfloat16 [8, 5120, 1280], P('exp', 'tok'), may hold values from -0.078125 to 0.078125
- slot_norm: float32 [2048], P('exp'), may hold values from -1 to 6
- token_norm: float32 [3072], P('tok'), may hold values from -1 to 6
Outputs:
- grad_tokens: float32 [3072, 1280], P('tok', 'exp')
- grad_slot_proj: float32 [1280, 2048], P('tok', 'exp')
- grad_weight_in: float32 [8, 1280, 5120], P('exp', None, 'tok')
- grad_weight_out: float32 [8, 5120, 1280], P('exp', 'tok')
All inputs are finite; a program needn't handle non-finite values.
Results may differ from a plain program's by a relative error of at most 0.012.
The roundings to bfloat16 on the way count: a program that leaves them out, or rounds other values in their place, can miss the bound.
Values may be sent and summed in bfloat16 or wider, within the bound.
No kernel may reach another device: no remote copies, remote signals or barrier semaphores. Data moves between devices by JAX's collectives and lax.ppermute only.
A program may use at most 64 MiB of HBM per device.

v0:
```python
import jax
import jax.numpy as jnp
from jax import lax
from jax.sharding import PartitionSpec as P

GELU_C = 0.7978845608028654


def gelu_parts(pre_act):
    inner = GELU_C * (pre_act + 0.044715 * pre_act**3)
    tangent = jnp.tanh(inner)
    value = 0.5 * pre_act * (1.0 + tangent)
    slope = 0.5 * (1.0 + tangent) + 0.5 * pre_act * (1.0 - tangent * tangent) * GELU_C * (
        1.0 + 3.0 * 0.044715 * pre_act * pre_act
    )
    return (value, slope)


def local(tokens, out_grad, slot_proj, weight_in, weight_out, slot_norm, token_norm):
    tok_rows, grad_rows = (
        lax.all_gather(tokens.astype(jnp.bfloat16), "exp", axis=1, tiled=True),
        lax.all_gather(out_grad.astype(jnp.bfloat16), "exp", axis=1, tiled=True),
    )
    width = tok_rows.shape[1]
    slot_total = slot_proj.shape[1]
    local_experts = weight_in.shape[0]
    slot_count = slot_total // local_experts
    tok_total = tok_rows.shape[0] * lax.axis_size("tok")
    all_slots = slot_total * lax.axis_size("exp")
    logits = jnp.dot(tok_rows, slot_proj, preferred_element_type=jnp.float32)
    dispatch = jnp.exp(logits - slot_norm[None, :]) / jnp.float32(tok_total)
    combine = jnp.exp(logits - token_norm[:, None]) / jnp.float32(all_slots)
    dispatch_half = dispatch.astype(jnp.bfloat16)
    combine_half = combine.astype(jnp.bfloat16)
    slot_in_part = jnp.einsum(
        "ns,nd->sd", dispatch_half, tok_rows, preferred_element_type=jnp.float32
    )
    slot_grad_part = jnp.einsum(
        "ns,nd->sd", combine_half, grad_rows, preferred_element_type=jnp.float32
    )
    slot_in, slot_grad = lax.psum((slot_in_part, slot_grad_part), "tok")
    slot_in_half = slot_in.reshape(local_experts, slot_count, width).astype(jnp.bfloat16)
    pre_act = jnp.einsum(
        "esd,edf->esf", slot_in_half, weight_in, preferred_element_type=jnp.float32
    )
    gelu_out, gelu_slope = gelu_parts(pre_act)
    hidden = gelu_out.astype(jnp.bfloat16)
    slot_out_part = jnp.einsum(
        "esf,efd->esd", hidden, weight_out, preferred_element_type=jnp.float32
    )
    slot_out = lax.psum(slot_out_part, "tok")
    slot_out_half = slot_out.reshape(slot_total, width).astype(jnp.bfloat16)
    slot_grad_half = slot_grad.reshape(local_experts, slot_count, width).astype(jnp.bfloat16)
    grad_weight_out = jnp.einsum(
        "esf,esd->efd", hidden, slot_grad_half, preferred_element_type=jnp.float32
    )
    hidden_grad = jnp.einsum(
        "esd,efd->esf", slot_grad_half, weight_out, preferred_element_type=jnp.float32
    )
    pre_grad = (hidden_grad * gelu_slope).astype(jnp.bfloat16)
    grad_weight_in = jnp.einsum(
        "esd,esf->edf", slot_in_half, pre_grad, preferred_element_type=jnp.float32
    )
    slot_in_grad_part = jnp.einsum(
        "esf,edf->esd", pre_grad, weight_in, preferred_element_type=jnp.float32
    )
    slot_in_grad = lax.psum(slot_in_grad_part, "tok")
    slot_in_grad_half = slot_in_grad.reshape(slot_total, width).astype(jnp.bfloat16)
    comb_grad = jnp.einsum(
        "nd,sd->ns", grad_rows, slot_out_half, preferred_element_type=jnp.float32
    )
    row_part = jnp.sum(combine * comb_grad, axis=1)
    disp_grad = jnp.einsum(
        "nd,sd->ns", tok_rows, slot_in_grad_half, preferred_element_type=jnp.float32
    )
    col_stat = jnp.sum(slot_in * slot_in_grad_half.astype(jnp.float32), axis=1)
    disp_part = dispatch * (disp_grad - col_stat[None, :])
    inner_grad = (combine * comb_grad + disp_part).astype(jnp.bfloat16)
    direct_term = jnp.einsum(
        "ns,sd->nd", dispatch_half, slot_in_grad_half, preferred_element_type=jnp.float32
    )
    row_stat = lax.psum(row_part, "exp")
    token_term = jnp.einsum("ns,ds->nd", inner_grad, slot_proj, preferred_element_type=jnp.float32)
    token_term = token_term - row_stat[:, None] * jnp.einsum(
        "ns,ds->nd", combine_half, slot_proj, preferred_element_type=jnp.float32
    )
    token_term = token_term + direct_term
    grad_tokens = lax.psum_scatter(token_term, "exp", scatter_dimension=1, tiled=True)
    logit_grad = (combine * (comb_grad - row_stat[:, None]) + disp_part).astype(jnp.bfloat16)
    proj_part = jnp.einsum("nd,ns->ds", tok_rows, logit_grad, preferred_element_type=jnp.float32)
    grad_slot_proj = lax.psum_scatter(proj_part, "tok", scatter_dimension=0, tiled=True)
    return (grad_tokens, grad_slot_proj, grad_weight_in, grad_weight_out)


def solution(mesh):
    return jax.shard_map(
        local,
        mesh=mesh,
        in_specs=(
            P("tok", "exp"),
            P("tok", "exp"),
            P(None, "exp"),
            P("exp", None, "tok"),
            P("exp", "tok", None),
            P("exp"),
            P("tok"),
        ),
        out_specs=(P("tok", "exp"), P("tok", "exp"), P("exp", None, "tok"), P("exp", "tok", None)),
        check_vma=False,
    )
```

profile of v0, /device:TPU:0, one launch (start us, length us, event | category | flops | bytes accessed | tf_op | source)
XLA Modules:
  0.0 378.0 jit_solution(13233165193195597924)
XLA Ops:
  7.2 0.0 copy-start
  7.2 0.0 all-gather.3.cloned.1.call-start
  7.2 1.9 convert_element_type.49
  9.1 0.0 all-gather.3.cloned.1.call-update
  9.1 0.0 all-gather.5.cloned.1.call-start
  9.2 1.8 convert_element_type.55
  11.0 0.0 all-gather.5.cloned.1.call-update
  11.0 0.0 copy-start.18
  11.0 0.0 all-reduce.5.cloned.1.call-start
  11.0 50.0 %all-gather.3.cloned.1.call-done = bf16[768,1280]{0,1:T(8,128)(2,1)} async-done(((bf16[768,160]{0,1:T(8,128)(2,1)}), bf16[768,1280]{0,1:T(8,128)(2,1)}) %all-gather.3.cloned.1.call-update) | async-done | bytes 1966096 | tf_op jit(solution)/shard_map/all_gather | solution.py:21
  61.0 3.3 fusion.61
  64.3 46.1 %all-gather.5.cloned.1.call-done = bf16[768,1280]{0,1:T(8,128)(2,1)} async-done(((bf16[768,160]{0,1:T(8,128)(2,1)}), bf16[768,1280]{0,1:T(8,128)(2,1)}) %all-gather.5.cloned.1.call-update) | async-done | bytes 1966096 | tf_op jit(solution)/shard_map/all_gather | solution.py:22
  110.4 0.0 copy-done.18
  110.4 3.7 fusion.50
  114.1 0.0 copy-done.19
  114.1 0.0 copy-done.1
  114.1 0.0 copy-done.4
  114.1 1.8 fusion.59
  116.0 0.0 all-reduce.5.cloned.1.call-update
  116.0 0.0 reduce-scatter.7.cloned.1.call-start
  116.0 40.7 %all-reduce.6 = bf16[256,1280]{1,0:T(8,128)(2,1)} all-reduce(f32[256,1280]{1,0:T(8,128)} %fusion.50), channel_id=1, replica_groups=mesh['tok'=4,'exp'=8] {'tok'}, use_global_device_ids=true, to_apply=%region_2.0 | all-reduce | flops 327680 | bytes 1966080 | tf_op jit(solution)/shard_map/psum | solution.py:41
  156.8 8.5 %all-reduce.5.cloned.1.call-done = f32[256,1280]{1,0:T(8,128)} async-done(((f32[256,1280]{1,0:T(8,128)}), f32[256,1280]{1,0:T(8,128)}) %all-reduce.5.cloned.1.call-update) | async-done | bytes 1310736 | tf_op jit(solution)/shard_map/psum | solution.py:41
  165.3 3.3 fusion.8
  168.7 0.0 copy-done
  168.7 0.0 copy-start.6
  168.7 0.0 copy-start.15
  168.7 2.3 fusion.16
  171.0 0.0 copy-done.6
  171.0 0.0 copy-done.15
  171.0 1.3 fusion.19
  172.3 0.0 copy-start.17
  172.4 0.8 copy-done.17
  173.2 0.0 copy-done.13
  173.2 2.1 fusion.13
  175.3 50.6 %all-reduce.7 = (bf16[1,256,1280]{2,1,0:T(8,128)(2,1)}, bf16[1,256,1280]{2,1,0:T(8,128)(2,1)}) all-reduce(f32[1,256,1280]{2,1,0:T(8,128)} %fusion.13, f32[1,256,1280]{2,1,0:T(8,128)} %fusion.16), channel_id=1, replica_groups=mesh['tok'=4,'exp'=8] {'tok'}, use_global_device_ids=true, to_apply=%region_3.0 | all-reduce | flops 655360 | bytes 3932160 | tf_op jit(solution)/shard_map/psum | solution.py:67
  225.9 3.6 fusion.47
  229.5 19.2 %psum.39 = f32[768]{0:T(1024)S(1)} all-reduce(f32[768]{0:T(1024)S(1)} %get-tuple-element.14), channel_id=1, replica_groups=mesh['tok'=4,'exp'=8] {'exp'}, use_global_device_ids=true, to_apply=%region_6.0 | all-reduce | flops 768 | bytes 6144 | tf_op jit(solution)/shard_map/psum | solution.py:82
  248.7 1.8 multiply_reduce_fusion
  250.5 0.0 copy-done.2
  250.5 0.1 copy-done.12
  250.6 2.4 fusion.30
  253.0 0.0 copy-start.10
  253.0 0.9 copy-done.10
  253.8 0.0 copy-done.5
  253.8 0.0 copy-done.8
  253.8 1.8 convolution_bitcast_fusion.2
  255.7 2.8 copy.13
  258.5 0.0 reduce-scatter.7.cloned.1.call-update
  258.5 0.2 reduce-scatter.5.cloned.1.call-start
  258.7 0.0 copy-start.3
  258.7 0.0 copy-start.9
  258.8 0.0 copy-start.11
  258.8 0.0 copy-start.14
  258.8 2.3 fusion.31
  261.1 0.0 copy-done.3
  261.1 0.8 fusion.39
  261.9 2.6 fusion.1
  264.5 0.0 reduce-scatter.5.cloned.1.call-update
  264.5 0.0 copy-start.7
  264.5 0.0 copy-start.16
  264.6 5.5 %convolution_bitcast_fusion.1 = f32[1,1280,1280]{2,1,0:T(8,128)} fusion(bf16[256,1280]{1,0:T(8,128)(2,1)} %copy-done.17, f32[256,1280]{1,0:T(8,128)} %all-reduce.5.cloned.1.call-done), kind=kOutput, calls=%fused_computation.1 | convolution fusion | flops 839188480 | bytes 8519680 | tf_op jit(solution)/shard_map/esd,esf->edf/dot_general | solution.py:61
  270.1 4.2 %convolution_bitcast_fusion = f32[1,1280,1280]{2,1,0:T(8,128)} fusion(bf16[256,1280]{1,0:T(8,128)(2,1)S(1)} %copy-done.16, f32[256,1280]{1,0:T(8,128)S(1)} %copy-done.7), kind=kOutput, calls=%fused_computation | convolution fusion | flops 841809920 | bytes 8519680 | tf_op jit(solution)/shard_map/esf,esd->efd/dot_general | solution.py:54
  274.2 8.3 %reduce-scatter.7.cloned.1.call-done = f32[320,256]{1,0:T(8,128)} async-done(((f32[1280,256]{1,0:T(8,128)}), f32[320,256]{1,0:T(8,128)}) %reduce-scatter.7.cloned.1.call-update) | async-done | bytes 327696
  282.6 88.9 %reduce-scatter.5.cloned.1.call-done = f32[768,160]{0,1:T(8,128)} async-done(((f32[768,1280]{0,1:T(8,128)}), f32[768,160]{0,1:T(8,128)}) %reduce-scatter.5.cloned.1.call-update) | async-done | bytes 491536 | tf_op jit(solution)/shard_map/reduce_scatter | solution.py:88
  (13 shorter events, 0.0 us)
Async XLA Ops:
  7.2 161.5 %copy-start = (bf16[1,1280,1280]{2,1,0:T(8,128)(2,1)S(1)}, bf16[1,1280,1280]{2,1,0:T(8,128)(2,1)}, u32[]{:S(2)}) copy-start(bf16[1,1280,1280]{2,1,0:T(8,128)(2,1)} %param.11) | copy-start | bytes 9830404
  7.2 53.8 %all-gather.3.cloned.1.call-start = ((), (), s32[]{:S(2)}) async-start(), calls=%async_computation.2 | async-start | bytes 2211840 | tf_op jit(solution)/shard_map/all_gather | solution.py:21
  9.1 101.3 %all-gather.5.cloned.1.call-start = ((), (), s32[]{:S(2)}) async-start(), calls=%async_computation.4 | async-start | bytes 2211840 | tf_op jit(solution)/shard_map/all_gather | solution.py:22
  11.0 99.4 %copy-start.18 = (f32[768]{0:T(1024)S(1)}, f32[768]{0:T(1024)}, u32[]{:S(2)}) copy-start(f32[768]{0:T(1024)} %param.13) | copy-start | bytes 9220
  11.0 154.3 %all-reduce.5.cloned.1.call-start = ((), (), s32[]{:S(2)}) async-start(), calls=%async_computation.3 | async-start | bytes 2621440 | tf_op jit(solution)/shard_map/psum | solution.py:41
  64.3 49.8 %copy-start.19 = (f32[256]{0:T(256)S(1)}, f32[256]{0:T(256)}, u32[]{:S(2)}) copy-start(f32[256]{0:T(256)} %param.12) | copy-start | bytes 3076
  110.4 3.7 copy-start.1
  110.4 3.7 copy-start.4
  116.0 166.6 %reduce-scatter.7.cloned.1.call-start = ((), (), s32[]{:S(2)}) async-start(), calls=%async_computation.6 | async-start | bytes 1638400
  168.7 2.3 copy-start.6
  168.7 2.3 copy-start.15
  171.0 2.2 copy-start.13
  172.3 0.8 copy-start.17
  248.6 1.8 copy-start.2
  248.6 1.9 copy-start.12
  250.6 3.3 copy-start.5
  250.6 3.3 copy-start.8
  253.0 0.9 copy-start.10
  258.5 113.0 %reduce-scatter.5.cloned.1.call-start = ((), (), s32[]{:S(2)}) async-start(), calls=%async_computation.5 | async-start | bytes 4423680 | tf_op jit(solution)/shard_map/reduce_scatter | solution.py:88
  258.7 2.3 copy-start.3
  258.7 2.3 copy-start.9
  258.8 2.3 copy-start.11
  258.8 2.3 copy-start.14
  264.5 5.5 %copy-start.7 = (f32[256,1280]{1,0:T(8,128)S(1)}, f32[256,1280]{1,0:T(8,128)}, u32[]{:S(2)}) copy-start(f32[256,1280]{1,0:T(8,128)} %copy-done.6) | copy-start | bytes 3932164
  264.5 5.5 %copy-start.16 = (bf16[256,1280]{1,0:T(8,128)(2,1)S(1)}, bf16[256,1280]{1,0:T(8,128)(2,1)}, u32[]{:S(2)}) copy-start(bf16[256,1280]{1,0:T(8,128)(2,1)} %all-reduce.6) | copy-start | bytes 1966084
Sparse Core Ops, SparseCore 0:
  10.8 50.2 all-gather.2
  63.8 46.5 all-gather.4
  116.1 49.1 all-reduce.4
  258.6 23.8 reduce-scatter.6
  287.1 84.3 reduce-scatter.4
where the time goes:
time: 378 us
  waiting for transfers between devices  202 us (53%)
  blocking collectives  111 us (29%)
  matrix products  41.1 us (11%)
  between operations  14 us (4%)
  other arithmetic  5.45 us (1%)
  local copies, waits for them, and re-layouts  4.68 us (1%)
    reduce_scatter x1, waiting for transfers between devices, local(): lax.psum_scatter(token_term, 'exp', scatter_dimension=1, tiled=True)  88.9 us
    psum x1, blocking collectives, local(): slot_in_grad = lax.psum(slot_in_grad_part, 'tok')  50.6 us
    all_gather x1, waiting for transfers between devices, local(): lax.all_gather(tokens.astype(jnp.bfloat16), 'exp', axis=1, tiled=True)  50 us
    all_gather x1, waiting for transfers between devices, local(): lax.all_gather(out_grad.astype(jnp.bfloat16), 'exp', axis=1, tiled=True)  46.1 us
    psum x1, blocking collectives, local(): slot_in, slot_grad = lax.psum((slot_in_part, slot_grad_part), 'tok')  40.7 us
    psum x1, blocking collectives, local(): row_stat = lax.psum(row_part, 'exp')  19.2 us
    psum x1, waiting for transfers between devices, local(): slot_in, slot_grad = lax.psum((slot_in_part, slot_grad_part), 'tok')  8.54 us
    unnamed x6, waiting for transfers between devices  8.41 us
  transfers between devices with their start and end apart: 5, of which 5 were waited for; matrix products, arithmetic and copies ran while one was open for 5% of the time, Pallas kernels for 0%

commit v1 on v0

v1 whole, which is shorter than its diff:
```python
import jax
import jax.numpy as jnp
from jax import lax
from jax.sharding import PartitionSpec as P

GELU_C = 0.7978845608028654
BF16 = jnp.bfloat16
F32 = jnp.float32


def gelu_parts(pre_act):
    inner = GELU_C * (pre_act + 0.044715 * pre_act**3)
    tangent = jnp.tanh(inner)
    value = 0.5 * pre_act * (1.0 + tangent)
    slope = 0.5 * (1.0 + tangent) + 0.5 * pre_act * (1.0 - tangent * tangent) * GELU_C * (
        1.0 + 3.0 * 0.044715 * pre_act * pre_act
    )
    return (value, slope)


def swap(x, axis, k):
    n = lax.axis_size(axis)
    return lax.ppermute(x, axis, [(i, i ^ k) for i in range(n)])


def split_of(n):
    bits = n.bit_length() - 1
    return 1 << (bits // 2)


def gather_exp(block):
    n = lax.axis_size("exp")
    inner = split_of(n)
    held = {0: block}
    for ko in range(inner, n, inner):
        held[ko] = swap(block, "exp", ko)
    for ko in range(0, n, inner):
        for ki in range(1, inner):
            held[ko + ki] = swap(held[ko], "exp", ki)
    return [held[k] for k in range(n)]


def scatter_exp(blocks):
    n = lax.axis_size("exp")
    inner = split_of(n)
    sums = {}
    for ko in reversed(range(0, n, inner)):
        total = blocks[ko]
        for ki in range(1, inner):
            total = total + swap(blocks[ko + ki].astype(BF16), "exp", ki).astype(F32)
        sums[ko] = total
    out = sums[0]
    for ko in reversed(range(inner, n, inner)):
        out = out + swap(sums[ko].astype(BF16), "exp", ko).astype(F32)
    return out


def scatter_core(part):
    half = part.shape[0] // 2
    core = lax.axis_index("tok") % 2
    mine = lax.dynamic_slice_in_dim(part, core * half, half, 0)
    other = lax.dynamic_slice_in_dim(part, (1 - core) * half, half, 0)
    return mine + swap(other.astype(BF16), "tok", 1).astype(F32)


def sum_tok(part):
    core = lax.axis_index("tok") % 2
    mine = scatter_core(part)
    sent = mine.astype(BF16)
    for k in range(2, lax.axis_size("tok"), 2):
        mine = mine + swap(sent, "tok", k).astype(F32)
    mine = mine.astype(BF16)
    other = swap(mine, "tok", 1)
    low = jnp.where(core == 0, mine, other)
    high = jnp.where(core == 0, other, mine)
    return jnp.concatenate([low, high], axis=0)


def local(tokens, out_grad, slot_proj, weight_in, weight_out, slot_norm, token_norm):
    n_exp = lax.axis_size("exp")
    n_tok = lax.axis_size("tok")
    me = lax.axis_index("exp")
    rows, feat = tokens.shape
    width = feat * n_exp
    slots = slot_proj.shape[1]
    order = jnp.arange(n_exp) ^ me

    def reorder(x):
        return x.reshape(n_exp, feat, x.shape[1])[order].reshape(x.shape)

    proj_rel = reorder(slot_proj)
    tok_t = jnp.concatenate(gather_exp(tokens.T.astype(BF16)), axis=0)
    grad_t = jnp.concatenate(gather_exp(out_grad.T.astype(BF16)), axis=0)

    def dot(a, b, ca, cb):
        return lax.dot_general(a, b, (((ca,), (cb,)), ((), ())), preferred_element_type=F32)

    logits = dot(proj_rel, tok_t, 0, 0)
    dispatch = jnp.exp(logits - slot_norm[:, None]) / F32(rows * n_tok)
    combine = jnp.exp(logits - token_norm[None, :]) / F32(slots * n_exp)
    dispatch_half = dispatch.astype(BF16)
    combine_half = combine.astype(BF16)
    slot_in_half = sum_tok(dot(tok_t, dispatch_half, 1, 1))
    slot_grad_half = sum_tok(dot(grad_t, combine_half, 1, 1))
    slot_in_c = reorder(slot_in_half)
    slot_grad_c = reorder(slot_grad_half)
    w_in, w_out = weight_in[0], weight_out[0]
    pre_act = dot(slot_in_c, w_in, 0, 0)
    gelu_out, gelu_slope = gelu_parts(pre_act)
    hidden = gelu_out.astype(BF16)
    slot_out = sum_tok(dot(w_out, hidden, 0, 1))
    hidden_grad = dot(slot_grad_c, w_out, 0, 1)
    pre_grad = (hidden_grad * gelu_slope).astype(BF16)
    slot_in_grad = sum_tok(dot(w_in, pre_grad, 1, 1))
    grad_weight_out = dot(hidden, slot_grad_c, 0, 1)[None]
    grad_weight_in = dot(slot_in_c, pre_grad, 1, 0)[None]
    out_rel = reorder(slot_out)
    ingrad_rel = reorder(slot_in_grad)
    comb_grad = dot(out_rel, grad_t, 0, 0)
    row_stat = jnp.sum(combine * comb_grad, axis=0, keepdims=True)
    k = 1
    while k < n_exp:
        row_stat = row_stat + swap(row_stat, "exp", k)
        k *= 2
    disp_grad = dot(ingrad_rel, tok_t, 0, 0)
    col_stat = jnp.sum(slot_in_half.astype(F32) * ingrad_rel.astype(F32), axis=0)
    logit_grad = (combine * (comb_grad - row_stat) + dispatch * (disp_grad - col_stat[:, None])).astype(BF16)
    proj_part = dot(tok_t, logit_grad, 1, 1)
    term = dot(
        jnp.concatenate([proj_rel, ingrad_rel], axis=1),
        jnp.concatenate([logit_grad, dispatch_half], axis=0),
        1,
        0,
    )
    grad_tokens = scatter_exp([term[k * feat : (k + 1) * feat] for k in range(n_exp)]).T

    share = width // n_tok
    proj_part = reorder(proj_part)
    core = lax.axis_index("tok") % 2
    by_core = proj_part.reshape(n_tok // 2, 2, share, slots)
    mine = lax.dynamic_index_in_dim(by_core, core, 1, keepdims=False)
    other = lax.dynamic_index_in_dim(by_core, 1 - core, 1, keepdims=False)
    mine = mine + swap(other.astype(BF16), "tok", 1).astype(F32)
    place = lax.axis_index("tok") // 2
    grad_proj = lax.dynamic_index_in_dim(mine, place, 0, keepdims=False)
    for k in range(1, n_tok // 2):
        sent = lax.dynamic_index_in_dim(mine, place ^ k, 0, keepdims=False).astype(BF16)
        grad_proj = grad_proj + swap(sent, "tok", 2 * k).astype(F32)
    return (grad_tokens, grad_proj, grad_weight_in, grad_weight_out)


def solution(mesh):
    return jax.shard_map(
        local,
        mesh=mesh,
        in_specs=(
            P("tok", "exp"),
            P("tok", "exp"),
            P(None, "exp"),
            P("exp", None, "tok"),
            P("exp", "tok", None),
            P("exp"),
            P("tok"),
        ),
        out_specs=(P("tok", "exp"), P("tok", "exp"), P("exp", None, "tok"), P("exp", "tok", None)),
        check_vma=False,
    )
```

time: 378 us -> 201 us (0.53)
  waiting for transfers between devices: 202 us -> 76.9 us
  blocking collectives: 111 us -> 0 us
  starting transfers between devices: 0.39 us -> 39 us
  local copies, waits for them, and re-layouts: 4.68 us -> 30 us
  other arithmetic: 5.45 us -> 23 us
  between operations: 14 us -> 1.22 us
  matrix products: 41.1 us -> 30.2 us
    psum x3 -> x0, blocking collectives: 111 us -> none  [the longest x1 50.6 us: local(): slot_in_grad = lax.psum(slot_in_grad_part, 'tok')]
    all_gather x2 -> x0, waiting for transfers between devices: 96.1 us -> none  [the longest x1 50 us: local(): lax.all_gather(tokens.astype(jnp.bfloat16), 'exp', axis=1, tiled=True)]
    reduce_scatter x1 -> x0, waiting for transfers between devices: 88.9 us -> none  [local(): lax.psum_scatter(token_term, 'exp', scatter_dimension=1, tiled=True)]
    ppermute x0 -> x38, waiting for transfers between devices: none -> 76.9 us  [swap(): return lax.ppermute(x, axis, [(i, i ^ k) for i in range(n)])]
    ppermute x0 -> x38, starting transfers between devices: none -> 39 us  [swap(): return lax.ppermute(x, axis, [(i, i ^ k) for i in range(n)])]
    gather x0 -> x6, local copies, waits for them, and re-layouts: none -> 14.7 us  [reorder(): return x.reshape(n_exp, feat, x.shape[1])[order].reshape(x.shape)]
    dot_general x15 -> x13, matrix products: 41.1 us -> 30.2 us  [dot(): lax.dot_general(a, b, (((ca,), (cb,)), ((), ())), preferred_element_type=...]
    psum x1 -> x0, waiting for transfers between devices: 8.54 us -> none  [local(): slot_in, slot_grad = lax.psum((slot_in_part, slot_grad_part), 'tok')]
  transfers between devices with their start and end apart: 5 -> 38, of which waited for: 5 -> 17; matrix products, arithmetic and copies ran while one was open for 5% -> 34% of each run, Pallas kernels for 0% -> 0%
where the time goes in v1:
time: 201 us; the launch traced here: 200 us
  waiting for transfers between devices  76.9 us (38%)
  starting transfers between devices  39 us (19%)
  matrix products  30.2 us (15%)
  local copies, waits for them, and re-layouts  30 us (15%)
  other arithmetic  23 us (11%)
    ppermute x38, waiting for transfers between devices, swap(): return lax.ppermute(x, axis, [(i, i ^ k) for i in range(n)])  76.9 us
    ppermute x38, starting transfers between devices, swap(): return lax.ppermute(x, axis, [(i, i ^ k) for i in range(n)])  39 us
    dot_general x13, matrix products, dot(): lax.dot_general(a, b, (((ca,), (cb,)), ((), ())), preferred_element_type=...  30.2 us
    gather x6, local copies, waits for them, and re-layouts, reorder(): return x.reshape(n_exp, feat, x.shape[1])[order].reshape(x.shape)  14.7 us
    unnamed x82, local copies, waits for them, and re-layouts  12.3 us
    convert_element_type x4, other arithmetic, sum_tok(): mine = mine.astype(BF16)  5.81 us
    select_n x4, other arithmetic, sum_tok(): low = jnp.where(core == 0, mine, other)  4.62 us
  transfers between devices with their start and end apart: 38, of which 17 were waited for; matrix products, arithmetic and copies ran while one was open for 34% of the time, Pallas kernels for 0%

profile of v1, /device:TPU:0, one launch (start us, length us, event | category | flops | bytes accessed | tf_op | source)
XLA Modules:
  0.0 200.4 jit_solution(7775924287129939892)
XLA Ops:
  0.7 2.0 constant_dynamic-update-slice_fusion.15
  2.7 5.0 %collective-permute-start.12 = (bf16[160,768]{1,0:T(8,128)(2,1)}, bf16[160,768]{1,0:T(8,128)(2,1)S(1)}, u32[]{:S(2)}, u32[]{:S(2)}) collective-permute-start(bf16[160,768]{1,0:T(8,128)(2,1)} %get-tuple-element.5), channel_id=1, source_target_pairs={{0,6},{1,7},{2,4},{3,5},{4,2},{5,3},{6,0},{7,1},{8,14},{9,15},{10,... | collective-permute-start | bytes 737288 | tf_op jit(solution)/shard_map/ppermute | solution.py:23
  8.3 1.7 collective-permute-start.7
  11.1 2.5 %gather_fusion = bf16[8,160,256]{2,1,0:T(8,128)(2,1)} fusion(bf16[8,160,256]{2,1,0:T(8,128)(2,1)} %bitcast.98, s32[1024]{0:T(1024)S(1)} %pad_clamp_fusion), kind=kCustom, calls=%fused_computation | custom fusion | bytes 1310752 | tf_op jit(solution)/shard_map/gather | solution.py:89
  13.7 3.8 %collective-permute-done.7 = bf16[160,768]{1,0:T(8,128)(2,1)} collective-permute-done((bf16[160,768]{1,0:T(8,128)(2,1)}, bf16[160,768]{1,0:T(8,128)(2,1)}, u32[]{:S(2)}, u32[]{:S(2)}) %collective-permute-start.7) | collective-permute-done | bytes 245792 | tf_op jit(solution)/shard_map/ppermute | solution.py:23
  17.5 1.5 collective-permute-start.1
  18.9 1.7 constant_dynamic-update-slice_fusion.14
  20.6 8.4 %collective-permute-done.10 = bf16[160,768]{1,0:T(8,128)(2,1)} collective-permute-done((bf16[160,768]{1,0:T(8,128)(2,1)}, bf16[160,768]{1,0:T(8,128)(2,1)}, u32[]{:S(2)}, u32[]{:S(2)}) %collective-permute-start.10) | collective-permute-done | bytes 245792 | tf_op jit(solution)/shard_map/ppermute | solution.py:23
  29.0 2.5 %collective-permute-start.5 = (bf16[160,768]{1,0:T(8,128)(2,1)}, bf16[160,768]{1,0:T(8,128)(2,1)S(1)}, u32[]{:S(2)}, u32[]{:S(2)}) collective-permute-start(bf16[160,768]{1,0:T(8,128)(2,1)} %get-tuple-element.7), channel_id=1, source_target_pairs={{0,6},{1,7},{2,4},{3,5},{4,2},{5,3},{6,0},{7,1},{8,14},{9,15},{10,... | collective-permute-start | bytes 737288 | tf_op jit(solution)/shard_map/ppermute | solution.py:23
  31.5 1.6 collective-permute-start.9
  33.1 1.7 constant_dynamic-update-slice_fusion.13
  34.8 1.7 constant_dynamic-update-slice_fusion.6
  37.7 1.5 collective-permute-start.2
  40.0 1.5 collective-permute-start.13
  41.5 9.4 %collective-permute-done.3 = bf16[160,768]{1,0:T(8,128)(2,1)S(1)} collective-permute-done((bf16[160,768]{1,0:T(8,128)(2,1)}, bf16[160,768]{1,0:T(8,128)(2,1)S(1)}, u32[]{:S(2)}, u32[]{:S(2)}) %collective-permute-start.3) | collective-permute-done | bytes 245792 | tf_op jit(solution)/shard_map/ppermute | solution.py:23
  50.9 1.5 collective-permute-start.6
  53.6 1.7 constant_dynamic-update-slice_fusion.11
  57.4 2.4 %fusion.29 = (bf16[256,768]{1,0:T(8,128)(2,1)S(1)}, f32[256,768]{1,0:T(8,128)S(1)}) fusion(f32[256]{0:T(256)S(1)} %copy-done.33, bf16[1280,256]{1,0:T(8,128)(2,1)S(1)} %bitcast.84, bf16[1280,768]{1,0:T(8,128)(2,1)} %constant_dynamic-update-slice_fusion.8), kind=kOutput, calls=%fused_computation.60 | convolution fusion | flops 503906304 | bytes 3802112 | tf_op jit(solution)/shard_map/dot_general | solution.py:96
  60.8 1.1 copy-done.8
  61.9 2.7 %collective-permute-done.4 = bf16[160,768]{1,0:T(8,128)(2,1)S(1)} collective-permute-done((bf16[160,768]{1,0:T(8,128)(2,1)S(1)}, bf16[160,768]{1,0:T(8,128)(2,1)S(1)}, u32[]{:S(2)}, u32[]{:S(2)}) %collective-permute-start.4) | collective-permute-done | bytes 245792 | tf_op jit(solution)/shard_map/ppermute | solution.py:23
  66.2 1.6 collective-permute-start.18
  68.6 1.5 collective-permute-start.15
  70.1 6.7 %collective-permute-done.18 = bf16[640,256]{1,0:T(8,128)(2,1)S(1)} collective-permute-done((bf16[640,256]{1,0:T(8,128)(2,1)S(1)}, bf16[640,256]{1,0:T(8,128)(2,1)S(1)}, u32[]{:S(2)}, u32[]{:S(2)}) %collective-permute-start.18) | collective-permute-done | bytes 327712 | tf_op jit(solution)/shard_map/ppermute | solution.py:23
  77.6 5.9 %collective-permute-done.15 = bf16[640,256]{1,0:T(8,128)(2,1)} collective-permute-done((bf16[640,256]{1,0:T(8,128)(2,1)}, bf16[640,256]{1,0:T(8,128)(2,1)}, u32[]{:S(2)}, u32[]{:S(2)}) %collective-permute-start.15) | collective-permute-done | bytes 327712 | tf_op jit(solution)/shard_map/ppermute | solution.py:23
  83.5 2.1 %add_convert_fusion.4 = bf16[640,256]{1,0:T(8,128)(2,1)} fusion(bf16[640,256]{1,0:T(8,128)(2,1)} %collective-permute-done.15, bf16[640,256]{1,0:T(8,128)(2,1)} %copy-done.28, f32[1280,256]{1,0:T(8,128)} %copy-done.11, s32[]{:T(128)S(6)} %select_n.107), kind=kLoop, calls=%fused_computation.57 | loop fusion | flops 819200 | bytes 1638404 | tf_op jit(solution)/shard_map/convert_element_type | solution.py:72
  85.6 1.1 broadcast_select_fusion.5
  88.4 2.5 %gather_fusion.2 = bf16[8,160,256]{2,1,0:T(8,128)(2,1)} fusion(bf16[8,160,256]{2,1,0:T(8,128)(2,1)} %bitcast.97, s32[1024]{0:T(1024)S(1)} %pad_clamp_fusion), kind=kCustom, calls=%fused_computation.2 | custom fusion | bytes 1310752 | tf_op jit(solution)/shard_map/gather | solution.py:89
  90.9 3.2 %fusion.2 = f32[256,1280]{1,0:T(8,128)S(1)} fusion(bf16[1280,256]{1,0:T(8,128)(2,1)} %bitcast.89, bf16[1,1280,1280]{2,1,0:T(8,128)(2,1)} %param.10), kind=kOutput, calls=%fused_computation.10 | convolution fusion | flops 838860800 | bytes 5242880 | tf_op jit(solution)/shard_map/dot_general | solution.py:96
  94.1 1.5 fusion.4
  97.0 1.1 broadcast_select_fusion.7
  99.0 2.5 %gather_fusion.1 = bf16[8,160,256]{2,1,0:T(8,128)(2,1)} fusion(bf16[8,160,256]{2,1,0:T(8,128)(2,1)} %bitcast.94, s32[1024]{0:T(1024)S(1)} %pad_clamp_fusion), kind=kCustom, calls=%fused_computation.1 | custom fusion | bytes 1310752 | tf_op jit(solution)/shard_map/gather | solution.py:89
  101.6 3.0 %fusion.11 = bf16[256,1280]{1,0:T(8,128)(2,1)S(1)} fusion(bf16[1280,256]{1,0:T(8,128)(2,1)} %bitcast.91, bf16[1,1280,1280]{2,1,0:T(8,128)(2,1)S(1)} %copy-done, f32[256,1280]{1,0:T(8,128)} %copy-done.19), kind=kOutput, calls=%fused_computation.17 | convolution fusion | flops 845086720 | bytes 5898240 | tf_op jit(solution)/shard_map/dot_general | solution.py:96
  104.6 1.1 fusion
  106.1 1.0 fusion.41
  107.2 1.6 collective-permute-start.24
  110.1 7.7 %collective-permute-done.24 = bf16[640,256]{1,0:T(8,128)(2,1)S(1)} collective-permute-done((bf16[640,256]{1,0:T(8,128)(2,1)S(1)}, bf16[640,256]{1,0:T(8,128)(2,1)S(1)}, u32[]{:S(2)}, u32[]{:S(2)}) %collective-permute-start.24) | collective-permute-done | bytes 327712 | tf_op jit(solution)/shard_map/ppermute | solution.py:23
  117.8 1.1 add_convert_fusion.1
  119.0 5.1 %collective-permute-done.21 = bf16[640,256]{1,0:T(8,128)(2,1)} collective-permute-done((bf16[640,256]{1,0:T(8,128)(2,1)}, bf16[640,256]{1,0:T(8,128)(2,1)}, u32[]{:S(2)}, u32[]{:S(2)}) %collective-permute-start.21) | collective-permute-done | bytes 327712 | tf_op jit(solution)/shard_map/ppermute | solution.py:23
  124.1 1.8 add_convert_fusion.2
  126.0 1.3 broadcast_select_fusion.1
  128.1 2.5 %gather_fusion.4 = bf16[8,160,256]{2,1,0:T(8,128)(2,1)} fusion(bf16[8,160,256]{2,1,0:T(8,128)(2,1)} %bitcast.95, s32[1024]{0:T(1024)S(1)} %pad_clamp_fusion), kind=kCustom, calls=%fused_computation.4 | custom fusion | bytes 1310752 | tf_op jit(solution)/shard_map/gather | solution.py:89
  130.7 2.7 %multiply_reduce_fusion.1 = (f32[768]{0:T(1024)S(1)}, f32[256,768]{1,0:T(8,128)}) fusion(f32[256,768]{1,0:T(8,128)S(1)} %copy-done.6, f32[768]{0:T(1024)S(1)} %copy-done.32, bf16[1280,256]{1,0:T(8,128)(2,1)} %bitcast.93, bf16[1280,768]{1,0:T(8,128)(2,1)S(1)} %copy-done.10), kind=kOutput, calls=%fused_computation.39 | convolution fusion | flops 504102144 | bytes 4200448 | tf_op jit(solution)/shard_map/dot_general | solution.py:96
  133.4 1.5 collective-permute-start.26
  134.9 1.1 broadcast_select_fusion.3
  137.0 1.7 collective-permute-start.27
  139.6 2.8 %gather_fusion.3 = bf16[8,160,256]{2,1,0:T(8,128)(2,1)} fusion(bf16[8,160,256]{2,1,0:T(8,128)(2,1)} %bitcast.96, s32[1024]{0:T(1024)S(1)} %pad_clamp_fusion), kind=kCustom, calls=%fused_computation.3 | custom fusion | bytes 1310752 | tf_op jit(solution)/shard_map/gather | solution.py:89
  143.4 1.4 multiply_reduce_fusion
  144.8 2.2 %collective-permute-done.28 = f32[1,768]{1,0:T(1,128)S(1)} collective-permute-done((f32[1,768]{1,0:T(1,128)S(1)}, f32[1,768]{1,0:T(1,128)S(1)}, u32[]{:S(2)}, u32[]{:S(2)}) %collective-permute-start.28) | collective-permute-done | bytes 3104 | tf_op jit(solution)/shard_map/ppermute | solution.py:23
  147.1 2.0 %add_convert_fusion = bf16[256,768]{1,0:T(8,128)(2,1)S(1)} fusion(f32[256,768]{1,0:T(8,128)} %get-tuple-element.26, bf16[1280,256]{1,0:T(8,128)(2,1)S(1)} %bitcast.82, bf16[1280,768]{1,0:T(8,128)(2,1)S(1)} %copy-done.3, f32[256,768]{1,0:T(8,128)S(1)} %copy-done.6, f32[256]{0:T(256)S(1)} %multiply_reduce_fusion, f32[768]{0:T(1024)S(1)} %add_reduce_fusion, ...), kind=kOutput, calls=%fused_computation.38 | convolution fusion | flops 505282560 | bytes 4595712 | tf_op jit(solution)/shard_map/dot_general | solution.py:96
  149.1 1.8 fusion.56
  150.9 3.1 %fusion.54 = (bf16[1280,768]{1,0:T(8,128)(2,1)S(1)}, f32[1280,768]{1,0:T(8,128)}) fusion(bf16[256,768]{1,0:T(8,128)(2,1)S(1)} %copy-done.18, bf16[256,768]{1,0:T(8,128)(2,1)S(1)} %add_convert_fusion, bf16[1280,256]{1,0:T(8,128)(2,1)S(1)} %bitcast.83, bf16[1280,256]{1,0:T(8,128)(2,1)S(1)} %bitcast.85), kind=kOutput, calls=%fused_computation.119 | convolution fusion | flops 1011810304 | bytes 7995392 | tf_op jit(solution)/shard_map/dot_general | solution.py:96
  154.0 1.7 gather_fusion.5
  155.7 1.3 fusion.48
  157.1 1.6 collective-permute-start.34
  159.2 1.5 collective-permute-start.30
  160.7 4.2 %convolution_bitcast_fusion = f32[1,1280,1280]{2,1,0:T(8,128)} fusion(bf16[1280,256]{1,0:T(8,128)(2,1)S(1)} %bitcast.92, f32[256,1280]{1,0:T(8,128)S(1)} %copy-done.20), kind=kOutput, calls=%fused_computation.6 | convolution fusion | flops 841809920 | bytes 8519680 | tf_op jit(solution)/shard_map/dot_general | solution.py:96
  165.9 5.3 %collective-permute-done.32 = bf16[160,768]{1,0:T(8,128)(2,1)S(1)} collective-permute-done((bf16[160,768]{1,0:T(8,128)(2,1)S(1)}, bf16[160,768]{1,0:T(8,128)(2,1)S(1)}, u32[]{:S(2)}, u32[]{:S(2)}) %collective-permute-start.32) | collective-permute-done | bytes 245792 | tf_op jit(solution)/shard_map/ppermute | solution.py:23
  171.2 5.3 %collective-permute-done.30 = bf16[160,768]{1,0:T(8,128)(2,1)S(1)} collective-permute-done((bf16[160,768]{1,0:T(8,128)(2,1)S(1)}, bf16[160,768]{1,0:T(8,128)(2,1)S(1)}, u32[]{:S(2)}, u32[]{:S(2)}) %collective-permute-start.30) | collective-permute-done | bytes 245792 | tf_op jit(solution)/shard_map/ppermute | solution.py:23
  176.7 2.4 %collective-permute-start.31 = (bf16[160,768]{1,0:T(8,128)(2,1)S(1)}, bf16[160,768]{1,0:T(8,128)(2,1)S(1)}, u32[]{:S(2)}, u32[]{:S(2)}) collective-permute-start(bf16[160,768]{1,0:T(8,128)(2,1)S(1)} %get-tuple-element.8), channel_id=1, source_target_pairs={{0,6},{1,7},{2,4},{3,5},{4,2},{5,3},{6,0},{7,1},{8,14},{9,15},{10,... | collective-permute-start | bytes 737288 | tf_op jit(solution)/shard_map/ppermute | solution.py:23
  179.0 2.1 %collective-permute-start.33 = (bf16[160,768]{1,0:T(8,128)(2,1)S(1)}, bf16[160,768]{1,0:T(8,128)(2,1)S(1)}, u32[]{:S(2)}, u32[]{:S(2)}) collective-permute-start(bf16[160,768]{1,0:T(8,128)(2,1)S(1)} %get-tuple-element.10), channel_id=1, source_target_pairs={{0,4},{1,5},{2,6},{3,7},{4,0},{5,1},{6,2},{7,3},{8,12},{9,13},{10,... | collective-permute-start | bytes 737288 | tf_op jit(solution)/shard_map/ppermute | solution.py:23
  181.3 1.6 collective-permute-start.37
  182.8 3.8 %convolution_bitcast_fusion.1 = f32[1,1280,1280]{2,1,0:T(8,128)} fusion(bf16[1280,256]{1,0:T(8,128)(2,1)S(1)} %bitcast.90, bf16[256,1280]{1,0:T(8,128)(2,1)S(1)} %copy-done.30), kind=kOutput, calls=%fused_computation.7 | convolution fusion | flops 838860800 | bytes 7864320 | tf_op jit(solution)/shard_map/dot_general | solution.py:96
  187.5 5.9 %collective-permute-done.35 = bf16[160,768]{1,0:T(8,128)(2,1)S(1)} collective-permute-done((bf16[160,768]{1,0:T(8,128)(2,1)S(1)}, bf16[160,768]{1,0:T(8,128)(2,1)S(1)}, u32[]{:S(2)}, u32[]{:S(2)}) %collective-permute-start.35) | collective-permute-done | bytes 245792 | tf_op jit(solution)/shard_map/ppermute | solution.py:23
  193.3 6.1 %collective-permute-done.33 = bf16[160,768]{1,0:T(8,128)(2,1)S(1)} collective-permute-done((bf16[160,768]{1,0:T(8,128)(2,1)S(1)}, bf16[160,768]{1,0:T(8,128)(2,1)S(1)}, u32[]{:S(2)}, u32[]{:S(2)}) %collective-permute-start.33) | collective-permute-done | bytes 245792 | tf_op jit(solution)/shard_map/ppermute | solution.py:23
  (151 shorter events, 24.4 us)
Async XLA Ops:
  0.6 93.5 %copy-start = (bf16[1,1280,1280]{2,1,0:T(8,128)(2,1)S(1)}, bf16[1,1280,1280]{2,1,0:T(8,128)(2,1)}, u32[]{:S(2)}) copy-start(bf16[1,1280,1280]{2,1,0:T(8,128)(2,1)} %param.11) | copy-start | bytes 9830404
  0.6 9.4 %copy-start.31 = (f32[768,160]{0,1:T(8,128)S(1)}, f32[768,160]{0,1:T(8,128)}, u32[]{:S(2)}) copy-start(f32[768,160]{0,1:T(8,128)} %param.8) | copy-start | bytes 1474564
  2.7 35.0 %collective-permute-start.12 = (bf16[160,768]{1,0:T(8,128)(2,1)}, bf16[160,768]{1,0:T(8,128)(2,1)S(1)}, u32[]{:S(2)}, u32[]{:S(2)}) collective-permute-start(bf16[160,768]{1,0:T(8,128)(2,1)} %get-tuple-element.5), channel_id=1, source_target_pairs={{0,6},{1,7},{2,4},{3,5},{4,2},{5,3},{6,0},{7,1},{8,14},{9,15},{10,... | collective-permute-start | bytes 737288 | tf_op jit(solution)/shard_map/ppermute | solution.py:23
  7.7 21.3 %collective-permute-start.10 = (bf16[160,768]{1,0:T(8,128)(2,1)}, bf16[160,768]{1,0:T(8,128)(2,1)}, u32[]{:S(2)}, u32[]{:S(2)}) collective-permute-start(bf16[160,768]{1,0:T(8,128)(2,1)} %get-tuple-element.5), channel_id=1, source_target_pairs={{0,4},{1,5},{2,6},{3,7},{4,0},{5,1},{6,2},{7,3},{8,12},{9,13},{10,... | collective-permute-start | bytes 737288 | tf_op jit(solution)/shard_map/ppermute | solution.py:23
  7.7 23.8 %collective-permute-start.8 = (bf16[160,768]{1,0:T(8,128)(2,1)}, bf16[160,768]{1,0:T(8,128)(2,1)}, u32[]{:S(2)}, u32[]{:S(2)}) collective-permute-start(bf16[160,768]{1,0:T(8,128)(2,1)} %get-tuple-element.5), channel_id=1, source_target_pairs={{0,2},{1,3},{2,0},{3,1},{4,6},{5,7},{6,4},{7,5},{8,10},{9,11},{10,... | collective-permute-start | bytes 737288 | tf_op jit(solution)/shard_map/ppermute | solution.py:23
  8.3 9.2 %collective-permute-start.7 = (bf16[160,768]{1,0:T(8,128)(2,1)}, bf16[160,768]{1,0:T(8,128)(2,1)}, u32[]{:S(2)}, u32[]{:S(2)}) collective-permute-start(bf16[160,768]{1,0:T(8,128)(2,1)} %get-tuple-element.5), channel_id=1, source_target_pairs={{0,1},{1,0},{2,3},{3,2},{4,5},{5,4},{6,7},{7,6},{8,9},{9,8},{10,11... | collective-permute-start | bytes 737288 | tf_op jit(solution)/shard_map/ppermute | solution.py:23
  10.8 20.7 %collective-permute-start = (bf16[160,768]{1,0:T(8,128)(2,1)}, bf16[160,768]{1,0:T(8,128)(2,1)}, u32[]{:S(2)}, u32[]{:S(2)}) collective-permute-start(bf16[160,768]{1,0:T(8,128)(2,1)} %get-tuple-element.7), channel_id=1, source_target_pairs={{0,1},{1,0},{2,3},{3,2},{4,5},{5,4},{6,7},{7,6},{8,9},{9,8},{10,11... | collective-permute-start | bytes 737288 | tf_op jit(solution)/shard_map/ppermute | solution.py:23
  17.5 19.0 %collective-permute-start.1 = (bf16[160,768]{1,0:T(8,128)(2,1)}, bf16[160,768]{1,0:T(8,128)(2,1)S(1)}, u32[]{:S(2)}, u32[]{:S(2)}) collective-permute-start(bf16[160,768]{1,0:T(8,128)(2,1)} %get-tuple-element.7), channel_id=1, source_target_pairs={{0,2},{1,3},{2,0},{3,1},{4,6},{5,7},{6,4},{7,5},{8,10},{9,11},{10,... | collective-permute-start | bytes 737288 | tf_op jit(solution)/shard_map/ppermute | solution.py:23
  29.0 11.0 %collective-permute-start.5 = (bf16[160,768]{1,0:T(8,128)(2,1)}, bf16[160,768]{1,0:T(8,128)(2,1)S(1)}, u32[]{:S(2)}, u32[]{:S(2)}) collective-permute-start(bf16[160,768]{1,0:T(8,128)(2,1)} %get-tuple-element.7), channel_id=1, source_target_pairs={{0,6},{1,7},{2,4},{3,5},{4,2},{5,3},{6,0},{7,1},{8,14},{9,15},{10,... | collective-permute-start | bytes 737288 | tf_op jit(solution)/shard_map/ppermute | solution.py:23
  31.5 19.4 %collective-permute-start.3 = (bf16[160,768]{1,0:T(8,128)(2,1)}, bf16[160,768]{1,0:T(8,128)(2,1)S(1)}, u32[]{:S(2)}, u32[]{:S(2)}) collective-permute-start(bf16[160,768]{1,0:T(8,128)(2,1)} %get-tuple-element.7), channel_id=1, source_target_pairs={{0,4},{1,5},{2,6},{3,7},{4,0},{5,1},{6,2},{7,3},{8,12},{9,13},{10,... | collective-permute-start | bytes 737288 | tf_op jit(solution)/shard_map/ppermute | solution.py:23
  31.5 20.9 %collective-permute-start.9 = (bf16[160,768]{1,0:T(8,128)(2,1)}, bf16[160,768]{1,0:T(8,128)(2,1)S(1)}, u32[]{:S(2)}, u32[]{:S(2)}) collective-permute-start(bf16[160,768]{1,0:T(8,128)(2,1)} %collective-permute-done.8), channel_id=1, source_target_pairs={{0,1},{1,0},{2,3},{3,2},{4,5},{5,4},{6,7},{7,6},{8,9},{9,8},{10,11... | collective-permute-start | bytes 737288 | tf_op jit(solution)/shard_map/ppermute | solution.py:23
  36.4 18.9 %collective-permute-start.11 = (bf16[160,768]{1,0:T(8,128)(2,1)}, bf16[160,768]{1,0:T(8,128)(2,1)S(1)}, u32[]{:S(2)}, u32[]{:S(2)}) collective-permute-start(bf16[160,768]{1,0:T(8,128)(2,1)} %collective-permute-done.10), channel_id=1, source_target_pairs={{0,1},{1,0},{2,3},{3,2},{4,5},{5,4},{6,7},{7,6},{8,9},{9,8},{10,11... | collective-permute-start | bytes 737288 | tf_op jit(solution)/shard_map/ppermute | solution.py:23
  37.7 19.8 %copy-start.12 = (bf16[8,160,256]{2,1,0:T(8,128)(2,1)S(1)}, bf16[8,160,256]{2,1,0:T(8,128)(2,1)}, u32[]{:S(2)}) copy-start(bf16[8,160,256]{2,1,0:T(8,128)(2,1)} %gather_fusion) | copy-start | bytes 1966084
  37.7 19.8 %copy-start.33 = (f32[256]{0:T(256)S(1)}, f32[256]{0:T(256)}, u32[]{:S(2)}) copy-start(f32[256]{0:T(256)} %param.12) | copy-start | bytes 3076
  37.7 23.1 %collective-permute-start.2 = (bf16[160,768]{1,0:T(8,128)(2,1)S(1)}, bf16[160,768]{1,0:T(8,128)(2,1)S(1)}, u32[]{:S(2)}, u32[]{:S(2)}) collective-permute-start(bf16[160,768]{1,0:T(8,128)(2,1)S(1)} %collective-permute-done.1), channel_id=1, source_target_pairs={{0,1},{1,0},{2,3},{3,2},{4,5},{5,4},{6,7},{7,6},{8,9},{9,8},{10,11... | collective-permute-start | bytes 737288 | tf_op jit(solution)/shard_map/ppermute | solution.py:23
  40.0 16.7 %collective-permute-start.13 = (bf16[160,768]{1,0:T(8,128)(2,1)S(1)}, bf16[160,768]{1,0:T(8,128)(2,1)S(1)}, u32[]{:S(2)}, u32[]{:S(2)}) collective-permute-start(bf16[160,768]{1,0:T(8,128)(2,1)S(1)} %collective-permute-done.12), channel_id=1, source_target_pairs={{0,1},{1,0},{2,3},{3,2},{4,5},{5,4},{6,7},{7,6},{8,9},{9,8},{10,11... | collective-permute-start | bytes 737288 | tf_op jit(solution)/shard_map/ppermute | solution.py:23
  50.9 13.8 %collective-permute-start.6 = (bf16[160,768]{1,0:T(8,128)(2,1)S(1)}, bf16[160,768]{1,0:T(8,128)(2,1)S(1)}, u32[]{:S(2)}, u32[]{:S(2)}) collective-permute-start(bf16[160,768]{1,0:T(8,128)(2,1)S(1)} %collective-permute-done.5), channel_id=1, source_target_pairs={{0,1},{1,0},{2,3},{3,2},{4,5},{5,4},{6,7},{7,6},{8,9},{9,8},{10,11... | collective-permute-start | bytes 737288 | tf_op jit(solution)/shard_map/ppermute | solution.py:23
  52.4 12.2 %collective-permute-start.4 = (bf16[160,768]{1,0:T(8,128)(2,1)S(1)}, bf16[160,768]{1,0:T(8,128)(2,1)S(1)}, u32[]{:S(2)}, u32[]{:S(2)}) collective-permute-start(bf16[160,768]{1,0:T(8,128)(2,1)S(1)} %collective-permute-done.3), channel_id=1, source_target_pairs={{0,1},{1,0},{2,3},{3,2},{4,5},{5,4},{6,7},{7,6},{8,9},{9,8},{10,11... | collective-permute-start | bytes 737288 | tf_op jit(solution)/shard_map/ppermute | solution.py:23
  57.4 2.4 %copy-start.2 = (bf16[1280,768]{1,0:T(8,128)(2,1)S(1)}, bf16[1280,768]{1,0:T(8,128)(2,1)}, u32[]{:S(2)}) copy-start(bf16[1280,768]{1,0:T(8,128)(2,1)} %constant_dynamic-update-slice_fusion.8) | copy-start | bytes 5898244
  59.9 4.8 %copy-start.5 = (f32[256,768]{1,0:T(8,128)}, f32[256,768]{1,0:T(8,128)S(1)}, u32[]{:S(2)}) copy-start(f32[256,768]{1,0:T(8,128)S(1)} %get-tuple-element.24) | copy-start | bytes 2359300
  59.9 2.0 copy-start.8
  60.7 4.0 %copy-start.32 = (f32[768]{0:T(1024)S(1)}, f32[768]{0:T(1024)}, u32[]{:S(2)}) copy-start(f32[768]{0:T(1024)} %param.13) | copy-start | bytes 9220
  60.7 5.4 %collective-permute-start.17 = (bf16[640,256]{1,0:T(8,128)(2,1)S(1)}, bf16[640,256]{1,0:T(8,128)(2,1)S(1)}, u32[]{:S(2)}, u32[]{:S(2)}) collective-permute-start(bf16[640,256]{1,0:T(8,128)(2,1)S(1)} %dynamic-slice_convert_fusion.3), channel_id=1, source_target_pairs={{0,8},{8,0},{16,24},{24,16},{1,9},{9,1},{17,25},{25,17},{2,10},{10... | collective-permute-start | bytes 983048 | tf_op jit(solution)/shard_map/ppermute | solution.py:23
  66.0 2.6 %copy-start.11 = (f32[1280,256]{1,0:T(8,128)}, f32[1280,256]{1,0:T(8,128)S(1)}, u32[]{:S(2)}) copy-start(f32[1280,256]{1,0:T(8,128)S(1)} %fusion.42) | copy-start | bytes 3932164
  66.0 1.7 collective-permute-start.14
  66.2 10.6 %collective-permute-start.18 = (bf16[640,256]{1,0:T(8,128)(2,1)S(1)}, bf16[640,256]{1,0:T(8,128)(2,1)S(1)}, u32[]{:S(2)}, u32[]{:S(2)}) collective-permute-start(bf16[640,256]{1,0:T(8,128)(2,1)S(1)} %fusion.39), channel_id=1, source_target_pairs={{0,16},{8,24},{16,0},{24,8},{1,17},{9,25},{17,1},{25,9},{2,18},{10... | collective-permute-start | bytes 983048 | tf_op jit(solution)/shard_map/ppermute | solution.py:23
  67.7 9.8 %copy-start.28 = (bf16[640,256]{1,0:T(8,128)(2,1)}, bf16[640,256]{1,0:T(8,128)(2,1)S(1)}, u32[]{:S(2)}) copy-start(bf16[640,256]{1,0:T(8,128)(2,1)S(1)} %collective-permute-done.14) | copy-start | bytes 983044
  68.6 14.9 %collective-permute-start.15 = (bf16[640,256]{1,0:T(8,128)(2,1)}, bf16[640,256]{1,0:T(8,128)(2,1)}, u32[]{:S(2)}, u32[]{:S(2)}) collective-permute-start(bf16[640,256]{1,0:T(8,128)(2,1)} %fusion.38), channel_id=1, source_target_pairs={{0,16},{8,24},{16,0},{24,8},{1,17},{9,25},{17,1},{25,9},{2,18},{10... | collective-permute-start | bytes 983048 | tf_op jit(solution)/shard_map/ppermute | solution.py:23
  77.6 8.0 %collective-permute-start.19 = (bf16[640,256]{1,0:T(8,128)(2,1)}, bf16[640,256]{1,0:T(8,128)(2,1)}, u32[]{:S(2)}, u32[]{:S(2)}) collective-permute-start(bf16[640,256]{1,0:T(8,128)(2,1)} %add_convert_fusion.3), channel_id=1, source_target_pairs={{0,8},{8,0},{16,24},{24,16},{1,9},{9,1},{17,25},{25,17},{2,10},{10... | collective-permute-start | bytes 983048 | tf_op jit(solution)/shard_map/ppermute | solution.py:23
  85.6 11.4 %collective-permute-start.16 = (bf16[640,256]{1,0:T(8,128)(2,1)}, bf16[640,256]{1,0:T(8,128)(2,1)}, u32[]{:S(2)}, u32[]{:S(2)}) collective-permute-start(bf16[640,256]{1,0:T(8,128)(2,1)} %add_convert_fusion.4), channel_id=1, source_target_pairs={{0,8},{8,0},{16,24},{24,16},{1,9},{9,1},{17,25},{25,17},{2,10},{10... | collective-permute-start | bytes 983048 | tf_op jit(solution)/shard_map/ppermute | solution.py:23
  95.7 3.4 %copy-start.25 = (f32[256,1280]{0,1:T(8,128)}, f32[256,1280]{0,1:T(8,128)S(1)}, u32[]{:S(2)}) copy-start(f32[256,1280]{0,1:T(8,128)S(1)} %fusion.4) | copy-start | bytes 3932164
  96.5 9.3 %collective-permute-start.23 = (bf16[640,256]{1,0:T(8,128)(2,1)}, bf16[640,256]{1,0:T(8,128)(2,1)}, u32[]{:S(2)}, u32[]{:S(2)}) collective-permute-start(bf16[640,256]{1,0:T(8,128)(2,1)} %fusion.47), channel_id=1, source_target_pairs={{0,8},{8,0},{16,24},{24,16},{1,9},{9,1},{17,25},{25,17},{2,10},{10... | collective-permute-start | bytes 983048 | tf_op jit(solution)/shard_map/ppermute | solution.py:23
  101.6 3.0 %copy-start.34 = (bf16[1,1280,1280]{2,1,0:T(8,128)(2,1)S(1)}, bf16[1,1280,1280]{2,1,0:T(8,128)(2,1)}, u32[]{:S(2)}) copy-start(bf16[1,1280,1280]{2,1,0:T(8,128)(2,1)} %param.10) | copy-start | bytes 9830404
  105.7 3.0 %collective-permute-start.20 = (bf16[640,256]{1,0:T(8,128)(2,1)S(1)}, bf16[640,256]{1,0:T(8,128)(2,1)S(1)}, u32[]{:S(2)}, u32[]{:S(2)}) collective-permute-start(bf16[640,256]{1,0:T(8,128)(2,1)S(1)} %fusion.46), channel_id=1, source_target_pairs={{0,8},{8,0},{16,24},{24,16},{1,9},{9,1},{17,25},{25,17},{2,10},{10... | collective-permute-start | bytes 983048 | tf_op jit(solution)/shard_map/ppermute | solution.py:23
  107.2 10.6 %collective-permute-start.24 = (bf16[640,256]{1,0:T(8,128)(2,1)S(1)}, bf16[640,256]{1,0:T(8,128)(2,1)S(1)}, u32[]{:S(2)}, u32[]{:S(2)}) collective-permute-start(bf16[640,256]{1,0:T(8,128)(2,1)S(1)} %fusion.41), channel_id=1, source_target_pairs={{0,16},{8,24},{16,0},{24,8},{1,17},{9,25},{17,1},{25,9},{2,18},{10... | collective-permute-start | bytes 983048 | tf_op jit(solution)/shard_map/ppermute | solution.py:23
  109.5 14.6 %collective-permute-start.21 = (bf16[640,256]{1,0:T(8,128)(2,1)}, bf16[640,256]{1,0:T(8,128)(2,1)}, u32[]{:S(2)}, u32[]{:S(2)}) collective-permute-start(bf16[640,256]{1,0:T(8,128)(2,1)} %fusion.40), channel_id=1, source_target_pairs={{0,16},{8,24},{16,0},{24,8},{1,17},{9,25},{17,1},{25,9},{2,18},{10... | collective-permute-start | bytes 983048 | tf_op jit(solution)/shard_map/ppermute | solution.py:23
  118.9 7.1 %copy-start.27 = (bf16[640,256]{1,0:T(8,128)(2,1)}, bf16[640,256]{1,0:T(8,128)(2,1)S(1)}, u32[]{:S(2)}) copy-start(bf16[640,256]{1,0:T(8,128)(2,1)S(1)} %add_convert_fusion.1) | copy-start | bytes 983044
  118.9 7.1 %collective-permute-start.25 = (bf16[640,256]{1,0:T(8,128)(2,1)S(1)}, bf16[640,256]{1,0:T(8,128)(2,1)}, u32[]{:S(2)}, u32[]{:S(2)}) collective-permute-start(bf16[640,256]{1,0:T(8,128)(2,1)S(1)} %add_convert_fusion.1), channel_id=1, source_target_pairs={{0,8},{8,0},{16,24},{24,16},{1,9},{9,1},{17,25},{25,17},{2,10},{10... | collective-permute-start | bytes 983048 | tf_op jit(solution)/shard_map/ppermute | solution.py:23
  125.9 8.9 %collective-permute-start.22 = (bf16[640,256]{1,0:T(8,128)(2,1)}, bf16[640,256]{1,0:T(8,128)(2,1)}, u32[]{:S(2)}, u32[]{:S(2)}) collective-permute-start(bf16[640,256]{1,0:T(8,128)(2,1)} %add_convert_fusion.2), channel_id=1, source_target_pairs={{0,8},{8,0},{16,24},{24,16},{1,9},{9,1},{17,25},{25,17},{2,10},{10... | collective-permute-start | bytes 983048 | tf_op jit(solution)/shard_map/ppermute | solution.py:23
  125.9 4.7 %copy-start.10 = (bf16[1280,768]{1,0:T(8,128)(2,1)S(1)}, bf16[1280,768]{1,0:T(8,128)(2,1)}, u32[]{:S(2)}) copy-start(bf16[1280,768]{1,0:T(8,128)(2,1)} %copy-done.9) | copy-start | bytes 5898244
  127.2 3.4 %copy-start.6 = (f32[256,768]{1,0:T(8,128)S(1)}, f32[256,768]{1,0:T(8,128)}, u32[]{:S(2)}) copy-start(f32[256,768]{1,0:T(8,128)} %copy-done.5) | copy-start | bytes 2359300
  133.4 3.6 %collective-permute-start.26 = (f32[1,768]{1,0:T(1,128)S(1)}, f32[1,768]{1,0:T(1,128)S(1)}, u32[]{:S(2)}, u32[]{:S(2)}) collective-permute-start(f32[1,768]{1,0:T(1,128)S(1)} %broadcast_in_dim.6), channel_id=1, source_target_pairs={{0,1},{1,0},{2,3},{3,2},{4,5},{5,4},{6,7},{7,6},{8,9},{9,8},{10,11... | collective-permute-start | bytes 9224 | tf_op jit(solution)/shard_map/ppermute | solution.py:23
  137.0 5.5 %collective-permute-start.27 = (f32[1,768]{1,0:T(1,128)S(1)}, f32[1,768]{1,0:T(1,128)S(1)}, u32[]{:S(2)}, u32[]{:S(2)}) collective-permute-start(f32[1,768]{1,0:T(1,128)S(1)} %reshape_add_fusion), channel_id=1, source_target_pairs={{0,2},{1,3},{2,0},{3,1},{4,6},{5,7},{6,4},{7,5},{8,10},{9,11},{10,... | collective-permute-start | bytes 9224 | tf_op jit(solution)/shard_map/ppermute | solution.py:23
  138.7 4.7 %copy-start.22 = (bf16[640,256]{1,0:T(8,128)(2,1)S(1)}, bf16[640,256]{1,0:T(8,128)(2,1)}, u32[]{:S(2)}) copy-start(bf16[640,256]{1,0:T(8,128)(2,1)} %copy-done.21) | copy-start | bytes 983044
  139.6 7.4 %copy-start.3 = (bf16[1280,768]{1,0:T(8,128)(2,1)S(1)}, bf16[1280,768]{1,0:T(8,128)(2,1)}, u32[]{:S(2)}) copy-start(bf16[1280,768]{1,0:T(8,128)(2,1)} %constant_dynamic-update-slice_fusion.8) | copy-start | bytes 5898244
  142.5 4.6 %copy-start.7 = (bf16[8,160,256]{2,1,0:T(8,128)(2,1)S(1)}, bf16[8,160,256]{2,1,0:T(8,128)(2,1)}, u32[]{:S(2)}) copy-start(bf16[8,160,256]{2,1,0:T(8,128)(2,1)} %gather_fusion.3) | copy-start | bytes 1966084
  142.5 4.6 %collective-permute-start.28 = (f32[1,768]{1,0:T(1,128)S(1)}, f32[1,768]{1,0:T(1,128)S(1)}, u32[]{:S(2)}, u32[]{:S(2)}) collective-permute-start(f32[1,768]{1,0:T(1,128)S(1)} %add.148), channel_id=1, source_target_pairs={{0,4},{1,5},{2,6},{3,7},{4,0},{5,1},{6,2},{7,3},{8,12},{9,13},{10,... | collective-permute-start | bytes 9224 | tf_op jit(solution)/shard_map/ppermute | solution.py:23
  150.9 3.1 %copy-start.14 = (f32[1280,256]{1,0:T(8,128)S(1)}, f32[1280,256]{1,0:T(8,128)}, u32[]{:S(2)}) copy-start(f32[1280,256]{1,0:T(8,128)} %fusion.56) | copy-start | bytes 3932164
  155.7 5.0 %copy-start.20 = (f32[256,1280]{1,0:T(8,128)S(1)}, f32[256,1280]{1,0:T(8,128)}, u32[]{:S(2)}) copy-start(f32[256,1280]{1,0:T(8,128)} %copy-done.19) | copy-start | bytes 3932164
  155.7 5.0 %copy-start.24 = (bf16[8,160,256]{2,1,0:T(8,128)(2,1)S(1)}, bf16[8,160,256]{2,1,0:T(8,128)(2,1)}, u32[]{:S(2)}) copy-start(bf16[8,160,256]{2,1,0:T(8,128)(2,1)} %gather_fusion.1) | copy-start | bytes 1966084
  157.0 24.2 %collective-permute-start.36 = (bf16[2,320,256]{2,1,0:T(8,128)(2,1)S(1)}, bf16[2,320,256]{2,1,0:T(8,128)(2,1)S(1)}, u32[]{:S(2)}, u32[]{:S(2)}) collective-permute-start(bf16[2,320,256]{2,1,0:T(8,128)(2,1)S(1)} %fusion.48), channel_id=1, source_target_pairs={{0,8},{8,0},{16,24},{24,16},{1,9},{9,1},{17,25},{25,17},{2,10},{10... | collective-permute-start | bytes 983048 | tf_op jit(solution)/shard_map/ppermute | solution.py:23
  157.1 8.8 %collective-permute-start.34 = (bf16[160,768]{1,0:T(8,128)(2,1)S(1)}, bf16[160,768]{1,0:T(8,128)(2,1)S(1)}, u32[]{:S(2)}, u32[]{:S(2)}) collective-permute-start(bf16[160,768]{1,0:T(8,128)(2,1)S(1)} %get-tuple-element.12), channel_id=1, source_target_pairs={{0,1},{1,0},{2,3},{3,2},{4,5},{5,4},{6,7},{7,6},{8,9},{9,8},{10,11... | collective-permute-start | bytes 737288 | tf_op jit(solution)/shard_map/ppermute | solution.py:23
  158.7 12.5 %collective-permute-start.32 = (bf16[160,768]{1,0:T(8,128)(2,1)S(1)}, bf16[160,768]{1,0:T(8,128)(2,1)S(1)}, u32[]{:S(2)}, u32[]{:S(2)}) collective-permute-start(bf16[160,768]{1,0:T(8,128)(2,1)S(1)} %get-tuple-element.13), channel_id=1, source_target_pairs={{0,1},{1,0},{2,3},{3,2},{4,5},{5,4},{6,7},{7,6},{8,9},{9,8},{10,11... | collective-permute-start | bytes 737288 | tf_op jit(solution)/shard_map/ppermute | solution.py:23
  159.2 17.3 %copy-start.4 = (f32[1280,768]{1,0:T(8,128)S(1)}, f32[1280,768]{1,0:T(8,128)}, u32[]{:S(2)}) copy-start(f32[1280,768]{1,0:T(8,128)} %get-tuple-element.28) | copy-start | bytes 11796484
  159.2 17.3 %collective-permute-start.30 = (bf16[160,768]{1,0:T(8,128)(2,1)S(1)}, bf16[160,768]{1,0:T(8,128)(2,1)S(1)}, u32[]{:S(2)}, u32[]{:S(2)}) collective-permute-start(bf16[160,768]{1,0:T(8,128)(2,1)S(1)} %get-tuple-element.14), channel_id=1, source_target_pairs={{0,1},{1,0},{2,3},{3,2},{4,5},{5,4},{6,7},{7,6},{8,9},{9,8},{10,11... | collective-permute-start | bytes 737288 | tf_op jit(solution)/shard_map/ppermute | solution.py:23
  164.9 22.5 %collective-permute-start.29 = (bf16[160,768]{1,0:T(8,128)(2,1)S(1)}, bf16[160,768]{1,0:T(8,128)(2,1)S(1)}, u32[]{:S(2)}, u32[]{:S(2)}) collective-permute-start(bf16[160,768]{1,0:T(8,128)(2,1)S(1)} %get-tuple-element.11), channel_id=1, source_target_pairs={{0,1},{1,0},{2,3},{3,2},{4,5},{5,4},{6,7},{7,6},{8,9},{9,8},{10,11... | collective-permute-start | bytes 737288 | tf_op jit(solution)/shard_map/ppermute | solution.py:23
  176.5 4.7 %copy-start.15 = (f32[8,160,256]{2,1,0:T(8,128)S(1)}, f32[8,160,256]{2,1,0:T(8,128)}, u32[]{:S(2)}) copy-start(f32[8,160,256]{2,1,0:T(8,128)} %gather_fusion.5) | copy-start | bytes 3932164
  176.7 6.1 %copy-start.16 = (bf16[8,160,256]{2,1,0:T(8,128)(2,1)S(1)}, bf16[8,160,256]{2,1,0:T(8,128)(2,1)}, u32[]{:S(2)}) copy-start(bf16[8,160,256]{2,1,0:T(8,128)(2,1)} %gather_fusion.2) | copy-start | bytes 1966084
  176.7 6.1 %copy-start.30 = (bf16[256,1280]{1,0:T(8,128)(2,1)S(1)}, bf16[256,1280]{1,0:T(8,128)(2,1)}, u32[]{:S(2)}) copy-start(bf16[256,1280]{1,0:T(8,128)(2,1)} %copy-done.29) | copy-start | bytes 1966084
  176.7 10.8 %collective-permute-start.31 = (bf16[160,768]{1,0:T(8,128)(2,1)S(1)}, bf16[160,768]{1,0:T(8,128)(2,1)S(1)}, u32[]{:S(2)}, u32[]{:S(2)}) collective-permute-start(bf16[160,768]{1,0:T(8,128)(2,1)S(1)} %get-tuple-element.8), channel_id=1, source_target_pairs={{0,6},{1,7},{2,4},{3,5},{4,2},{5,3},{6,0},{7,1},{8,14},{9,15},{10,... | collective-permute-start | bytes 737288 | tf_op jit(solution)/shard_map/ppermute | solution.py:23
  179.0 14.3 %collective-permute-start.35 = (bf16[160,768]{1,0:T(8,128)(2,1)S(1)}, bf16[160,768]{1,0:T(8,128)(2,1)S(1)}, u32[]{:S(2)}, u32[]{:S(2)}) collective-permute-start(bf16[160,768]{1,0:T(8,128)(2,1)S(1)} %get-tuple-element.9), channel_id=1, source_target_pairs={{0,2},{1,3},{2,0},{3,1},{4,6},{5,7},{6,4},{7,5},{8,10},{9,11},{10,... | collective-permute-start | bytes 737288 | tf_op jit(solution)/shard_map/ppermute | solution.py:23
  179.0 20.4 %collective-permute-start.33 = (bf16[160,768]{1,0:T(8,128)(2,1)S(1)}, bf16[160,768]{1,0:T(8,128)(2,1)S(1)}, u32[]{:S(2)}, u32[]{:S(2)}) collective-permute-start(bf16[160,768]{1,0:T(8,128)(2,1)S(1)} %get-tuple-element.10), channel_id=1, source_target_pairs={{0,4},{1,5},{2,6},{3,7},{4,0},{5,1},{6,2},{7,3},{8,12},{9,13},{10,... | collective-permute-start | bytes 737288 | tf_op jit(solution)/shard_map/ppermute | solution.py:23
  181.3 5.4 %collective-permute-start.37 = (bf16[320,256]{1,0:T(8,128)(2,1)S(1)}, bf16[320,256]{1,0:T(8,128)(2,1)S(1)}, u32[]{:S(2)}, u32[]{:S(2)}) collective-permute-start(bf16[320,256]{1,0:T(8,128)(2,1)S(1)} %fusion.49), channel_id=1, source_target_pairs={{0,16},{8,24},{16,0},{24,8},{1,17},{9,25},{17,1},{25,9},{2,18},{10... | collective-permute-start | bytes 491528 | tf_op jit(solution)/shard_map/ppermute | solution.py:23
  182.8 17.6 %copy-start.1 = (bf16[1,1280,1280]{2,1,0:T(8,128)(2,1)S(1)}, bf16[1,1280,1280]{2,1,0:T(8,128)(2,1)}, u32[]{:S(2)}) copy-start(bf16[1,1280,1280]{2,1,0:T(8,128)(2,1)} %param.11) | copy-start | bytes 9830404
  (9 other events, 12.2 us)

commit v2 on v1

v2 whole, which is shorter than its diff:
```python
import functools

import jax
import jax.numpy as jnp
from jax import lax
from jax.experimental import pallas as pl
from jax.experimental.pallas import tpu as pltpu
from jax.sharding import PartitionSpec as P

GELU_C = 0.7978845608028654
BF16 = jnp.bfloat16
F16 = jnp.float16
F32 = jnp.float32
LANES = 128
MIB = 1024 * 1024


def gelu_parts(pre_act):
    square = pre_act * pre_act
    tangent = jnp.tanh(GELU_C * (pre_act + 0.044715 * (square * pre_act)))
    value = 0.5 * pre_act * (1.0 + tangent)
    slope = 0.5 * (1.0 + tangent) + 0.5 * pre_act * (1.0 - tangent * tangent) * GELU_C * (
        1.0 + 3.0 * 0.044715 * square
    )
    return (value, slope)


def dot(a, b, ca, cb):
    return lax.dot_general(a, b, (((ca,), (cb,)), ((), ())), preferred_element_type=F32)


def swap(x, axis, k):
    n = lax.axis_size(axis)
    return lax.ppermute(x, axis, [(i, i ^ k) for i in range(n)])


def tree_of(n):
    def parent(k):
        bits = [b for b in (1 << i for i in range(n.bit_length())) if k & b]
        return k - (bits[1] if len(bits) > 2 else bits[0])

    def depth(k):
        return 1 + depth(parent(k)) if k else 0

    return {k: parent(k) for k in sorted(range(1, n), key=lambda k: (depth(k), -k))}


def gather_exp(block):
    tree = tree_of(lax.axis_size("exp"))
    held = {0: block}
    for k, source in tree.items():
        held[k] = swap(held[source], "exp", k ^ source)
    return [held[k] for k in range(len(held))]


def scatter_exp(blocks):
    tree = tree_of(lax.axis_size("exp"))
    for k, target in reversed(tree.items()):
        blocks[target] = blocks[target] + swap(blocks[k].astype(BF16), "exp", k ^ target).astype(F32)
    return blocks[0]


def to_half(x):
    top = jnp.maximum(jnp.max(jnp.abs(x), axis=1, keepdims=True), 1e-30)
    power = jnp.floor(jnp.log2(top))
    scaled = (x * jnp.exp2(14.0 - power)).astype(F16)
    return jnp.concatenate([scaled, jnp.broadcast_to(power.astype(F16), (x.shape[0], LANES))], axis=1)


def from_half(sent):
    return sent[:, :-LANES].astype(F32) * jnp.exp2(sent[:, -1:].astype(F32) - 14.0)


def call(body, outs, args, flops, scratch=(), waits=0, vmem=48):
    in_specs = [pl.BlockSpec(memory_space=pltpu.SMEM)]
    in_specs += [pl.BlockSpec(memory_space=pltpu.VMEM)] * (len(args) - 1 - waits)
    in_specs += [pl.BlockSpec(memory_space=pl.ANY)] * waits
    size = sum(a.size * a.dtype.itemsize for a in args) + sum(
        o.size * o.dtype.itemsize for o in outs
    )
    return pl.pallas_call(
        body,
        out_shape=outs,
        in_specs=in_specs,
        out_specs=[pl.BlockSpec(memory_space=pltpu.VMEM)] * len(outs),
        scratch_shapes=list(scratch),
        compiler_params=pltpu.CompilerParams(vmem_limit_bytes=vmem * MIB),
        cost_estimate=pl.CostEstimate(flops=flops, bytes_accessed=size, transcendentals=0),
    )(*args)


def sds(shape, dtype):
    return jax.ShapeDtypeStruct(shape, dtype)


def add_kernel(ours, got, *refs):
    refs[-1][...] = (ours[...] + got[...].astype(F32)).astype(refs[-1].dtype)


def add(ours, got, dtype, waits=()):
    if not waits:
        return (ours + got.astype(F32)).astype(dtype)
    corners = [corner(w) for w in waits]
    return pl.pallas_call(
        add_kernel,
        out_shape=sds(ours.shape, dtype),
        in_specs=[pl.BlockSpec(memory_space=pltpu.VMEM)] * (2 + len(corners)),
        out_specs=pl.BlockSpec(memory_space=pltpu.VMEM),
        compiler_params=pltpu.CompilerParams(vmem_limit_bytes=8 * MIB),
        cost_estimate=pl.CostEstimate(flops=ours.size, bytes_accessed=10 * ours.size, transcendentals=0),
    )(ours, got, *corners)


def corner(x):
    return lax.slice(x, (0, 0), (min(16, x.shape[0]), LANES))


def gate_kernel(idx, *refs):
    for i in range(idx.shape[0]):
        refs[-1][i] = idx[i]


def gate(idx, waits):
    corners = [corner(w) for w in waits]
    return pl.pallas_call(
        gate_kernel,
        out_shape=sds(idx.shape, idx.dtype),
        in_specs=[pl.BlockSpec(memory_space=pltpu.SMEM)] + [pl.BlockSpec(memory_space=pltpu.VMEM)] * len(corners),
        out_specs=pl.BlockSpec(memory_space=pltpu.SMEM),
        compiler_params=pltpu.CompilerParams(vmem_limit_bytes=MIB),
    )(idx, *corners)


def sum_core(mine, other, waits=()):
    return add(mine, swap(other, "tok", 1), F32, waits)


def sum_chips(mine, fine=False, waits=()):
    sent = to_half(mine) if fine else mine.astype(BF16)
    steps = range(2, lax.axis_size("tok"), 2)
    for k in steps:
        got = swap(sent, "tok", k)
        last = k == steps[-1]
        mine = add(mine, from_half(got) if fine else got, BF16 if last else F32, waits if last else ())
    return mine, swap(mine, "tok", 1)


def put_halves(core, part, mine, other):
    half = mine.shape[0]
    mine[...] = part[pl.ds(pl.multiple_of(core * half, half), half), :]
    other[...] = part[pl.ds(pl.multiple_of((1 - core) * half, half), half), :].astype(other.dtype)


def join_halves(core, mine, other, out):
    half = mine.shape[0]
    out[pl.ds(pl.multiple_of(core * half, half), half), :] = mine[...]
    out[pl.ds(pl.multiple_of((1 - core) * half, half), half), :] = other[...]


def place_blocks(me, blocks, out):
    feat = blocks[0].shape[0]
    for k, block in enumerate(blocks):
        out[pl.ds(pl.multiple_of((me ^ k) * feat, 16), feat), :] = block[...]


def slot_in_kernel(n, scale, idx, *refs):
    blocks = refs[:n]
    proj, slot_norm = refs[n : n + 2]
    tok, logits, mine, other, part = refs[-5:]
    place_blocks(idx[0], blocks, tok)
    value = dot(proj[...], tok[...], 0, 0)
    logits[...] = value
    dispatch = (jnp.exp(value - slot_norm[...]) / scale).astype(BF16)
    part[...] = dot(dispatch, tok[...], 1, 1)
    put_halves(idx[1], part, mine, other)


def slot_grad_kernel(n, scale, idx, *refs):
    blocks = refs[:n]
    logits, token_norm, grad, mine, other, part = refs[n:]
    place_blocks(idx[0], blocks, grad)
    combine = (jnp.exp(logits[...] - token_norm[...]) / scale).astype(BF16)
    part[...] = dot(combine, grad[...], 1, 1)
    put_halves(idx[1], part, mine, other)


def forward_kernel(idx, got_mine, got_other, w_in, w_out, _, slot_in, hidden, slope, mine, other, part):
    join_halves(idx[1], got_mine, got_other, slot_in)
    value, rate = gelu_parts(dot(slot_in[...], w_in[...], 1, 0))
    slope[...] = rate
    hidden[...] = value.astype(BF16)
    part[...] = dot(hidden[...], w_out[...], 1, 0)
    put_halves(idx[1], part, mine, other)


def backward_kernel(idx, got_mine, got_other, w_in, w_out, slope, slot_grad, pre_grad, mine, other, part):
    join_halves(idx[1], got_mine, got_other, slot_grad)
    hidden_grad = dot(slot_grad[...], w_out[...], 1, 1)
    pre_grad[...] = (hidden_grad * slope[...]).astype(BF16)
    part[...] = dot(pre_grad[...], w_in[...], 1, 1)
    put_halves(idx[1], part, mine, other)


def comb_kernel(scale, idx, got_mine, got_other, grad, logits, token_norm, weighted, row_part, joined):
    join_halves(idx[1], got_mine, got_other, joined)
    combine = jnp.exp(logits[...] - token_norm[...]) / scale
    value = combine * dot(joined[...], grad[...], 1, 0)
    weighted[...] = value
    row_part[...] = jnp.sum(value, axis=0, keepdims=True)


def final_kernel(tok_scale, slot_scale, idx, got_mine, got_other, tok, logits, slot_norm, token_norm, weighted,
                 row_stat, slot_in, proj, logit_grad, *refs):
    *blocks, joined, term = refs
    join_halves(idx[1], got_mine, got_other, joined)
    in_grad = joined[...]
    combine = jnp.exp(logits[...] - token_norm[...]) / slot_scale
    dispatch = jnp.exp(logits[...] - slot_norm[...]) / tok_scale
    col_stat = jnp.sum(slot_in[...].astype(F32) * in_grad.astype(F32), axis=1, keepdims=True)
    disp_grad = dot(in_grad, tok[...], 1, 0)
    value = weighted[...] - combine * row_stat[...] + dispatch * (disp_grad - col_stat)
    half = value.astype(BF16)
    logit_grad[...] = half
    term[...] = dot(proj[...], half, 1, 0) + dot(in_grad, dispatch.astype(BF16), 0, 0)
    feat = blocks[0].shape[0]
    for k, block in enumerate(blocks):
        block[...] = term[pl.ds(pl.multiple_of((idx[0] ^ k) * feat, 16), feat), :].astype(block.dtype)


def weight_grad_kernel(left, right, _, out):
    out[...] = dot(left[...], right[...], 0, 0)


def weight_grad(left, right, wait):
    slots, rows = left.shape
    columns = right.shape[1]
    block = 256 if rows % 256 == 0 else rows
    return pl.pallas_call(
        weight_grad_kernel,
        out_shape=sds((rows, columns), F32),
        grid=(rows // block,),
        in_specs=[
            pl.BlockSpec((slots, block), lambda i: (0, i)),
            pl.BlockSpec((slots, columns), lambda i: (0, 0)),
            pl.BlockSpec(memory_space=pl.ANY),
        ],
        out_specs=pl.BlockSpec((block, columns), lambda i: (i, 0)),
        compiler_params=pltpu.CompilerParams(vmem_limit_bytes=16 * MIB),
        cost_estimate=pl.CostEstimate(
            flops=2 * slots * rows * columns, bytes_accessed=4 * rows * columns, transcendentals=0
        ),
    )(left, right, wait)


def local(tokens, out_grad, slot_proj, weight_in, weight_out, slot_norm, token_norm):
    n_exp = lax.axis_size("exp")
    n_tok = lax.axis_size("tok")
    me = lax.axis_index("exp")
    place = lax.axis_index("tok")
    rows, feat = tokens.shape
    width = feat * n_exp
    slots = slot_proj.shape[1]
    half = slots // 2
    idx = jnp.stack([me, place % 2]).astype(jnp.int32)
    w_in, w_out = weight_in[0], weight_out[0]
    hidden_units = w_in.shape[1]
    slot_norm = slot_norm[:, None]
    token_norm = token_norm[None, :]
    tok_scale = float(rows * n_tok)
    slot_scale = float(slots * n_exp)
    halves = [sds((half, width), F32), sds((half, width), BF16)]
    wide = [sds((half, width), F32)] * 2
    part = pltpu.VMEM((slots, width), F32)

    tok_blocks = gather_exp(tokens.T.astype(BF16))
    grad_blocks = gather_exp(out_grad.T.astype(BF16))
    macs = 2 * rows * width * slots
    tok, logits, mine, other = call(
        functools.partial(slot_in_kernel, n_exp, tok_scale),
        [sds((width, rows), BF16), sds((slots, rows), F32), *wide],
        [gate(idx, [grad_blocks[k] for k in (4,)]), *tok_blocks, slot_proj, slot_norm],
        2 * macs,
        [part],
        vmem=50,
    )
    mine = sum_core(mine, other, [grad_blocks[k] for k in ()])
    got_in = sum_chips(mine, True, [grad_blocks[k] for k in (5, 6)])
    grad, grad_mine, grad_other = call(
        functools.partial(slot_grad_kernel, n_exp, slot_scale),
        [sds((width, rows), BF16), *halves],
        [idx, *grad_blocks, logits, token_norm],
        macs,
        [part],
        vmem=48,
    )
    slot_in, hidden, slope, mine, other = call(
        forward_kernel,
        [sds((slots, width), BF16), sds((slots, hidden_units), BF16), sds((slots, hidden_units), F32), *halves],
        [idx, *got_in, w_in, w_out, grad_other],
        4 * slots * width * hidden_units,
        [part],
        1,
        vmem=24,
    )
    out_mine = sum_core(mine, other)
    got_grad = sum_chips(sum_core(grad_mine, grad_other))
    got_out = sum_chips(out_mine)
    weighted, row_stat = call(
        functools.partial(comb_kernel, slot_scale),
        [sds((slots, rows), F32), sds((1, rows), F32)],
        [idx, *got_out, grad, logits, token_norm],
        macs,
        [pltpu.VMEM((slots, width), BF16)],
        vmem=24,
    )
    k = 1
    while k < n_exp:
        row_stat = row_stat + swap(row_stat, "exp", k)
        k *= 2
    slot_grad, pre_grad, mine, other = call(
        backward_kernel,
        [sds((slots, width), BF16), sds((slots, hidden_units), BF16), *halves],
        [idx, *got_grad, w_in, w_out, slope],
        4 * slots * width * hidden_units,
        [part],
        vmem=24,
    )
    got_in_grad = sum_chips(sum_core(mine, other), waits=[row_stat])
    summed = {0, *tree_of(n_exp).values()}
    blocks = [sds((feat, rows), F32 if k in summed else BF16) for k in range(n_exp)]
    logit_grad, *blocks = call(
        functools.partial(final_kernel, tok_scale, slot_scale),
        [sds((slots, rows), BF16), *blocks],
        [idx, *got_in_grad, tok, logits, slot_norm, token_norm, weighted, row_stat, slot_in, slot_proj],
        3 * macs,
        [pltpu.VMEM((slots, width), BF16), pltpu.VMEM((width, rows), F32)],
        vmem=40,
    )
    grad_tokens = scatter_exp(blocks).T

    grad_weight_out = weight_grad(hidden, slot_grad, logit_grad)[None]
    grad_weight_in = weight_grad(slot_in, pre_grad, logit_grad)[None]
    share = width // n_tok
    by_core = dot(tok, logit_grad, 1, 1).reshape(n_tok // 2, 2, share, slots)
    core, chip = place % 2, place // 2
    mine = lax.dynamic_index_in_dim(by_core, core, 1, keepdims=False)
    other = lax.dynamic_index_in_dim(by_core, 1 - core, 1, keepdims=False)
    mine = mine + swap(other.astype(BF16), "tok", 1).astype(F32)
    grad_proj = lax.dynamic_index_in_dim(mine, chip, 0, keepdims=False)
    for k in range(1, n_tok // 2):
        sent = lax.dynamic_index_in_dim(mine, chip ^ k, 0, keepdims=False).astype(BF16)
        grad_proj = grad_proj + swap(sent, "tok", 2 * k).astype(F32)
    return (grad_tokens, grad_proj, grad_weight_in, grad_weight_out)


def solution(mesh):
    return jax.shard_map(
        local,
        mesh=mesh,
        in_specs=(
            P("tok", "exp"),
            P("tok", "exp"),
            P(None, "exp"),
            P("exp", None, "tok"),
            P("exp", "tok", None),
            P("exp"),
            P("tok"),
        ),
        out_specs=(P("tok", "exp"), P("tok", "exp"), P("exp", None, "tok"), P("exp", "tok", None)),
        check_vma=False,
    )
```

time: 201 us -> 141 us (0.70)
  matrix products: 30.2 us -> 0.71 us
  local copies, waits for them, and re-layouts: 30 us -> 4.32 us
  Pallas kernels: 0 us -> 25.1 us
  waiting for transfers between devices: 76.9 us -> 58.7 us
  other arithmetic: 23 us -> 5.26 us
  starting transfers between devices: 39 us -> 45.1 us
    dot_general x13 -> x1, matrix products: 30.2 us -> 0.71 us  [dot(): lax.dot_general(a, b, (((ca,), (cb,)), ((), ())), preferred_element_type=...]
    pallas_call x0 -> x11, Pallas kernels: none -> 25.1 us  [the longest x6 14.3 us: call(): pl.pallas_call(body, out_shape=outs, in_specs=in_specs, out_specs=[pl.Blo...]
    ppermute x38, waiting for transfers between devices: 76.9 us -> 58.7 us  [swap(): return lax.ppermute(x, axis, [(i, i ^ k) for i in range(n)])]
    gather x6 -> x0, local copies, waits for them, and re-layouts: 14.7 us -> none  [reorder(): return x.reshape(n_exp, feat, x.shape[1])[order].reshape(x.shape)]
    unnamed x82 -> x30, local copies, waits for them, and re-layouts: 12.3 us -> 3.36 us
    ppermute x38, starting transfers between devices: 39 us -> 45.1 us  [swap(): return lax.ppermute(x, axis, [(i, i ^ k) for i in range(n)])]
    convert_element_type x9 -> x11, other arithmetic: 8.77 us -> 2.9 us  [the longest x1 1.06 us: local(): tok_blocks = gather_exp(tokens.T.astype(BF16))]
    select_n x5 -> x0, other arithmetic: 4.62 us -> none  [the longest x4 4.62 us: sum_tok(): low = jnp.where(core == 0, mine, other)]
  transfers between devices with their start and end apart: 38 -> 38, of which waited for: 17 -> 21; matrix products, arithmetic and copies ran while one was open for 34% -> 4% of each run, Pallas kernels for 0% -> 13%
where the time goes in v2:
time: 141 us; the launch traced here: 140 us
  waiting for transfers between devices  58.7 us (42%)
  starting transfers between devices  45.1 us (32%)
  Pallas kernels  25.1 us (18%)
  other arithmetic  5.26 us (4%)
  local copies, waits for them, and re-layouts  4.32 us (3%)
    ppermute x38, waiting for transfers between devices, swap(): return lax.ppermute(x, axis, [(i, i ^ k) for i in range(n)])  58.7 us
    ppermute x38, starting transfers between devices, swap(): return lax.ppermute(x, axis, [(i, i ^ k) for i in range(n)])  45.1 us
    pallas_call x6, Pallas kernels, call(): pl.pallas_call(body, out_shape=outs, in_specs=in_specs, out_specs=[pl.Blo...  14.3 us
    pallas_call x2, Pallas kernels, weight_grad(): pl.pallas_call(weight_grad_kernel, out_shape=sds((rows, columns), F32), g...  8.72 us
    unnamed x30, local copies, waits for them, and re-layouts  3.36 us
  transfers between devices with their start and end apart: 38, of which 21 were waited for; matrix products, arithmetic and copies ran while one was open for 4% of the time, Pallas kernels for 13%

profile of v2, /device:TPU:0, one launch (start us, length us, event | category | flops | bytes accessed | tf_op | source)
XLA Modules:
  0.0 140.2 jit_solution(12422748851072190773)
XLA Ops:
  0.6 1.1 convert_bitcast_fusion.refs_0_
  1.7 4.1 %collective-permute-start.10 = (bf16[160,768]{1,0:T(8,128)(2,1)S(1)}, bf16[160,768]{1,0:T(8,128)(2,1)S(1)}, u32[]{:S(2)}, u32[]{:S(2)}) collective-permute-start(bf16[160,768]{1,0:T(8,128)(2,1)S(1)} %convert_bitcast_fusion.refs_0_), channel_id=1, source_target_pairs={{0,4},{1,5},{2,6},{3,7},{4,0},{5,1},{6,2},{7,3},{8,12},{9,13},{10,... | collective-permute-start | bytes 737288 | tf_op jit(solution)/shard_map/ppermute | solution.py:34
  5.8 1.6 %collective-permute-start.8 = (bf16[160,768]{1,0:T(8,128)(2,1)S(1)}, bf16[160,768]{1,0:T(8,128)(2,1)S(1)}, u32[]{:S(2)}, u32[]{:S(2)}) collective-permute-start(bf16[160,768]{1,0:T(8,128)(2,1)S(1)} %convert_bitcast_fusion.refs_0_), channel_id=1, source_target_pairs={{0,2},{1,3},{2,0},{3,1},{4,6},{5,7},{6,4},{7,5},{8,10},{9,11},{10,... | collective-permute-start | bytes 737288 | tf_op jit(solution)/shard_map/ppermute | solution.py:34
  7.4 9.7 %collective-permute-done.10.refs_4_ = bf16[160,768]{1,0:T(8,128)(2,1)S(1)} collective-permute-done((bf16[160,768]{1,0:T(8,128)(2,1)S(1)}, bf16[160,768]{1,0:T(8,128)(2,1)S(1)}, u32[]{:S(2)}, u32[]{:S(2)}) %collective-permute-start.10) | collective-permute-done | bytes 245792 | tf_op jit(solution)/shard_map/ppermute | solution.py:34
  17.1 1.6 %collective-permute-start.11 = (bf16[160,768]{1,0:T(8,128)(2,1)S(1)}, bf16[160,768]{1,0:T(8,128)(2,1)S(1)}, u32[]{:S(2)}, u32[]{:S(2)}) collective-permute-start(bf16[160,768]{1,0:T(8,128)(2,1)S(1)} %collective-permute-done.10.refs_4_), channel_id=1, source_target_pairs={{0,1},{1,0},{2,3},{3,2},{4,5},{5,4},{6,7},{7,6},{8,9},{9,8},{10,11... | collective-permute-start | bytes 737288 | tf_op jit(solution)/shard_map/ppermute | solution.py:34
  18.7 1.1 convert_bitcast_fusion.1.refs_0_
  19.8 0.5 collective-permute-start.7
  20.3 3.9 %collective-permute-start.12 = (bf16[160,768]{1,0:T(8,128)(2,1)S(1)}, bf16[160,768]{1,0:T(8,128)(2,1)S(1)}, u32[]{:S(2)}, u32[]{:S(2)}) collective-permute-start(bf16[160,768]{1,0:T(8,128)(2,1)S(1)} %collective-permute-done.10.refs_4_), channel_id=1, source_target_pairs={{0,2},{1,3},{2,0},{3,1},{4,6},{5,7},{6,4},{7,5},{8,10},{9,11},{10,... | collective-permute-start | bytes 737288 | tf_op jit(solution)/shard_map/ppermute | solution.py:34
  24.3 1.5 %collective-permute-start.9 = (bf16[160,768]{1,0:T(8,128)(2,1)S(1)}, bf16[160,768]{1,0:T(8,128)(2,1)S(1)}, u32[]{:S(2)}, u32[]{:S(2)}) collective-permute-start(bf16[160,768]{1,0:T(8,128)(2,1)S(1)} %collective-permute-done.8.refs_2_), channel_id=1, source_target_pairs={{0,1},{1,0},{2,3},{3,2},{4,5},{5,4},{6,7},{7,6},{8,9},{9,8},{10,11... | collective-permute-start | bytes 737288 | tf_op jit(solution)/shard_map/ppermute | solution.py:34
  26.0 0.8 copy.15.refs_9_.slot_norm
  26.9 5.7 %collective-permute-done.3.refs_4_ = bf16[160,768]{1,0:T(8,128)(2,1)S(1)} collective-permute-done((bf16[160,768]{1,0:T(8,128)(2,1)S(1)}, bf16[160,768]{1,0:T(8,128)(2,1)S(1)}, u32[]{:S(2)}, u32[]{:S(2)}) %collective-permute-start.3) | collective-permute-done | bytes 245792 | tf_op jit(solution)/shard_map/ppermute | solution.py:34
  32.6 1.1 shard_map.102.idx
  33.7 0.7 collective-permute-done.12.refs_6_
  34.7 3.4 %collective-permute-done.13.refs_7_ = bf16[160,768]{1,0:T(8,128)(2,1)S(1)} collective-permute-done((bf16[160,768]{1,0:T(8,128)(2,1)S(1)}, bf16[160,768]{1,0:T(8,128)(2,1)S(1)}, u32[]{:S(2)}, u32[]{:S(2)}) %collective-permute-start.13) | collective-permute-done | bytes 245792 | tf_op jit(solution)/shard_map/ppermute | solution.py:34
  38.2 1.1 copy-done.12
  39.2 2.3 %shard_map.103 = (bf16[1280,768]{1,0:T(8,128)(2,1)}, f32[256,768]{1,0:T(8,128)}, f32[128,1280]{1,0:T(8,128)S(1)}, f32[128,1280]{1,0:T(8,128)S(1)}) custom-call(s32[2]{0:T(128)S(1)} %shard_map.102.idx, bf16[160,768]{1,0:T(8,128)(2,1)S(1)} %convert_bitcast_fusion.refs_0_, bf16[160,768]{1,0:T(8,128)(2,1)S(1)} %collective-permute-done.7.refs_1_, ...), custom_call_target="tpu_custom_call" | custom-call | flops 1006632960 | bytes 6685704 | tf_op jit(solution)/shard_map/pallas_call | solution.py:81
  41.7 1.8 %collective-permute-start.4 = (bf16[160,768]{1,0:T(8,128)(2,1)S(1)}, bf16[160,768]{1,0:T(8,128)(2,1)S(1)}, u32[]{:S(2)}, u32[]{:S(2)}) collective-permute-start(bf16[160,768]{1,0:T(8,128)(2,1)S(1)} %collective-permute-done.3.refs_4_), channel_id=1, source_target_pairs={{0,1},{1,0},{2,3},{3,2},{4,5},{5,4},{6,7},{7,6},{8,9},{9,8},{10,11... | collective-permute-start | bytes 737288 | tf_op jit(solution)/shard_map/ppermute | solution.py:34
  44.2 1.6 %collective-permute-start.18 = (f16[128,1408]{1,0:T(8,128)(2,1)S(1)}, f16[128,1408]{1,0:T(8,128)(2,1)S(1)}, u32[]{:S(2)}, u32[]{:S(2)}) collective-permute-start(f16[128,1408]{1,0:T(8,128)(2,1)S(1)} %pad_maximum_fusion), channel_id=1, source_target_pairs={{0,16},{8,24},{16,0},{24,8},{1,17},{9,25},{17,1},{25,9},{2,18},{10... | collective-permute-start | bytes 1081352 | tf_op jit(solution)/shard_map/ppermute | solution.py:34
  45.7 1.5 %collective-permute-start = (bf16[160,768]{1,0:T(8,128)(2,1)S(1)}, bf16[160,768]{1,0:T(8,128)(2,1)S(1)}, u32[]{:S(2)}, u32[]{:S(2)}) collective-permute-start(bf16[160,768]{1,0:T(8,128)(2,1)S(1)} %convert_bitcast_fusion.1.refs_0_), channel_id=1, source_target_pairs={{0,1},{1,0},{2,3},{3,2},{4,5},{5,4},{6,7},{7,6},{8,9},{9,8},{10,11... | collective-permute-start | bytes 737288 | tf_op jit(solution)/shard_map/ppermute | solution.py:34
  47.3 0.5 collective-permute-start.5
  47.8 2.6 %collective-permute-done.1.refs_2_ = bf16[160,768]{1,0:T(8,128)(2,1)S(1)} collective-permute-done((bf16[160,768]{1,0:T(8,128)(2,1)S(1)}, bf16[160,768]{1,0:T(8,128)(2,1)S(1)}, u32[]{:S(2)}, u32[]{:S(2)}) %collective-permute-start.1) | collective-permute-done | bytes 245792 | tf_op jit(solution)/shard_map/ppermute | solution.py:34
  50.4 1.8 %collective-permute-start.2 = (bf16[160,768]{1,0:T(8,128)(2,1)S(1)}, bf16[160,768]{1,0:T(8,128)(2,1)S(1)}, u32[]{:S(2)}, u32[]{:S(2)}) collective-permute-start(bf16[160,768]{1,0:T(8,128)(2,1)S(1)} %collective-permute-done.1.refs_2_), channel_id=1, source_target_pairs={{0,1},{1,0},{2,3},{3,2},{4,5},{5,4},{6,7},{7,6},{8,9},{9,8},{10,11... | collective-permute-start | bytes 737288 | tf_op jit(solution)/shard_map/ppermute | solution.py:34
  52.2 0.3 collective-permute-start.6
  52.5 3.7 %collective-permute-done.5.refs_6_ = bf16[160,768]{1,0:T(8,128)(2,1)S(1)} collective-permute-done((bf16[160,768]{1,0:T(8,128)(2,1)S(1)}, bf16[160,768]{1,0:T(8,128)(2,1)S(1)}, u32[]{:S(2)}, u32[]{:S(2)}) %collective-permute-start.5) | collective-permute-done | bytes 245792 | tf_op jit(solution)/shard_map/ppermute | solution.py:34
  56.2 4.4 %collective-permute-done.2.refs_3_ = bf16[160,768]{1,0:T(8,128)(2,1)S(1)} collective-permute-done((bf16[160,768]{1,0:T(8,128)(2,1)S(1)}, bf16[160,768]{1,0:T(8,128)(2,1)S(1)}, u32[]{:S(2)}, u32[]{:S(2)}) %collective-permute-start.2) | collective-permute-done | bytes 245792 | tf_op jit(solution)/shard_map/ppermute | solution.py:34
  60.5 1.5 %shard_map.104 = (bf16[1280,768]{1,0:T(8,128)(2,1)S(1)}, f32[128,1280]{1,0:T(8,128)S(1)}, bf16[128,1280]{1,0:T(8,128)(2,1)S(1)}) custom-call(s32[2]{0:T(128)S(1)} %pad_add_fusion.idx, bf16[160,768]{1,0:T(8,128)(2,1)S(1)} %convert_bitcast_fusion.1.refs_0_, bf16[160,768]{1,0:T(8,128)(2,1)S(1)} %collective-permute-done.refs_1_, ...), custom_call_target="tpu_custom_call" | custom-call | flops 503316480 | bytes 5704712 | tf_op jit(solution)/shard_map/pallas_call | solution.py:81
  62.5 0.6 collective-permute-start.19
  63.1 0.7 collective-permute-done.14
  63.8 1.5 %collective-permute-start.15 = (bf16[128,1280]{1,0:T(8,128)(2,1)S(1)}, bf16[128,1280]{1,0:T(8,128)(2,1)S(1)}, u32[]{:S(2)}, u32[]{:S(2)}) collective-permute-start(bf16[128,1280]{1,0:T(8,128)(2,1)S(1)} %fusion), channel_id=1, source_target_pairs={{0,16},{8,24},{16,0},{24,8},{1,17},{9,25},{17,1},{25,9},{2,18},{10... | collective-permute-start | bytes 983048 | tf_op jit(solution)/shard_map/ppermute | solution.py:34
  65.3 3.2 %shard_map.106 = (bf16[256,1280]{1,0:T(8,128)(2,1)S(1)}, bf16[256,1280]{1,0:T(8,128)(2,1)S(1)}, f32[256,1280]{1,0:T(8,128)S(1)}, f32[128,1280]{1,0:T(8,128)S(1)}, bf16[128,1280]{1,0:T(8,128)(2,1)S(1)}) custom-call(s32[2]{0:T(128)S(1)} %pad_add_fusion.idx, bf16[128,1280]{1,0:T(8,128)(2,1)S(1)} %shard_map.105.got_mine, ...), custom_call_target="tpu_custom_call" | custom-call | flops 1677721600 | bytes 11141128 | tf_op jit(solution)/shard_map/pallas_call | solution.py:81
  68.6 5.0 %collective-permute-done.15 = bf16[128,1280]{1,0:T(8,128)(2,1)S(1)} collective-permute-done((bf16[128,1280]{1,0:T(8,128)(2,1)S(1)}, bf16[128,1280]{1,0:T(8,128)(2,1)S(1)}, u32[]{:S(2)}, u32[]{:S(2)}) %collective-permute-start.15) | collective-permute-done | bytes 327712 | tf_op jit(solution)/shard_map/ppermute | solution.py:34
  73.9 1.5 %collective-permute-start.23 = (bf16[128,1280]{1,0:T(8,128)(2,1)S(1)}, bf16[128,1280]{1,0:T(8,128)(2,1)S(1)}, u32[]{:S(2)}, u32[]{:S(2)}) collective-permute-start(bf16[128,1280]{1,0:T(8,128)(2,1)S(1)} %fusion.1), channel_id=1, source_target_pairs={{0,16},{8,24},{16,0},{24,8},{1,17},{9,25},{17,1},{25,9},{2,18},{10... | collective-permute-start | bytes 983048 | tf_op jit(solution)/shard_map/ppermute | solution.py:34
  75.4 2.7 %shard_map.107 = (bf16[256,1280]{1,0:T(8,128)(2,1)S(1)}, bf16[256,1280]{1,0:T(8,128)(2,1)S(1)}, f32[128,1280]{1,0:T(8,128)S(1)}, bf16[128,1280]{1,0:T(8,128)(2,1)S(1)}) custom-call(s32[2]{0:T(128)S(1)} %pad_add_fusion.idx, bf16[128,1280]{1,0:T(8,128)(2,1)S(1)} %add_convert_fusion.1.got_mine, bf16[128,1280]{1,0:T(8,128)(2,1)S(1)} %collective-permute-done.16.got_other, ...), custom_call_target="tpu_custom_call" | custom-call | flops 1677721600 | bytes 10813448 | tf_op jit(solution)/shard_map/pallas_call | solution.py:81
  78.4 5.7 %collective-permute-done.23 = bf16[128,1280]{1,0:T(8,128)(2,1)S(1)} collective-permute-done((bf16[128,1280]{1,0:T(8,128)(2,1)S(1)}, bf16[128,1280]{1,0:T(8,128)(2,1)S(1)}, u32[]{:S(2)}, u32[]{:S(2)}) %collective-permute-start.23) | collective-permute-done | bytes 327712 | tf_op jit(solution)/shard_map/ppermute | solution.py:34
  84.4 1.5 %collective-permute-start.21 = (bf16[128,1280]{1,0:T(8,128)(2,1)S(1)}, bf16[128,1280]{1,0:T(8,128)(2,1)S(1)}, u32[]{:S(2)}, u32[]{:S(2)}) collective-permute-start(bf16[128,1280]{1,0:T(8,128)(2,1)S(1)} %get-tuple-element.58), channel_id=1, source_target_pairs={{0,16},{8,24},{16,0},{24,8},{1,17},{9,25},{17,1},{25,9},{2,18},{10... | collective-permute-start | bytes 983048 | tf_op jit(solution)/shard_map/ppermute | solution.py:34
  85.9 1.3 shard_map.108
  87.2 1.8 %collective-permute-start.25 = (f32[1,768]{1,0:T(1,128)S(1)}, f32[1,768]{1,0:T(1,128)S(1)}, u32[]{:S(2)}, u32[]{:S(2)}) collective-permute-start(f32[1,768]{1,0:T(1,128)S(1)} %get-tuple-element.42), channel_id=1, source_target_pairs={{0,1},{1,0},{2,3},{3,2},{4,5},{5,4},{6,7},{7,6},{8,9},{9,8},{10,11... | collective-permute-start | bytes 9224 | tf_op jit(solution)/shard_map/ppermute | solution.py:34
  89.0 1.9 %collective-permute-done.25 = f32[1,768]{1,0:T(1,128)S(1)} collective-permute-done((f32[1,768]{1,0:T(1,128)S(1)}, f32[1,768]{1,0:T(1,128)S(1)}, u32[]{:S(2)}, u32[]{:S(2)}) %collective-permute-start.25) | collective-permute-done | bytes 3104 | tf_op jit(solution)/shard_map/ppermute | solution.py:34
  90.9 1.7 %collective-permute-start.26 = (f32[1,768]{1,0:T(1,128)S(1)}, f32[1,768]{1,0:T(1,128)S(1)}, u32[]{:S(2)}, u32[]{:S(2)}) collective-permute-start(f32[1,768]{1,0:T(1,128)S(1)} %add.83), channel_id=1, source_target_pairs={{0,2},{1,3},{2,0},{3,1},{4,6},{5,7},{6,4},{7,5},{8,10},{9,11},{10,... | collective-permute-start | bytes 9224 | tf_op jit(solution)/shard_map/ppermute | solution.py:34
  92.6 1.9 %collective-permute-done.26 = f32[1,768]{1,0:T(1,128)S(1)} collective-permute-done((f32[1,768]{1,0:T(1,128)S(1)}, f32[1,768]{1,0:T(1,128)S(1)}, u32[]{:S(2)}, u32[]{:S(2)}) %collective-permute-start.26) | collective-permute-done | bytes 3104 | tf_op jit(solution)/shard_map/ppermute | solution.py:34
  94.5 3.8 %collective-permute-start.27 = (f32[1,768]{1,0:T(1,128)S(1)}, f32[1,768]{1,0:T(1,128)S(1)}, u32[]{:S(2)}, u32[]{:S(2)}) collective-permute-start(f32[1,768]{1,0:T(1,128)S(1)} %add.84), channel_id=1, source_target_pairs={{0,4},{1,5},{2,6},{3,7},{4,0},{5,1},{6,2},{7,3},{8,12},{9,13},{10,... | collective-permute-start | bytes 9224 | tf_op jit(solution)/shard_map/ppermute | solution.py:34
  98.3 1.6 %collective-permute-done.27 = f32[1,768]{1,0:T(1,128)S(1)} collective-permute-done((f32[1,768]{1,0:T(1,128)S(1)}, f32[1,768]{1,0:T(1,128)S(1)}, u32[]{:S(2)}, u32[]{:S(2)}) %collective-permute-start.27) | collective-permute-done | bytes 3104 | tf_op jit(solution)/shard_map/ppermute | solution.py:34
  99.9 0.8 shard_map.109.got_mine
  100.7 2.0 %collective-permute-done.28.got_other = bf16[128,1280]{1,0:T(8,128)(2,1)} collective-permute-done((bf16[128,1280]{1,0:T(8,128)(2,1)}, bf16[128,1280]{1,0:T(8,128)(2,1)}, u32[]{:S(2)}, u32[]{:S(2)}) %collective-permute-start.28) | collective-permute-done | bytes 327712 | tf_op jit(solution)/shard_map/ppermute | solution.py:34
  102.6 1.1 copy-done.5
  103.8 1.1 copy-done.13
  104.9 3.4 %shard_map.110 = (bf16[256,768]{1,0:T(8,128)(2,1)S(1)}, f32[160,768]{1,0:T(8,128)S(1)}, bf16[160,768]{1,0:T(8,128)(2,1)S(1)}, f32[160,768]{1,0:T(8,128)S(1)}, bf...) custom-call(s32[2]{0:T(128)S(1)} %pad_add_fusion.idx, ...), custom_call_target="tpu_custom_call" | custom-call | flops 1509949440 | bytes 8854536 | tf_op jit(solution)/shard_map/pallas_call | solution.py:81
  108.2 1.5 %collective-permute-start.30 = (bf16[160,768]{1,0:T(8,128)(2,1)S(1)}, bf16[160,768]{1,0:T(8,128)(2,1)S(1)}, u32[]{:S(2)}, u32[]{:S(2)}) collective-permute-start(bf16[160,768]{1,0:T(8,128)(2,1)S(1)} %get-tuple-element.49), channel_id=1, source_target_pairs={{0,1},{1,0},{2,3},{3,2},{4,5},{5,4},{6,7},{7,6},{8,9},{9,8},{10,11... | collective-permute-start | bytes 737288 | tf_op jit(solution)/shard_map/ppermute | solution.py:34
  109.8 0.7 fusion.6
  110.5 0.6 collective-permute-start.29
  111.1 0.9 collective-permute-start.32
  112.0 1.1 collective-permute-start.34
  113.3 4.4 %shard_map.111 = f32[1280,1280]{1,0:T(8,128)} custom-call(bf16[256,1280]{1,0:T(8,128)(2,1)S(1)} %get-tuple-element.45.slot_in.left, bf16[256,1280]{1,0:T(8,128)(2,1)S(1)} %copy-done.11, bf16[256,768]{1,0:T(8,128)(2,1)S(1)} %get-tuple-element.54._), custom_call_target="tpu_custom_call" | custom-call | flops 838860800 | bytes 6553600 | tf_op jit(solution)/shard_map/pallas_call | solution.py:238
  117.7 1.0 collective-permute-start.31
  118.7 1.3 collective-permute-done.32
  120.1 1.5 %collective-permute-start.33 = (bf16[160,768]{1,0:T(8,128)(2,1)S(1)}, bf16[160,768]{1,0:T(8,128)(2,1)S(1)}, u32[]{:S(2)}, u32[]{:S(2)}) collective-permute-start(bf16[160,768]{1,0:T(8,128)(2,1)S(1)} %add_convert_fusion.3), channel_id=1, source_target_pairs={{0,1},{1,0},{2,3},{3,2},{4,5},{5,4},{6,7},{7,6},{8,9},{9,8},{10,11... | collective-permute-start | bytes 737288 | tf_op jit(solution)/shard_map/ppermute | solution.py:34
  121.7 1.5 %collective-permute-start.37 = (bf16[320,256]{1,0:T(8,128)(2,1)S(1)}, bf16[320,256]{1,0:T(8,128)(2,1)S(1)}, u32[]{:S(2)}, u32[]{:S(2)}) collective-permute-start(bf16[320,256]{1,0:T(8,128)(2,1)S(1)} %fusion.3), channel_id=1, source_target_pairs={{0,16},{8,24},{16,0},{24,8},{1,17},{9,25},{17,1},{25,9},{2,18},{10... | collective-permute-start | bytes 491528 | tf_op jit(solution)/shard_map/ppermute | solution.py:34
  123.2 2.0 %collective-permute-done.34 = bf16[160,768]{1,0:T(8,128)(2,1)S(1)} collective-permute-done((bf16[160,768]{1,0:T(8,128)(2,1)S(1)}, bf16[160,768]{1,0:T(8,128)(2,1)S(1)}, u32[]{:S(2)}, u32[]{:S(2)}) %collective-permute-start.34) | collective-permute-done | bytes 245792 | tf_op jit(solution)/shard_map/ppermute | solution.py:34
  125.3 1.6 %collective-permute-done.33 = bf16[160,768]{1,0:T(8,128)(2,1)S(1)} collective-permute-done((bf16[160,768]{1,0:T(8,128)(2,1)S(1)}, bf16[160,768]{1,0:T(8,128)(2,1)S(1)}, u32[]{:S(2)}, u32[]{:S(2)}) %collective-permute-start.33) | collective-permute-done | bytes 245792 | tf_op jit(solution)/shard_map/ppermute | solution.py:34
  126.9 3.0 %collective-permute-start.35 = (bf16[160,768]{1,0:T(8,128)(2,1)S(1)}, bf16[160,768]{1,0:T(8,128)(2,1)S(1)}, u32[]{:S(2)}, u32[]{:S(2)}) collective-permute-start(bf16[160,768]{1,0:T(8,128)(2,1)S(1)} %add_convert_fusion.2), channel_id=1, source_target_pairs={{0,4},{1,5},{2,6},{3,7},{4,0},{5,1},{6,2},{7,3},{8,12},{9,13},{10,... | collective-permute-start | bytes 737288 | tf_op jit(solution)/shard_map/ppermute | solution.py:34
  129.9 4.4 %shard_map.112 = f32[1280,1280]{1,0:T(8,128)} custom-call(bf16[256,1280]{1,0:T(8,128)(2,1)S(1)} %copy-done.7, bf16[256,1280]{1,0:T(8,128)(2,1)S(1)} %copy-done.9, bf16[256,768]{1,0:T(8,128)(2,1)S(1)} %get-tuple-element.54._), custom_call_target="tpu_custom_call" | custom-call | flops 838860800 | bytes 6553600 | tf_op jit(solution)/shard_map/pallas_call | solution.py:238
  134.3 0.8 bitcast_add_fusion.1
  135.0 4.2 %collective-permute-done.35 = bf16[160,768]{1,0:T(8,128)(2,1)S(1)} collective-permute-done((bf16[160,768]{1,0:T(8,128)(2,1)S(1)}, bf16[160,768]{1,0:T(8,128)(2,1)S(1)}, u32[]{:S(2)}, u32[]{:S(2)}) %collective-permute-start.35) | collective-permute-done | bytes 245792 | tf_op jit(solution)/shard_map/ppermute | solution.py:34
  139.3 0.9 add_bitcast_fusion
  (86 shorter events, 3.3 us)
Async XLA Ops:
  1.7 15.4 %collective-permute-start.10 = (bf16[160,768]{1,0:T(8,128)(2,1)S(1)}, bf16[160,768]{1,0:T(8,128)(2,1)S(1)}, u32[]{:S(2)}, u32[]{:S(2)}) collective-permute-start(bf16[160,768]{1,0:T(8,128)(2,1)S(1)} %convert_bitcast_fusion.refs_0_), channel_id=1, source_target_pairs={{0,4},{1,5},{2,6},{3,7},{4,0},{5,1},{6,2},{7,3},{8,12},{9,13},{10,... | collective-permute-start | bytes 737288 | tf_op jit(solution)/shard_map/ppermute | solution.py:34
  5.8 18.5 %collective-permute-start.8 = (bf16[160,768]{1,0:T(8,128)(2,1)S(1)}, bf16[160,768]{1,0:T(8,128)(2,1)S(1)}, u32[]{:S(2)}, u32[]{:S(2)}) collective-permute-start(bf16[160,768]{1,0:T(8,128)(2,1)S(1)} %convert_bitcast_fusion.refs_0_), channel_id=1, source_target_pairs={{0,2},{1,3},{2,0},{3,1},{4,6},{5,7},{6,4},{7,5},{8,10},{9,11},{10,... | collective-permute-start | bytes 737288 | tf_op jit(solution)/shard_map/ppermute | solution.py:34
  17.1 8.9 %collective-permute-start.11 = (bf16[160,768]{1,0:T(8,128)(2,1)S(1)}, bf16[160,768]{1,0:T(8,128)(2,1)S(1)}, u32[]{:S(2)}, u32[]{:S(2)}) collective-permute-start(bf16[160,768]{1,0:T(8,128)(2,1)S(1)} %collective-permute-done.10.refs_4_), channel_id=1, source_target_pairs={{0,1},{1,0},{2,3},{3,2},{4,5},{5,4},{6,7},{7,6},{8,9},{9,8},{10,11... | collective-permute-start | bytes 737288 | tf_op jit(solution)/shard_map/ppermute | solution.py:34
  19.7 12.8 %collective-permute-start.3 = (bf16[160,768]{1,0:T(8,128)(2,1)S(1)}, bf16[160,768]{1,0:T(8,128)(2,1)S(1)}, u32[]{:S(2)}, u32[]{:S(2)}) collective-permute-start(bf16[160,768]{1,0:T(8,128)(2,1)S(1)} %convert_bitcast_fusion.1.refs_0_), channel_id=1, source_target_pairs={{0,4},{1,5},{2,6},{3,7},{4,0},{5,1},{6,2},{7,3},{8,12},{9,13},{10,... | collective-permute-start | bytes 737288 | tf_op jit(solution)/shard_map/ppermute | solution.py:34
  19.8 13.9 %collective-permute-start.7 = (bf16[160,768]{1,0:T(8,128)(2,1)S(1)}, bf16[160,768]{1,0:T(8,128)(2,1)S(1)}, u32[]{:S(2)}, u32[]{:S(2)}) collective-permute-start(bf16[160,768]{1,0:T(8,128)(2,1)S(1)} %convert_bitcast_fusion.refs_0_), channel_id=1, source_target_pairs={{0,1},{1,0},{2,3},{3,2},{4,5},{5,4},{6,7},{7,6},{8,9},{9,8},{10,11... | collective-permute-start | bytes 737288 | tf_op jit(solution)/shard_map/ppermute | solution.py:34
  20.3 14.1 %collective-permute-start.12 = (bf16[160,768]{1,0:T(8,128)(2,1)S(1)}, bf16[160,768]{1,0:T(8,128)(2,1)S(1)}, u32[]{:S(2)}, u32[]{:S(2)}) collective-permute-start(bf16[160,768]{1,0:T(8,128)(2,1)S(1)} %collective-permute-done.10.refs_4_), channel_id=1, source_target_pairs={{0,2},{1,3},{2,0},{3,1},{4,6},{5,7},{6,4},{7,5},{8,10},{9,11},{10,... | collective-permute-start | bytes 737288 | tf_op jit(solution)/shard_map/ppermute | solution.py:34
  24.3 10.5 %collective-permute-start.9 = (bf16[160,768]{1,0:T(8,128)(2,1)S(1)}, bf16[160,768]{1,0:T(8,128)(2,1)S(1)}, u32[]{:S(2)}, u32[]{:S(2)}) collective-permute-start(bf16[160,768]{1,0:T(8,128)(2,1)S(1)} %collective-permute-done.8.refs_2_), channel_id=1, source_target_pairs={{0,1},{1,0},{2,3},{3,2},{4,5},{5,4},{6,7},{7,6},{8,9},{9,8},{10,11... | collective-permute-start | bytes 737288 | tf_op jit(solution)/shard_map/ppermute | solution.py:34
  26.0 12.1 %collective-permute-start.13 = (bf16[160,768]{1,0:T(8,128)(2,1)S(1)}, bf16[160,768]{1,0:T(8,128)(2,1)S(1)}, u32[]{:S(2)}, u32[]{:S(2)}) collective-permute-start(bf16[160,768]{1,0:T(8,128)(2,1)S(1)} %collective-permute-done.11.refs_5_), channel_id=1, source_target_pairs={{0,2},{1,3},{2,0},{3,1},{4,6},{5,7},{6,4},{7,5},{8,10},{9,11},{10,... | collective-permute-start | bytes 737288 | tf_op jit(solution)/shard_map/ppermute | solution.py:34
  38.2 1.1 copy-start.12
  41.6 10.9 %copy-start.14 = (f32[768]{0:T(1024)S(1)}, f32[768]{0:T(1024)}, u32[]{:S(2)}) copy-start(f32[768]{0:T(1024)} %param.13) | copy-start | bytes 9220
  41.6 18.9 %copy-start.3 = (f32[256,768]{1,0:T(8,128)S(1)}, f32[256,768]{1,0:T(8,128)}, u32[]{:S(2)}) copy-start(f32[256,768]{1,0:T(8,128)} %get-tuple-element.31.refs_8_.logits) | copy-start | bytes 2359300
  41.6 2.1 %collective-permute-start.17 = (f32[128,1280]{1,0:T(8,128)S(1)}, f32[128,1280]{1,0:T(8,128)S(1)}, u32[]{:S(2)}, u32[]{:S(2)}) collective-permute-start(f32[128,1280]{1,0:T(8,128)S(1)} %get-tuple-element.35), channel_id=1, source_target_pairs={{0,8},{8,0},{16,24},{24,16},{1,9},{9,1},{17,25},{25,17},{2,10},{10... | collective-permute-start | bytes 1966088 | tf_op jit(solution)/shard_map/ppermute | solution.py:34
  41.6 8.8 %collective-permute-start.1 = (bf16[160,768]{1,0:T(8,128)(2,1)S(1)}, bf16[160,768]{1,0:T(8,128)(2,1)S(1)}, u32[]{:S(2)}, u32[]{:S(2)}) collective-permute-start(bf16[160,768]{1,0:T(8,128)(2,1)S(1)} %convert_bitcast_fusion.1.refs_0_), channel_id=1, source_target_pairs={{0,2},{1,3},{2,0},{3,1},{4,6},{5,7},{6,4},{7,5},{8,10},{9,11},{10,... | collective-permute-start | bytes 737288 | tf_op jit(solution)/shard_map/ppermute | solution.py:34
  41.7 10.5 %collective-permute-start.4 = (bf16[160,768]{1,0:T(8,128)(2,1)S(1)}, bf16[160,768]{1,0:T(8,128)(2,1)S(1)}, u32[]{:S(2)}, u32[]{:S(2)}) collective-permute-start(bf16[160,768]{1,0:T(8,128)(2,1)S(1)} %collective-permute-done.3.refs_4_), channel_id=1, source_target_pairs={{0,1},{1,0},{2,3},{3,2},{4,5},{5,4},{6,7},{7,6},{8,9},{9,8},{10,11... | collective-permute-start | bytes 737288 | tf_op jit(solution)/shard_map/ppermute | solution.py:34
  44.2 17.9 %collective-permute-start.18 = (f16[128,1408]{1,0:T(8,128)(2,1)S(1)}, f16[128,1408]{1,0:T(8,128)(2,1)S(1)}, u32[]{:S(2)}, u32[]{:S(2)}) collective-permute-start(f16[128,1408]{1,0:T(8,128)(2,1)S(1)} %pad_maximum_fusion), channel_id=1, source_target_pairs={{0,16},{8,24},{16,0},{24,8},{1,17},{9,25},{17,1},{25,9},{2,18},{10... | collective-permute-start | bytes 1081352 | tf_op jit(solution)/shard_map/ppermute | solution.py:34
  45.7 10.4 %collective-permute-start = (bf16[160,768]{1,0:T(8,128)(2,1)S(1)}, bf16[160,768]{1,0:T(8,128)(2,1)S(1)}, u32[]{:S(2)}, u32[]{:S(2)}) collective-permute-start(bf16[160,768]{1,0:T(8,128)(2,1)S(1)} %convert_bitcast_fusion.1.refs_0_), channel_id=1, source_target_pairs={{0,1},{1,0},{2,3},{3,2},{4,5},{5,4},{6,7},{7,6},{8,9},{9,8},{10,11... | collective-permute-start | bytes 737288 | tf_op jit(solution)/shard_map/ppermute | solution.py:34
  47.3 8.9 %collective-permute-start.5 = (bf16[160,768]{1,0:T(8,128)(2,1)S(1)}, bf16[160,768]{1,0:T(8,128)(2,1)S(1)}, u32[]{:S(2)}, u32[]{:S(2)}) collective-permute-start(bf16[160,768]{1,0:T(8,128)(2,1)S(1)} %collective-permute-done.3.refs_4_), channel_id=1, source_target_pairs={{0,2},{1,3},{2,0},{3,1},{4,6},{5,7},{6,4},{7,5},{8,10},{9,11},{10,... | collective-permute-start | bytes 737288 | tf_op jit(solution)/shard_map/ppermute | solution.py:34
  50.4 10.1 %collective-permute-start.2 = (bf16[160,768]{1,0:T(8,128)(2,1)S(1)}, bf16[160,768]{1,0:T(8,128)(2,1)S(1)}, u32[]{:S(2)}, u32[]{:S(2)}) collective-permute-start(bf16[160,768]{1,0:T(8,128)(2,1)S(1)} %collective-permute-done.1.refs_2_), channel_id=1, source_target_pairs={{0,1},{1,0},{2,3},{3,2},{4,5},{5,4},{6,7},{7,6},{8,9},{9,8},{10,11... | collective-permute-start | bytes 737288 | tf_op jit(solution)/shard_map/ppermute | solution.py:34
  52.2 8.3 %collective-permute-start.6 = (bf16[160,768]{1,0:T(8,128)(2,1)S(1)}, bf16[160,768]{1,0:T(8,128)(2,1)S(1)}, u32[]{:S(2)}, u32[]{:S(2)}) collective-permute-start(bf16[160,768]{1,0:T(8,128)(2,1)S(1)} %collective-permute-done.4.refs_5_), channel_id=1, source_target_pairs={{0,2},{1,3},{2,0},{3,1},{4,6},{5,7},{6,4},{7,5},{8,10},{9,11},{10,... | collective-permute-start | bytes 737288 | tf_op jit(solution)/shard_map/ppermute | solution.py:34
  60.5 4.8 %copy-start.1 = (bf16[1,1280,1280]{2,1,0:T(8,128)(2,1)S(1)}, bf16[1,1280,1280]{2,1,0:T(8,128)(2,1)}, u32[]{:S(2)}) copy-start(bf16[1,1280,1280]{2,1,0:T(8,128)(2,1)} %param.11) | copy-start | bytes 9830404
  62.0 1.7 %collective-permute-start.14 = (bf16[128,1280]{1,0:T(8,128)(2,1)S(1)}, bf16[128,1280]{1,0:T(8,128)(2,1)S(1)}, u32[]{:S(2)}, u32[]{:S(2)}) collective-permute-start(bf16[128,1280]{1,0:T(8,128)(2,1)S(1)} %get-tuple-element.33._), channel_id=1, source_target_pairs={{0,8},{8,0},{16,24},{24,16},{1,9},{9,1},{17,25},{25,17},{2,10},{10... | collective-permute-start | bytes 983048 | tf_op jit(solution)/shard_map/ppermute | solution.py:34
  62.3 3.0 %copy-start = (bf16[1,1280,1280]{2,1,0:T(8,128)(2,1)S(1)}, bf16[1,1280,1280]{2,1,0:T(8,128)(2,1)}, u32[]{:S(2)}) copy-start(bf16[1,1280,1280]{2,1,0:T(8,128)(2,1)} %param.10) | copy-start | bytes 9830404
  62.5 2.8 %collective-permute-start.19 = (bf16[128,1280]{1,0:T(8,128)(2,1)S(1)}, bf16[128,1280]{1,0:T(8,128)(2,1)S(1)}, u32[]{:S(2)}, u32[]{:S(2)}) collective-permute-start(bf16[128,1280]{1,0:T(8,128)(2,1)S(1)} %shard_map.105.got_mine), channel_id=1, source_target_pairs={{0,8},{8,0},{16,24},{24,16},{1,9},{9,1},{17,25},{25,17},{2,10},{10... | collective-permute-start | bytes 983048 | tf_op jit(solution)/shard_map/ppermute | solution.py:34
  63.8 9.8 %collective-permute-start.15 = (bf16[128,1280]{1,0:T(8,128)(2,1)S(1)}, bf16[128,1280]{1,0:T(8,128)(2,1)S(1)}, u32[]{:S(2)}, u32[]{:S(2)}) collective-permute-start(bf16[128,1280]{1,0:T(8,128)(2,1)S(1)} %fusion), channel_id=1, source_target_pairs={{0,16},{8,24},{16,0},{24,8},{1,17},{9,25},{17,1},{25,9},{2,18},{10... | collective-permute-start | bytes 983048 | tf_op jit(solution)/shard_map/ppermute | solution.py:34
  68.5 9.6 %copy-start.6 = (bf16[256,1280]{1,0:T(8,128)(2,1)}, bf16[256,1280]{1,0:T(8,128)(2,1)S(1)}, u32[]{:S(2)}) copy-start(bf16[256,1280]{1,0:T(8,128)(2,1)S(1)} %get-tuple-element.56.left) | copy-start | bytes 1966084
  68.6 5.3 %collective-permute-start.22 = (bf16[128,1280]{1,0:T(8,128)(2,1)S(1)}, bf16[128,1280]{1,0:T(8,128)(2,1)S(1)}, u32[]{:S(2)}, u32[]{:S(2)}) collective-permute-start(bf16[128,1280]{1,0:T(8,128)(2,1)S(1)} %get-tuple-element.40), channel_id=1, source_target_pairs={{0,8},{8,0},{16,24},{24,16},{1,9},{9,1},{17,25},{25,17},{2,10},{10... | collective-permute-start | bytes 983048 | tf_op jit(solution)/shard_map/ppermute | solution.py:34
  73.7 1.7 %collective-permute-start.16 = (bf16[128,1280]{1,0:T(8,128)(2,1)S(1)}, bf16[128,1280]{1,0:T(8,128)(2,1)S(1)}, u32[]{:S(2)}, u32[]{:S(2)}) collective-permute-start(bf16[128,1280]{1,0:T(8,128)(2,1)S(1)} %add_convert_fusion.1.got_mine), channel_id=1, source_target_pairs={{0,8},{8,0},{16,24},{24,16},{1,9},{9,1},{17,25},{25,17},{2,10},{10... | collective-permute-start | bytes 983048 | tf_op jit(solution)/shard_map/ppermute | solution.py:34
  73.9 10.2 %collective-permute-start.23 = (bf16[128,1280]{1,0:T(8,128)(2,1)S(1)}, bf16[128,1280]{1,0:T(8,128)(2,1)S(1)}, u32[]{:S(2)}, u32[]{:S(2)}) collective-permute-start(bf16[128,1280]{1,0:T(8,128)(2,1)S(1)} %fusion.1), channel_id=1, source_target_pairs={{0,16},{8,24},{16,0},{24,8},{1,17},{9,25},{17,1},{25,9},{2,18},{10... | collective-permute-start | bytes 983048 | tf_op jit(solution)/shard_map/ppermute | solution.py:34
  78.1 9.1 %copy-start.8 = (bf16[256,1280]{1,0:T(8,128)(2,1)}, bf16[256,1280]{1,0:T(8,128)(2,1)S(1)}, u32[]{:S(2)}) copy-start(bf16[256,1280]{1,0:T(8,128)(2,1)S(1)} %get-tuple-element.57.right) | copy-start | bytes 1966084
  78.1 9.1 %copy-start.10 = (bf16[256,1280]{1,0:T(8,128)(2,1)}, bf16[256,1280]{1,0:T(8,128)(2,1)S(1)}, u32[]{:S(2)}) copy-start(bf16[256,1280]{1,0:T(8,128)(2,1)S(1)} %get-tuple-element.55.right) | copy-start | bytes 1966084
  78.1 6.1 %collective-permute-start.20 = (bf16[128,1280]{1,0:T(8,128)(2,1)S(1)}, bf16[128,1280]{1,0:T(8,128)(2,1)S(1)}, u32[]{:S(2)}, u32[]{:S(2)}) collective-permute-start(bf16[128,1280]{1,0:T(8,128)(2,1)S(1)} %get-tuple-element.38), channel_id=1, source_target_pairs={{0,8},{8,0},{16,24},{24,16},{1,9},{9,1},{17,25},{25,17},{2,10},{10... | collective-permute-start | bytes 983048 | tf_op jit(solution)/shard_map/ppermute | solution.py:34
  84.2 1.7 %collective-permute-start.24 = (bf16[128,1280]{1,0:T(8,128)(2,1)S(1)}, bf16[128,1280]{1,0:T(8,128)(2,1)S(1)}, u32[]{:S(2)}, u32[]{:S(2)}) collective-permute-start(bf16[128,1280]{1,0:T(8,128)(2,1)S(1)} %add_convert_fusion.got_mine), channel_id=1, source_target_pairs={{0,8},{8,0},{16,24},{24,16},{1,9},{9,1},{17,25},{25,17},{2,10},{10... | collective-permute-start | bytes 983048 | tf_op jit(solution)/shard_map/ppermute | solution.py:34
  84.4 15.5 %collective-permute-start.21 = (bf16[128,1280]{1,0:T(8,128)(2,1)S(1)}, bf16[128,1280]{1,0:T(8,128)(2,1)S(1)}, u32[]{:S(2)}, u32[]{:S(2)}) collective-permute-start(bf16[128,1280]{1,0:T(8,128)(2,1)S(1)} %get-tuple-element.58), channel_id=1, source_target_pairs={{0,16},{8,24},{16,0},{24,8},{1,17},{9,25},{17,1},{25,9},{2,18},{10... | collective-permute-start | bytes 983048 | tf_op jit(solution)/shard_map/ppermute | solution.py:34
  85.9 16.7 %copy-start.2 = (bf16[1280,768]{1,0:T(8,128)(2,1)S(1)}, bf16[1280,768]{1,0:T(8,128)(2,1)}, u32[]{:S(2)}) copy-start(bf16[1280,768]{1,0:T(8,128)(2,1)} %get-tuple-element.43.tok) | copy-start | bytes 5898244
  87.2 13.5 %copy-start.4 = (f32[256,768]{1,0:T(8,128)}, f32[256,768]{1,0:T(8,128)S(1)}, u32[]{:S(2)}) copy-start(f32[256,768]{1,0:T(8,128)S(1)} %get-tuple-element.44.weighted) | copy-start | bytes 2359300
  87.2 3.7 %collective-permute-start.25 = (f32[1,768]{1,0:T(1,128)S(1)}, f32[1,768]{1,0:T(1,128)S(1)}, u32[]{:S(2)}, u32[]{:S(2)}) collective-permute-start(f32[1,768]{1,0:T(1,128)S(1)} %get-tuple-element.42), channel_id=1, source_target_pairs={{0,1},{1,0},{2,3},{3,2},{4,5},{5,4},{6,7},{7,6},{8,9},{9,8},{10,11... | collective-permute-start | bytes 9224 | tf_op jit(solution)/shard_map/ppermute | solution.py:34
  90.9 3.6 %collective-permute-start.26 = (f32[1,768]{1,0:T(1,128)S(1)}, f32[1,768]{1,0:T(1,128)S(1)}, u32[]{:S(2)}, u32[]{:S(2)}) collective-permute-start(f32[1,768]{1,0:T(1,128)S(1)} %add.83), channel_id=1, source_target_pairs={{0,2},{1,3},{2,0},{3,1},{4,6},{5,7},{6,4},{7,5},{8,10},{9,11},{10,... | collective-permute-start | bytes 9224 | tf_op jit(solution)/shard_map/ppermute | solution.py:34
  94.5 5.3 %collective-permute-start.27 = (f32[1,768]{1,0:T(1,128)S(1)}, f32[1,768]{1,0:T(1,128)S(1)}, u32[]{:S(2)}, u32[]{:S(2)}) collective-permute-start(f32[1,768]{1,0:T(1,128)S(1)} %add.84), channel_id=1, source_target_pairs={{0,4},{1,5},{2,6},{3,7},{4,0},{5,1},{6,2},{7,3},{8,12},{9,13},{10,... | collective-permute-start | bytes 9224 | tf_op jit(solution)/shard_map/ppermute | solution.py:34
  100.7 2.0 %collective-permute-start.28 = (bf16[128,1280]{1,0:T(8,128)(2,1)}, bf16[128,1280]{1,0:T(8,128)(2,1)}, u32[]{:S(2)}, u32[]{:S(2)}) collective-permute-start(bf16[128,1280]{1,0:T(8,128)(2,1)} %shard_map.109.got_mine), channel_id=1, source_target_pairs={{0,8},{8,0},{16,24},{24,16},{1,9},{9,1},{17,25},{25,17},{2,10},{10... | collective-permute-start | bytes 983048 | tf_op jit(solution)/shard_map/ppermute | solution.py:34
  102.6 1.1 copy-start.5
  103.8 1.1 copy-start.13
  108.2 9.4 %collective-permute-start.30 = (bf16[160,768]{1,0:T(8,128)(2,1)S(1)}, bf16[160,768]{1,0:T(8,128)(2,1)S(1)}, u32[]{:S(2)}, u32[]{:S(2)}) collective-permute-start(bf16[160,768]{1,0:T(8,128)(2,1)S(1)} %get-tuple-element.49), channel_id=1, source_target_pairs={{0,1},{1,0},{2,3},{3,2},{4,5},{5,4},{6,7},{7,6},{8,9},{9,8},{10,11... | collective-permute-start | bytes 737288 | tf_op jit(solution)/shard_map/ppermute | solution.py:34
  109.8 3.5 %copy-start.11 = (bf16[256,1280]{1,0:T(8,128)(2,1)S(1)}, bf16[256,1280]{1,0:T(8,128)(2,1)}, u32[]{:S(2)}) copy-start(bf16[256,1280]{1,0:T(8,128)(2,1)} %copy-done.10) | copy-start | bytes 1966084
  110.5 24.6 %collective-permute-start.29 = (bf16[160,768]{1,0:T(8,128)(2,1)S(1)}, bf16[160,768]{1,0:T(8,128)(2,1)S(1)}, u32[]{:S(2)}, u32[]{:S(2)}) collective-permute-start(bf16[160,768]{1,0:T(8,128)(2,1)S(1)} %get-tuple-element.47), channel_id=1, source_target_pairs={{0,1},{1,0},{2,3},{3,2},{4,5},{5,4},{6,7},{7,6},{8,9},{9,8},{10,11... | collective-permute-start | bytes 737288 | tf_op jit(solution)/shard_map/ppermute | solution.py:34
  111.1 8.9 %collective-permute-start.32 = (bf16[160,768]{1,0:T(8,128)(2,1)S(1)}, bf16[160,768]{1,0:T(8,128)(2,1)S(1)}, u32[]{:S(2)}, u32[]{:S(2)}) collective-permute-start(bf16[160,768]{1,0:T(8,128)(2,1)S(1)} %get-tuple-element.52), channel_id=1, source_target_pairs={{0,2},{1,3},{2,0},{3,1},{4,6},{5,7},{6,4},{7,5},{8,10},{9,11},{10,... | collective-permute-start | bytes 737288 | tf_op jit(solution)/shard_map/ppermute | solution.py:34
  112.0 13.3 %collective-permute-start.34 = (bf16[160,768]{1,0:T(8,128)(2,1)S(1)}, bf16[160,768]{1,0:T(8,128)(2,1)S(1)}, u32[]{:S(2)}, u32[]{:S(2)}) collective-permute-start(bf16[160,768]{1,0:T(8,128)(2,1)S(1)} %get-tuple-element.53), channel_id=1, source_target_pairs={{0,2},{1,3},{2,0},{3,1},{4,6},{5,7},{6,4},{7,5},{8,10},{9,11},{10,... | collective-permute-start | bytes 737288 | tf_op jit(solution)/shard_map/ppermute | solution.py:34
  113.2 8.4 %collective-permute-start.36 = (bf16[2,320,256]{2,1,0:T(8,128)(2,1)S(1)}, bf16[2,320,256]{2,1,0:T(8,128)(2,1)S(1)}, u32[]{:S(2)}, u32[]{:S(2)}) collective-permute-start(bf16[2,320,256]{2,1,0:T(8,128)(2,1)S(1)} %fusion.2), channel_id=1, source_target_pairs={{0,8},{8,0},{16,24},{24,16},{1,9},{9,1},{17,25},{25,17},{2,10},{10... | collective-permute-start | bytes 983048 | tf_op jit(solution)/shard_map/ppermute | solution.py:34
  117.7 17.3 %collective-permute-start.31 = (bf16[160,768]{1,0:T(8,128)(2,1)S(1)}, bf16[160,768]{1,0:T(8,128)(2,1)S(1)}, u32[]{:S(2)}, u32[]{:S(2)}) collective-permute-start(bf16[160,768]{1,0:T(8,128)(2,1)S(1)} %add_convert_fusion.4), channel_id=1, source_target_pairs={{0,2},{1,3},{2,0},{3,1},{4,6},{5,7},{6,4},{7,5},{8,10},{9,11},{10,... | collective-permute-start | bytes 737288 | tf_op jit(solution)/shard_map/ppermute | solution.py:34
  120.0 9.9 %copy-start.7 = (bf16[256,1280]{1,0:T(8,128)(2,1)S(1)}, bf16[256,1280]{1,0:T(8,128)(2,1)}, u32[]{:S(2)}) copy-start(bf16[256,1280]{1,0:T(8,128)(2,1)} %copy-done.6) | copy-start | bytes 1966084
  120.0 9.9 %copy-start.9 = (bf16[256,1280]{1,0:T(8,128)(2,1)S(1)}, bf16[256,1280]{1,0:T(8,128)(2,1)}, u32[]{:S(2)}) copy-start(bf16[256,1280]{1,0:T(8,128)(2,1)} %copy-done.8) | copy-start | bytes 1966084
  120.1 6.8 %collective-permute-start.33 = (bf16[160,768]{1,0:T(8,128)(2,1)S(1)}, bf16[160,768]{1,0:T(8,128)(2,1)S(1)}, u32[]{:S(2)}, u32[]{:S(2)}) collective-permute-start(bf16[160,768]{1,0:T(8,128)(2,1)S(1)} %add_convert_fusion.3), channel_id=1, source_target_pairs={{0,1},{1,0},{2,3},{3,2},{4,5},{5,4},{6,7},{7,6},{8,9},{9,8},{10,11... | collective-permute-start | bytes 737288 | tf_op jit(solution)/shard_map/ppermute | solution.py:34
  121.7 12.6 %collective-permute-start.37 = (bf16[320,256]{1,0:T(8,128)(2,1)S(1)}, bf16[320,256]{1,0:T(8,128)(2,1)S(1)}, u32[]{:S(2)}, u32[]{:S(2)}) collective-permute-start(bf16[320,256]{1,0:T(8,128)(2,1)S(1)} %fusion.3), channel_id=1, source_target_pairs={{0,16},{8,24},{16,0},{24,8},{1,17},{9,25},{17,1},{25,9},{2,18},{10... | collective-permute-start | bytes 491528 | tf_op jit(solution)/shard_map/ppermute | solution.py:34
  126.9 12.3 %collective-permute-start.35 = (bf16[160,768]{1,0:T(8,128)(2,1)S(1)}, bf16[160,768]{1,0:T(8,128)(2,1)S(1)}, u32[]{:S(2)}, u32[]{:S(2)}) collective-permute-start(bf16[160,768]{1,0:T(8,128)(2,1)S(1)} %add_convert_fusion.2), channel_id=1, source_target_pairs={{0,4},{1,5},{2,6},{3,7},{4,0},{5,1},{6,2},{7,3},{8,12},{9,13},{10,... | collective-permute-start | bytes 737288 | tf_op jit(solution)/shard_map/ppermute | solution.py:34

commit v3 on v2

--- a/solution.py
+++ b/solution.py
@@ -71,22 +71,27 @@
     return sent[:, :-LANES].astype(F32) * jnp.exp2(sent[:, -1:].astype(F32) - 14.0)
 
 
-def call(body, outs, args, flops, scratch=(), waits=0, vmem=48):
+def call(body, outs, args, flops, scratch=(), waits=(), vmem=48):
+    count = len(args)
     in_specs = [pl.BlockSpec(memory_space=pltpu.SMEM)]
-    in_specs += [pl.BlockSpec(memory_space=pltpu.VMEM)] * (len(args) - 1 - waits)
-    in_specs += [pl.BlockSpec(memory_space=pl.ANY)] * waits
+    in_specs += [pl.BlockSpec(memory_space=pltpu.VMEM)] * (count - 1)
+    in_specs += [pl.BlockSpec(memory_space=pl.ANY)] * len(waits)
     size = sum(a.size * a.dtype.itemsize for a in args) + sum(
         o.size * o.dtype.itemsize for o in outs
     )
+
+    def kernel(*refs):
+        body(*refs[:count], *refs[count + len(waits) :])
+
     return pl.pallas_call(
-        body,
+        kernel,
         out_shape=outs,
         in_specs=in_specs,
         out_specs=[pl.BlockSpec(memory_space=pltpu.VMEM)] * len(outs),
         scratch_shapes=list(scratch),
         compiler_params=pltpu.CompilerParams(vmem_limit_bytes=vmem * MIB),
         cost_estimate=pl.CostEstimate(flops=flops, bytes_accessed=size, transcendentals=0),
-    )(*args)
+    )(*args, *[corner(w) for w in waits])
 
 
 def sds(shape, dtype):
@@ -112,36 +117,21 @@
 
 
 def corner(x):
-    return lax.slice(x, (0, 0), (min(16, x.shape[0]), LANES))
-
-
-def gate_kernel(idx, *refs):
-    for i in range(idx.shape[0]):
-        refs[-1][i] = idx[i]
-
-
-def gate(idx, waits):
-    corners = [corner(w) for w in waits]
-    return pl.pallas_call(
-        gate_kernel,
-        out_shape=sds(idx.shape, idx.dtype),
-        in_specs=[pl.BlockSpec(memory_space=pltpu.SMEM)] + [pl.BlockSpec(memory_space=pltpu.VMEM)] * len(corners),
-        out_specs=pl.BlockSpec(memory_space=pltpu.SMEM),
-        compiler_params=pltpu.CompilerParams(vmem_limit_bytes=MIB),
-    )(idx, *corners)
+    piece = lax.slice(x, (0, 0), (min(16, x.shape[0]), LANES))
+    return piece.astype(F32) if x.dtype == F16 else piece
 
 
 def sum_core(mine, other, waits=()):
     return add(mine, swap(other, "tok", 1), F32, waits)
 
 
-def sum_chips(mine, fine=False, waits=()):
-    sent = to_half(mine) if fine else mine.astype(BF16)
+def sum_chips(mine, sent, waits=()):
     steps = range(2, lax.axis_size("tok"), 2)
     for k in steps:
+        last = k == steps[-1]
         got = swap(sent, "tok", k)
-        last = k == steps[-1]
-        mine = add(mine, from_half(got) if fine else got, BF16 if last else F32, waits if last else ())
+        got = from_half(got) if got.dtype == F16 else got
+        mine = add(mine, got, BF16 if last else F32, waits if last else ())
     return mine, swap(mine, "tok", 1)
 
 
@@ -184,7 +174,7 @@
     put_halves(idx[1], part, mine, other)
 
 
-def forward_kernel(idx, got_mine, got_other, w_in, w_out, _, slot_in, hidden, slope, mine, other, part):
+def forward_kernel(idx, got_mine, got_other, w_in, w_out, slot_in, hidden, slope, mine, other, part):
     join_halves(idx[1], got_mine, got_other, slot_in)
     value, rate = gelu_parts(dot(slot_in[...], w_in[...], 1, 0))
     slope[...] = rate
@@ -268,7 +258,6 @@
     token_norm = token_norm[None, :]
     tok_scale = float(rows * n_tok)
     slot_scale = float(slots * n_exp)
-    halves = [sds((half, width), F32), sds((half, width), BF16)]
     wide = [sds((half, width), F32)] * 2
     part = pltpu.VMEM((slots, width), F32)
 
@@ -278,33 +267,37 @@
     tok, logits, mine, other = call(
         functools.partial(slot_in_kernel, n_exp, tok_scale),
         [sds((width, rows), BF16), sds((slots, rows), F32), *wide],
-        [gate(idx, [grad_blocks[k] for k in (4,)]), *tok_blocks, slot_proj, slot_norm],
+        [idx, *tok_blocks, slot_proj, slot_norm],
         2 * macs,
         [part],
+        waits=[grad_blocks[k] for k in (4,)],
         vmem=50,
     )
     mine = sum_core(mine, other, [grad_blocks[k] for k in ()])
-    got_in = sum_chips(mine, True, [grad_blocks[k] for k in (5, 6)])
+    got_in = sum_chips(mine, mine, [grad_blocks[k] for k in (1,2,5,6)])
     grad, grad_mine, grad_other = call(
         functools.partial(slot_grad_kernel, n_exp, slot_scale),
-        [sds((width, rows), BF16), *halves],
+        [sds((width, rows), BF16), *wide],
         [idx, *grad_blocks, logits, token_norm],
         macs,
         [part],
+        waits=[got_in[0]],
         vmem=48,
     )
+    grad_mine = sum_core(grad_mine, grad_other)
+    grad_sent = to_half(grad_mine)
     slot_in, hidden, slope, mine, other = call(
         forward_kernel,
-        [sds((slots, width), BF16), sds((slots, hidden_units), BF16), sds((slots, hidden_units), F32), *halves],
-        [idx, *got_in, w_in, w_out, grad_other],
+        [sds((slots, width), BF16), sds((slots, hidden_units), BF16), sds((slots, hidden_units), F32), *wide],
+        [idx, *got_in, w_in, w_out],
         4 * slots * width * hidden_units,
         [part],
-        1,
+        waits=[grad_sent],
         vmem=24,
     )
     out_mine = sum_core(mine, other)
-    got_grad = sum_chips(sum_core(grad_mine, grad_other))
-    got_out = sum_chips(out_mine)
+    got_grad = sum_chips(grad_mine, grad_sent)
+    got_out = sum_chips(out_mine, to_half(out_mine))
     weighted, row_stat = call(
         functools.partial(comb_kernel, slot_scale),
         [sds((slots, rows), F32), sds((1, rows), F32)],
@@ -319,13 +312,14 @@
         k *= 2
     slot_grad, pre_grad, mine, other = call(
         backward_kernel,
-        [sds((slots, width), BF16), sds((slots, hidden_units), BF16), *halves],
+        [sds((slots, width), BF16), sds((slots, hidden_units), BF16), *wide],
         [idx, *got_grad, w_in, w_out, slope],
         4 * slots * width * hidden_units,
         [part],
         vmem=24,
     )
-    got_in_grad = sum_chips(sum_core(mine, other), waits=[row_stat])
+    mine = sum_core(mine, other)
+    got_in_grad = sum_chips(mine, to_half(mine), [row_stat])
     summed = {0, *tree_of(n_exp).values()}
     blocks = [sds((feat, rows), F32 if k in summed else BF16) for k in range(n_exp)]
     logit_grad, *blocks = call(

time: 141 us -> 147 us (1.043)
  waiting for transfers between devices: 58.7 us -> 67.3 us
  starting transfers between devices: 45.1 us -> 42.7 us
    ppermute x38, waiting for transfers between devices: 58.7 us -> 67.3 us  [swap(): return lax.ppermute(x, axis, [(i, i ^ k) for i in range(n)])]
    ppermute x38, starting transfers between devices: 45.1 us -> 42.7 us  [swap(): return lax.ppermute(x, axis, [(i, i ^ k) for i in range(n)])]
    pallas_call x7 -> x6, Pallas kernels: 15.5 us -> 14.4 us  [call(): pl.pallas_call(kernel, out_shape=outs, in_specs=in_specs, out_specs=[pl.B...]
  transfers between devices with their start and end apart: 38 -> 38, of which waited for: 21 -> 23; matrix products, arithmetic and copies ran while one was open for 4% -> 4% of each run, Pallas kernels for 13% -> 11%
where the time goes in v3:
time: 147 us
  waiting for transfers between devices  67.3 us (46%)
  starting transfers between devices  42.7 us (29%)
  Pallas kernels  24 us (16%)
  other arithmetic  6.43 us (4%)
  local copies, waits for them, and re-layouts  4.49 us (3%)
    ppermute x38, waiting for transfers between devices, swap(): return lax.ppermute(x, axis, [(i, i ^ k) for i in range(n)])  67.3 us
    ppermute x38, starting transfers between devices, swap(): return lax.ppermute(x, axis, [(i, i ^ k) for i in range(n)])  42.7 us
    pallas_call x6, Pallas kernels, call(): pl.pallas_call(kernel, out_shape=outs, in_specs=in_specs, out_specs=[pl.B...  14.4 us
    pallas_call x2, Pallas kernels, weight_grad(): pl.pallas_call(weight_grad_kernel, out_shape=sds((rows, columns), F32), g...  8.72 us
    unnamed x30, local copies, waits for them, and re-layouts  3.36 us
  transfers between devices with their start and end apart: 38, of which 23 were waited for; matrix products, arithmetic and copies ran while one was open for 4% of the time, Pallas kernels for 11%

profile of v3, /device:TPU:0, one launch (start us, length us, event | category | flops | bytes accessed | tf_op | source)
XLA Modules:
  0.0 146.7 jit_solution(17956452193606927432)
XLA Ops:
  0.6 1.1 convert_bitcast_fusion.refs_1_
  1.7 4.1 %collective-permute-start.10 = (bf16[160,768]{1,0:T(8,128)(2,1)S(1)}, bf16[160,768]{1,0:T(8,128)(2,1)S(1)}, u32[]{:S(2)}, u32[]{:S(2)}) collective-permute-start(bf16[160,768]{1,0:T(8,128)(2,1)S(1)} %convert_bitcast_fusion.refs_1_), channel_id=1, source_target_pairs={{0,4},{1,5},{2,6},{3,7},{4,0},{5,1},{6,2},{7,3},{8,12},{9,13},{10,... | collective-permute-start | bytes 737288 | tf_op jit(solution)/shard_map/ppermute | solution.py:34
  5.8 1.6 %collective-permute-start.8 = (bf16[160,768]{1,0:T(8,128)(2,1)S(1)}, bf16[160,768]{1,0:T(8,128)(2,1)S(1)}, u32[]{:S(2)}, u32[]{:S(2)}) collective-permute-start(bf16[160,768]{1,0:T(8,128)(2,1)S(1)} %convert_bitcast_fusion.refs_1_), channel_id=1, source_target_pairs={{0,2},{1,3},{2,0},{3,1},{4,6},{5,7},{6,4},{7,5},{8,10},{9,11},{10,... | collective-permute-start | bytes 737288 | tf_op jit(solution)/shard_map/ppermute | solution.py:34
  7.4 9.7 %collective-permute-done.10.refs_5_ = bf16[160,768]{1,0:T(8,128)(2,1)S(1)} collective-permute-done((bf16[160,768]{1,0:T(8,128)(2,1)S(1)}, bf16[160,768]{1,0:T(8,128)(2,1)S(1)}, u32[]{:S(2)}, u32[]{:S(2)}) %collective-permute-start.10) | collective-permute-done | bytes 245792 | tf_op jit(solution)/shard_map/ppermute | solution.py:34
  17.1 1.6 %collective-permute-start.11 = (bf16[160,768]{1,0:T(8,128)(2,1)S(1)}, bf16[160,768]{1,0:T(8,128)(2,1)S(1)}, u32[]{:S(2)}, u32[]{:S(2)}) collective-permute-start(bf16[160,768]{1,0:T(8,128)(2,1)S(1)} %collective-permute-done.10.refs_5_), channel_id=1, source_target_pairs={{0,1},{1,0},{2,3},{3,2},{4,5},{5,4},{6,7},{7,6},{8,9},{9,8},{10,11... | collective-permute-start | bytes 737288 | tf_op jit(solution)/shard_map/ppermute | solution.py:34
  19.1 1.1 convert_bitcast_fusion.1.refs_1_
  20.3 4.0 %collective-permute-start.12 = (bf16[160,768]{1,0:T(8,128)(2,1)S(1)}, bf16[160,768]{1,0:T(8,128)(2,1)S(1)}, u32[]{:S(2)}, u32[]{:S(2)}) collective-permute-start(bf16[160,768]{1,0:T(8,128)(2,1)S(1)} %collective-permute-done.10.refs_5_), channel_id=1, source_target_pairs={{0,2},{1,3},{2,0},{3,1},{4,6},{5,7},{6,4},{7,5},{8,10},{9,11},{10,... | collective-permute-start | bytes 737288 | tf_op jit(solution)/shard_map/ppermute | solution.py:34
  24.3 1.5 %collective-permute-start.9 = (bf16[160,768]{1,0:T(8,128)(2,1)S(1)}, bf16[160,768]{1,0:T(8,128)(2,1)S(1)}, u32[]{:S(2)}, u32[]{:S(2)}) collective-permute-start(bf16[160,768]{1,0:T(8,128)(2,1)S(1)} %collective-permute-done.8.refs_3_), channel_id=1, source_target_pairs={{0,1},{1,0},{2,3},{3,2},{4,5},{5,4},{6,7},{7,6},{8,9},{9,8},{10,11... | collective-permute-start | bytes 737288 | tf_op jit(solution)/shard_map/ppermute | solution.py:34
  26.0 0.5 collective-permute-start.13
  26.6 0.8 copy.15.refs_10_.refs_5_
  27.4 5.6 %collective-permute-done.3.refs_5_ = bf16[160,768]{1,0:T(8,128)(2,1)S(1)} collective-permute-done((bf16[160,768]{1,0:T(8,128)(2,1)S(1)}, bf16[160,768]{1,0:T(8,128)(2,1)S(1)}, u32[]{:S(2)}, u32[]{:S(2)}) %collective-permute-start.3) | collective-permute-done | bytes 245792 | tf_op jit(solution)/shard_map/ppermute | solution.py:34
  33.1 1.6 %collective-permute-done.12.refs_7_ = bf16[160,768]{1,0:T(8,128)(2,1)S(1)} collective-permute-done((bf16[160,768]{1,0:T(8,128)(2,1)S(1)}, bf16[160,768]{1,0:T(8,128)(2,1)S(1)}, u32[]{:S(2)}, u32[]{:S(2)}) %collective-permute-start.12) | collective-permute-done | bytes 245792 | tf_op jit(solution)/shard_map/ppermute | solution.py:34
  34.7 3.7 %collective-permute-done.13.refs_8_ = bf16[160,768]{1,0:T(8,128)(2,1)S(1)} collective-permute-done((bf16[160,768]{1,0:T(8,128)(2,1)S(1)}, bf16[160,768]{1,0:T(8,128)(2,1)S(1)}, u32[]{:S(2)}, u32[]{:S(2)}) %collective-permute-start.13) | collective-permute-done | bytes 245792 | tf_op jit(solution)/shard_map/ppermute | solution.py:34
  38.4 1.1 copy-done.12
  39.5 2.3 %shard_map.102 = (bf16[1280,768]{1,0:T(8,128)(2,1)}, f32[256,768]{1,0:T(8,128)}, f32[128,1280]{1,0:T(8,128)S(1)}, f32[128,1280]{1,0:T(8,128)S(1)}) custom-call(s32[2]{0:T(128)S(1)} %pad_add_fusion.refs_0_, bf16[160,768]{1,0:T(8,128)(2,1)S(1)} %convert_bitcast_fusion.refs_1_, bf16[160,768]{1,0:T(8,128)(2,1)S(1)} %collective-permute-done.7.refs_2_, ...), custom_call_target="tpu_custom_call" | custom-call | flops 1006632960 | bytes 6685704 | tf_op jit(solution)/shard_map/pallas_call | solution.py:86
  41.8 2.1 %collective-permute-done.14 = f32[128,1280]{1,0:T(8,128)S(1)} collective-permute-done((f32[128,1280]{1,0:T(8,128)S(1)}, f32[128,1280]{1,0:T(8,128)S(1)}, u32[]{:S(2)}, u32[]{:S(2)}) %collective-permute-start.14) | collective-permute-done | bytes 655392 | tf_op jit(solution)/shard_map/ppermute | solution.py:34
  44.0 1.3 collective-permute-start.15
  45.3 1.5 %collective-permute-start.4 = (bf16[160,768]{1,0:T(8,128)(2,1)S(1)}, bf16[160,768]{1,0:T(8,128)(2,1)S(1)}, u32[]{:S(2)}, u32[]{:S(2)}) collective-permute-start(bf16[160,768]{1,0:T(8,128)(2,1)S(1)} %collective-permute-done.3.refs_5_), channel_id=1, source_target_pairs={{0,1},{1,0},{2,3},{3,2},{4,5},{5,4},{6,7},{7,6},{8,9},{9,8},{10,11... | collective-permute-start | bytes 737288 | tf_op jit(solution)/shard_map/ppermute | solution.py:34
  46.9 0.5 collective-permute-start
  47.4 2.0 %collective-permute-start.5 = (bf16[160,768]{1,0:T(8,128)(2,1)S(1)}, bf16[160,768]{1,0:T(8,128)(2,1)S(1)}, u32[]{:S(2)}, u32[]{:S(2)}) collective-permute-start(bf16[160,768]{1,0:T(8,128)(2,1)S(1)} %collective-permute-done.3.refs_5_), channel_id=1, source_target_pairs={{0,2},{1,3},{2,0},{3,1},{4,6},{5,7},{6,4},{7,5},{8,10},{9,11},{10,... | collective-permute-start | bytes 737288 | tf_op jit(solution)/shard_map/ppermute | solution.py:34
  49.4 4.8 %collective-permute-done.1.refs_3_ = bf16[160,768]{1,0:T(8,128)(2,1)S(1)} collective-permute-done((bf16[160,768]{1,0:T(8,128)(2,1)S(1)}, bf16[160,768]{1,0:T(8,128)(2,1)S(1)}, u32[]{:S(2)}, u32[]{:S(2)}) %collective-permute-start.1) | collective-permute-done | bytes 245792 | tf_op jit(solution)/shard_map/ppermute | solution.py:34
  54.2 1.5 %collective-permute-start.2 = (bf16[160,768]{1,0:T(8,128)(2,1)S(1)}, bf16[160,768]{1,0:T(8,128)(2,1)S(1)}, u32[]{:S(2)}, u32[]{:S(2)}) collective-permute-start(bf16[160,768]{1,0:T(8,128)(2,1)S(1)} %collective-permute-done.1.refs_3_), channel_id=1, source_target_pairs={{0,1},{1,0},{2,3},{3,2},{4,5},{5,4},{6,7},{7,6},{8,9},{9,8},{10,11... | collective-permute-start | bytes 737288 | tf_op jit(solution)/shard_map/ppermute | solution.py:34
  55.7 0.5 collective-permute-start.6
  56.3 3.2 %collective-permute-done.refs_2_ = bf16[160,768]{1,0:T(8,128)(2,1)S(1)} collective-permute-done((bf16[160,768]{1,0:T(8,128)(2,1)S(1)}, bf16[160,768]{1,0:T(8,128)(2,1)S(1)}, u32[]{:S(2)}, u32[]{:S(2)}) %collective-permute-start) | collective-permute-done | bytes 245792 | tf_op jit(solution)/shard_map/ppermute | solution.py:34
  59.5 1.4 collective-permute-done.15.got
  61.0 2.6 %collective-permute-done.2.refs_4_ = bf16[160,768]{1,0:T(8,128)(2,1)S(1)} collective-permute-done((bf16[160,768]{1,0:T(8,128)(2,1)S(1)}, bf16[160,768]{1,0:T(8,128)(2,1)S(1)}, u32[]{:S(2)}, u32[]{:S(2)}) %collective-permute-start.2) | collective-permute-done | bytes 245792 | tf_op jit(solution)/shard_map/ppermute | solution.py:34
  63.6 1.5 %shard_map.104 = (bf16[1280,768]{1,0:T(8,128)(2,1)S(1)}, f32[128,1280]{1,0:T(8,128)S(1)}, f32[128,1280]{1,0:T(8,128)S(1)}) custom-call(s32[2]{0:T(128)S(1)} %pad_add_fusion.refs_0_, bf16[160,768]{1,0:T(8,128)(2,1)S(1)} %convert_bitcast_fusion.1.refs_1_, bf16[160,768]{1,0:T(8,128)(2,1)S(1)} %collective-permute-done.refs_2_, ...), custom_call_target="tpu_custom_call" | custom-call | flops 503316480 | bytes 6032392 | tf_op jit(solution)/shard_map/pallas_call | solution.py:86
  65.7 1.6 %collective-permute-done.16 = f32[128,1280]{1,0:T(8,128)S(1)} collective-permute-done((f32[128,1280]{1,0:T(8,128)S(1)}, f32[128,1280]{1,0:T(8,128)S(1)}, u32[]{:S(2)}, u32[]{:S(2)}) %collective-permute-start.16) | collective-permute-done | bytes 655392 | tf_op jit(solution)/shard_map/ppermute | solution.py:34
  67.8 0.8 collective-permute-start.17
  68.6 3.2 %shard_map.105 = (bf16[256,1280]{1,0:T(8,128)(2,1)S(1)}, bf16[256,1280]{1,0:T(8,128)(2,1)S(1)}, f32[256,1280]{1,0:T(8,128)S(1)}, f32[128,1280]{1,0:T(8,128)S(1)}, f32[128,1280]{1,0:T(8,128)S(1)}) custom-call(s32[2]{0:T(128)S(1)} %pad_add_fusion.refs_0_, bf16[128,1280]{1,0:T(8,128)(2,1)S(1)} %shard_map.103.refs_1_, ...), custom_call_target="tpu_custom_call" | custom-call | flops 1677721600 | bytes 11141128 | tf_op jit(solution)/shard_map/pallas_call | solution.py:86
  71.9 6.3 %collective-permute-done.17 = f16[128,1408]{1,0:T(8,128)(2,1)S(1)} collective-permute-done((f16[128,1408]{1,0:T(8,128)(2,1)S(1)}, f16[128,1408]{1,0:T(8,128)(2,1)S(1)}, u32[]{:S(2)}, u32[]{:S(2)}) %collective-permute-start.17) | collective-permute-done | bytes 360480 | tf_op jit(solution)/shard_map/ppermute | solution.py:34
  79.2 0.8 collective-permute-start.23
  80.3 2.7 %shard_map.106 = (bf16[256,1280]{1,0:T(8,128)(2,1)S(1)}, bf16[256,1280]{1,0:T(8,128)(2,1)S(1)}, f32[128,1280]{1,0:T(8,128)S(1)}, f32[128,1280]{1,0:T(8,128)S(1)}) custom-call(s32[2]{0:T(128)S(1)} %pad_add_fusion.refs_0_, bf16[128,1280]{1,0:T(8,128)(2,1)S(1)} %add_convert_fusion.1.refs_1_, bf16[128,1280]{1,0:T(8,128)(2,1)S(1)} %collective-permute-done.18.refs_2_, ...), custom_call_target="tpu_custom_call" | custom-call | flops 1677721600 | bytes 11141128 | tf_op jit(solution)/shard_map/pallas_call | solution.py:86
  83.2 6.9 %collective-permute-done.23 = f16[128,1408]{1,0:T(8,128)(2,1)S(1)} collective-permute-done((f16[128,1408]{1,0:T(8,128)(2,1)S(1)}, f16[128,1408]{1,0:T(8,128)(2,1)S(1)}, u32[]{:S(2)}, u32[]{:S(2)}) %collective-permute-start.23) | collective-permute-done | bytes 360480 | tf_op jit(solution)/shard_map/ppermute | solution.py:34
  91.1 0.8 collective-permute-start.21
  92.2 1.3 shard_map.107
  93.5 1.6 %collective-permute-start.25 = (f32[1,768]{1,0:T(1,128)S(1)}, f32[1,768]{1,0:T(1,128)S(1)}, u32[]{:S(2)}, u32[]{:S(2)}) collective-permute-start(f32[1,768]{1,0:T(1,128)S(1)} %get-tuple-element.42), channel_id=1, source_target_pairs={{0,1},{1,0},{2,3},{3,2},{4,5},{5,4},{6,7},{7,6},{8,9},{9,8},{10,11... | collective-permute-start | bytes 9224 | tf_op jit(solution)/shard_map/ppermute | solution.py:34
  95.1 2.1 %collective-permute-done.25 = f32[1,768]{1,0:T(1,128)S(1)} collective-permute-done((f32[1,768]{1,0:T(1,128)S(1)}, f32[1,768]{1,0:T(1,128)S(1)}, u32[]{:S(2)}, u32[]{:S(2)}) %collective-permute-start.25) | collective-permute-done | bytes 3104 | tf_op jit(solution)/shard_map/ppermute | solution.py:34
  97.1 1.7 %collective-permute-start.26 = (f32[1,768]{1,0:T(1,128)S(1)}, f32[1,768]{1,0:T(1,128)S(1)}, u32[]{:S(2)}, u32[]{:S(2)}) collective-permute-start(f32[1,768]{1,0:T(1,128)S(1)} %add.85), channel_id=1, source_target_pairs={{0,2},{1,3},{2,0},{3,1},{4,6},{5,7},{6,4},{7,5},{8,10},{9,11},{10,... | collective-permute-start | bytes 9224 | tf_op jit(solution)/shard_map/ppermute | solution.py:34
  98.9 1.9 %collective-permute-done.26 = f32[1,768]{1,0:T(1,128)S(1)} collective-permute-done((f32[1,768]{1,0:T(1,128)S(1)}, f32[1,768]{1,0:T(1,128)S(1)}, u32[]{:S(2)}, u32[]{:S(2)}) %collective-permute-start.26) | collective-permute-done | bytes 3104 | tf_op jit(solution)/shard_map/ppermute | solution.py:34
  100.7 3.8 %collective-permute-start.27 = (f32[1,768]{1,0:T(1,128)S(1)}, f32[1,768]{1,0:T(1,128)S(1)}, u32[]{:S(2)}, u32[]{:S(2)}) collective-permute-start(f32[1,768]{1,0:T(1,128)S(1)} %add.86), channel_id=1, source_target_pairs={{0,4},{1,5},{2,6},{3,7},{4,0},{5,1},{6,2},{7,3},{8,12},{9,13},{10,... | collective-permute-start | bytes 9224 | tf_op jit(solution)/shard_map/ppermute | solution.py:34
  104.5 1.6 %collective-permute-done.27 = f32[1,768]{1,0:T(1,128)S(1)} collective-permute-done((f32[1,768]{1,0:T(1,128)S(1)}, f32[1,768]{1,0:T(1,128)S(1)}, u32[]{:S(2)}, u32[]{:S(2)}) %collective-permute-start.27) | collective-permute-done | bytes 3104 | tf_op jit(solution)/shard_map/ppermute | solution.py:34
  106.4 0.8 shard_map.108.refs_1_
  107.2 2.0 %collective-permute-done.28.refs_2_ = bf16[128,1280]{1,0:T(8,128)(2,1)} collective-permute-done((bf16[128,1280]{1,0:T(8,128)(2,1)}, bf16[128,1280]{1,0:T(8,128)(2,1)}, u32[]{:S(2)}, u32[]{:S(2)}) %collective-permute-start.28) | collective-permute-done | bytes 327712 | tf_op jit(solution)/shard_map/ppermute | solution.py:34
  109.2 1.1 copy-done.5
  110.3 1.1 copy-done.13
  111.4 3.4 %shard_map.109 = (bf16[256,768]{1,0:T(8,128)(2,1)S(1)}, f32[160,768]{1,0:T(8,128)S(1)}, bf16[160,768]{1,0:T(8,128)(2,1)S(1)}, f32[160,768]{1,0:T(8,128)S(1)}, bf...) custom-call(s32[2]{0:T(128)S(1)} %pad_add_fusion.refs_0_, ...), custom_call_target="tpu_custom_call" | custom-call | flops 1509949440 | bytes 8854536 | tf_op jit(solution)/shard_map/pallas_call | solution.py:86
  114.8 1.6 %collective-permute-start.30 = (bf16[160,768]{1,0:T(8,128)(2,1)S(1)}, bf16[160,768]{1,0:T(8,128)(2,1)S(1)}, u32[]{:S(2)}, u32[]{:S(2)}) collective-permute-start(bf16[160,768]{1,0:T(8,128)(2,1)S(1)} %get-tuple-element.49), channel_id=1, source_target_pairs={{0,1},{1,0},{2,3},{3,2},{4,5},{5,4},{6,7},{7,6},{8,9},{9,8},{10,11... | collective-permute-start | bytes 737288 | tf_op jit(solution)/shard_map/ppermute | solution.py:34
  116.4 0.7 fusion.5
  117.1 0.6 collective-permute-start.29
  117.7 0.9 collective-permute-start.32
  118.6 1.1 collective-permute-start.34
  119.8 4.4 %shard_map.110 = f32[1280,1280]{1,0:T(8,128)} custom-call(bf16[256,1280]{1,0:T(8,128)(2,1)S(1)} %get-tuple-element.45.refs_9_.left, bf16[256,1280]{1,0:T(8,128)(2,1)S(1)} %copy-done.11, bf16[256,768]{1,0:T(8,128)(2,1)S(1)} %get-tuple-element.54._), custom_call_target="tpu_custom_call" | custom-call | flops 838860800 | bytes 6553600 | tf_op jit(solution)/shard_map/pallas_call | solution.py:228
  124.3 1.0 collective-permute-start.31
  125.2 1.3 collective-permute-done.32
  126.6 1.6 %collective-permute-start.33 = (bf16[160,768]{1,0:T(8,128)(2,1)S(1)}, bf16[160,768]{1,0:T(8,128)(2,1)S(1)}, u32[]{:S(2)}, u32[]{:S(2)}) collective-permute-start(bf16[160,768]{1,0:T(8,128)(2,1)S(1)} %add_convert_fusion.3), channel_id=1, source_target_pairs={{0,1},{1,0},{2,3},{3,2},{4,5},{5,4},{6,7},{7,6},{8,9},{9,8},{10,11... | collective-permute-start | bytes 737288 | tf_op jit(solution)/shard_map/ppermute | solution.py:34
  128.3 1.1 collective-permute-start.37
  129.4 2.4 %collective-permute-done.34 = bf16[160,768]{1,0:T(8,128)(2,1)S(1)} collective-permute-done((bf16[160,768]{1,0:T(8,128)(2,1)S(1)}, bf16[160,768]{1,0:T(8,128)(2,1)S(1)}, u32[]{:S(2)}, u32[]{:S(2)}) %collective-permute-start.34) | collective-permute-done | bytes 245792 | tf_op jit(solution)/shard_map/ppermute | solution.py:34
  131.8 1.6 %collective-permute-done.33 = bf16[160,768]{1,0:T(8,128)(2,1)S(1)} collective-permute-done((bf16[160,768]{1,0:T(8,128)(2,1)S(1)}, bf16[160,768]{1,0:T(8,128)(2,1)S(1)}, u32[]{:S(2)}, u32[]{:S(2)}) %collective-permute-start.33) | collective-permute-done | bytes 245792 | tf_op jit(solution)/shard_map/ppermute | solution.py:34
  133.5 3.0 %collective-permute-start.35 = (bf16[160,768]{1,0:T(8,128)(2,1)S(1)}, bf16[160,768]{1,0:T(8,128)(2,1)S(1)}, u32[]{:S(2)}, u32[]{:S(2)}) collective-permute-start(bf16[160,768]{1,0:T(8,128)(2,1)S(1)} %add_convert_fusion.2), channel_id=1, source_target_pairs={{0,4},{1,5},{2,6},{3,7},{4,0},{5,1},{6,2},{7,3},{8,12},{9,13},{10,... | collective-permute-start | bytes 737288 | tf_op jit(solution)/shard_map/ppermute | solution.py:34
  136.5 4.4 %shard_map.111 = f32[1280,1280]{1,0:T(8,128)} custom-call(bf16[256,1280]{1,0:T(8,128)(2,1)S(1)} %copy-done.7, bf16[256,1280]{1,0:T(8,128)(2,1)S(1)} %copy-done.9, bf16[256,768]{1,0:T(8,128)(2,1)S(1)} %get-tuple-element.54._), custom_call_target="tpu_custom_call" | custom-call | flops 838860800 | bytes 6553600 | tf_op jit(solution)/shard_map/pallas_call | solution.py:228
  140.8 0.8 bitcast_add_fusion.1
  141.6 4.2 %collective-permute-done.35 = bf16[160,768]{1,0:T(8,128)(2,1)S(1)} collective-permute-done((bf16[160,768]{1,0:T(8,128)(2,1)S(1)}, bf16[160,768]{1,0:T(8,128)(2,1)S(1)}, u32[]{:S(2)}, u32[]{:S(2)}) %collective-permute-start.35) | collective-permute-done | bytes 245792 | tf_op jit(solution)/shard_map/ppermute | solution.py:34
  145.8 0.9 add_bitcast_fusion
  (99 shorter events, 5.5 us)
Async XLA Ops:
  1.7 15.4 %collective-permute-start.10 = (bf16[160,768]{1,0:T(8,128)(2,1)S(1)}, bf16[160,768]{1,0:T(8,128)(2,1)S(1)}, u32[]{:S(2)}, u32[]{:S(2)}) collective-permute-start(bf16[160,768]{1,0:T(8,128)(2,1)S(1)} %convert_bitcast_fusion.refs_1_), channel_id=1, source_target_pairs={{0,4},{1,5},{2,6},{3,7},{4,0},{5,1},{6,2},{7,3},{8,12},{9,13},{10,... | collective-permute-start | bytes 737288 | tf_op jit(solution)/shard_map/ppermute | solution.py:34
  5.8 18.5 %collective-permute-start.8 = (bf16[160,768]{1,0:T(8,128)(2,1)S(1)}, bf16[160,768]{1,0:T(8,128)(2,1)S(1)}, u32[]{:S(2)}, u32[]{:S(2)}) collective-permute-start(bf16[160,768]{1,0:T(8,128)(2,1)S(1)} %convert_bitcast_fusion.refs_1_), channel_id=1, source_target_pairs={{0,2},{1,3},{2,0},{3,1},{4,6},{5,7},{6,4},{7,5},{8,10},{9,11},{10,... | collective-permute-start | bytes 737288 | tf_op jit(solution)/shard_map/ppermute | solution.py:34
  17.1 8.9 %collective-permute-start.11 = (bf16[160,768]{1,0:T(8,128)(2,1)S(1)}, bf16[160,768]{1,0:T(8,128)(2,1)S(1)}, u32[]{:S(2)}, u32[]{:S(2)}) collective-permute-start(bf16[160,768]{1,0:T(8,128)(2,1)S(1)} %collective-permute-done.10.refs_5_), channel_id=1, source_target_pairs={{0,1},{1,0},{2,3},{3,2},{4,5},{5,4},{6,7},{7,6},{8,9},{9,8},{10,11... | collective-permute-start | bytes 737288 | tf_op jit(solution)/shard_map/ppermute | solution.py:34
  18.7 14.4 %collective-permute-start.7 = (bf16[160,768]{1,0:T(8,128)(2,1)S(1)}, bf16[160,768]{1,0:T(8,128)(2,1)S(1)}, u32[]{:S(2)}, u32[]{:S(2)}) collective-permute-start(bf16[160,768]{1,0:T(8,128)(2,1)S(1)} %convert_bitcast_fusion.refs_1_), channel_id=1, source_target_pairs={{0,1},{1,0},{2,3},{3,2},{4,5},{5,4},{6,7},{7,6},{8,9},{9,8},{10,11... | collective-permute-start | bytes 737288 | tf_op jit(solution)/shard_map/ppermute | solution.py:34
  20.2 12.9 %collective-permute-start.3 = (bf16[160,768]{1,0:T(8,128)(2,1)S(1)}, bf16[160,768]{1,0:T(8,128)(2,1)S(1)}, u32[]{:S(2)}, u32[]{:S(2)}) collective-permute-start(bf16[160,768]{1,0:T(8,128)(2,1)S(1)} %convert_bitcast_fusion.1.refs_1_), channel_id=1, source_target_pairs={{0,4},{1,5},{2,6},{3,7},{4,0},{5,1},{6,2},{7,3},{8,12},{9,13},{10,... | collective-permute-start | bytes 737288 | tf_op jit(solution)/shard_map/ppermute | solution.py:34
  20.3 14.4 %collective-permute-start.12 = (bf16[160,768]{1,0:T(8,128)(2,1)S(1)}, bf16[160,768]{1,0:T(8,128)(2,1)S(1)}, u32[]{:S(2)}, u32[]{:S(2)}) collective-permute-start(bf16[160,768]{1,0:T(8,128)(2,1)S(1)} %collective-permute-done.10.refs_5_), channel_id=1, source_target_pairs={{0,2},{1,3},{2,0},{3,1},{4,6},{5,7},{6,4},{7,5},{8,10},{9,11},{10,... | collective-permute-start | bytes 737288 | tf_op jit(solution)/shard_map/ppermute | solution.py:34
  24.3 10.5 %collective-permute-start.9 = (bf16[160,768]{1,0:T(8,128)(2,1)S(1)}, bf16[160,768]{1,0:T(8,128)(2,1)S(1)}, u32[]{:S(2)}, u32[]{:S(2)}) collective-permute-start(bf16[160,768]{1,0:T(8,128)(2,1)S(1)} %collective-permute-done.8.refs_3_), channel_id=1, source_target_pairs={{0,1},{1,0},{2,3},{3,2},{4,5},{5,4},{6,7},{7,6},{8,9},{9,8},{10,11... | collective-permute-start | bytes 737288 | tf_op jit(solution)/shard_map/ppermute | solution.py:34
  26.0 12.4 %collective-permute-start.13 = (bf16[160,768]{1,0:T(8,128)(2,1)S(1)}, bf16[160,768]{1,0:T(8,128)(2,1)S(1)}, u32[]{:S(2)}, u32[]{:S(2)}) collective-permute-start(bf16[160,768]{1,0:T(8,128)(2,1)S(1)} %collective-permute-done.11.refs_6_), channel_id=1, source_target_pairs={{0,2},{1,3},{2,0},{3,1},{4,6},{5,7},{6,4},{7,5},{8,10},{9,11},{10,... | collective-permute-start | bytes 737288 | tf_op jit(solution)/shard_map/ppermute | solution.py:34
  33.1 23.2 %copy-start.14 = (f32[768]{0:T(1024)S(1)}, f32[768]{0:T(1024)}, u32[]{:S(2)}) copy-start(f32[768]{0:T(1024)} %param.13) | copy-start | bytes 9220
  38.4 1.1 copy-start.12
  41.8 21.8 %copy-start.3 = (f32[256,768]{1,0:T(8,128)S(1)}, f32[256,768]{1,0:T(8,128)}, u32[]{:S(2)}) copy-start(f32[256,768]{1,0:T(8,128)} %get-tuple-element.31.refs_9_.refs_4_) | copy-start | bytes 2359300
  41.8 2.1 %collective-permute-start.14 = (f32[128,1280]{1,0:T(8,128)S(1)}, f32[128,1280]{1,0:T(8,128)S(1)}, u32[]{:S(2)}, u32[]{:S(2)}) collective-permute-start(f32[128,1280]{1,0:T(8,128)S(1)} %get-tuple-element.33), channel_id=1, source_target_pairs={{0,8},{8,0},{16,24},{24,16},{1,9},{9,1},{17,25},{25,17},{2,10},{10... | collective-permute-start | bytes 1966088 | tf_op jit(solution)/shard_map/ppermute | solution.py:34
  44.0 16.8 %collective-permute-start.15 = (f32[128,1280]{1,0:T(8,128)S(1)}, f32[128,1280]{1,0:T(8,128)S(1)}, u32[]{:S(2)}, u32[]{:S(2)}) collective-permute-start(f32[128,1280]{1,0:T(8,128)S(1)} %add.79.ours), channel_id=1, source_target_pairs={{0,16},{8,24},{16,0},{24,8},{1,17},{9,25},{17,1},{25,9},{2,18},{10... | collective-permute-start | bytes 1966088 | tf_op jit(solution)/shard_map/ppermute | solution.py:34
  45.3 8.8 %collective-permute-start.1 = (bf16[160,768]{1,0:T(8,128)(2,1)S(1)}, bf16[160,768]{1,0:T(8,128)(2,1)S(1)}, u32[]{:S(2)}, u32[]{:S(2)}) collective-permute-start(bf16[160,768]{1,0:T(8,128)(2,1)S(1)} %convert_bitcast_fusion.1.refs_1_), channel_id=1, source_target_pairs={{0,2},{1,3},{2,0},{3,1},{4,6},{5,7},{6,4},{7,5},{8,10},{9,11},{10,... | collective-permute-start | bytes 737288 | tf_op jit(solution)/shard_map/ppermute | solution.py:34
  45.3 10.4 %collective-permute-start.4 = (bf16[160,768]{1,0:T(8,128)(2,1)S(1)}, bf16[160,768]{1,0:T(8,128)(2,1)S(1)}, u32[]{:S(2)}, u32[]{:S(2)}) collective-permute-start(bf16[160,768]{1,0:T(8,128)(2,1)S(1)} %collective-permute-done.3.refs_5_), channel_id=1, source_target_pairs={{0,1},{1,0},{2,3},{3,2},{4,5},{5,4},{6,7},{7,6},{8,9},{9,8},{10,11... | collective-permute-start | bytes 737288 | tf_op jit(solution)/shard_map/ppermute | solution.py:34
  46.9 12.6 %collective-permute-start = (bf16[160,768]{1,0:T(8,128)(2,1)S(1)}, bf16[160,768]{1,0:T(8,128)(2,1)S(1)}, u32[]{:S(2)}, u32[]{:S(2)}) collective-permute-start(bf16[160,768]{1,0:T(8,128)(2,1)S(1)} %convert_bitcast_fusion.1.refs_1_), channel_id=1, source_target_pairs={{0,1},{1,0},{2,3},{3,2},{4,5},{5,4},{6,7},{7,6},{8,9},{9,8},{10,11... | collective-permute-start | bytes 737288 | tf_op jit(solution)/shard_map/ppermute | solution.py:34
  47.4 12.1 %collective-permute-start.5 = (bf16[160,768]{1,0:T(8,128)(2,1)S(1)}, bf16[160,768]{1,0:T(8,128)(2,1)S(1)}, u32[]{:S(2)}, u32[]{:S(2)}) collective-permute-start(bf16[160,768]{1,0:T(8,128)(2,1)S(1)} %collective-permute-done.3.refs_5_), channel_id=1, source_target_pairs={{0,2},{1,3},{2,0},{3,1},{4,6},{5,7},{6,4},{7,5},{8,10},{9,11},{10,... | collective-permute-start | bytes 737288 | tf_op jit(solution)/shard_map/ppermute | solution.py:34
  54.2 9.4 %collective-permute-start.2 = (bf16[160,768]{1,0:T(8,128)(2,1)S(1)}, bf16[160,768]{1,0:T(8,128)(2,1)S(1)}, u32[]{:S(2)}, u32[]{:S(2)}) collective-permute-start(bf16[160,768]{1,0:T(8,128)(2,1)S(1)} %collective-permute-done.1.refs_3_), channel_id=1, source_target_pairs={{0,1},{1,0},{2,3},{3,2},{4,5},{5,4},{6,7},{7,6},{8,9},{9,8},{10,11... | collective-permute-start | bytes 737288 | tf_op jit(solution)/shard_map/ppermute | solution.py:34
  55.7 7.9 %collective-permute-start.6 = (bf16[160,768]{1,0:T(8,128)(2,1)S(1)}, bf16[160,768]{1,0:T(8,128)(2,1)S(1)}, u32[]{:S(2)}, u32[]{:S(2)}) collective-permute-start(bf16[160,768]{1,0:T(8,128)(2,1)S(1)} %collective-permute-done.4.refs_6_), channel_id=1, source_target_pairs={{0,2},{1,3},{2,0},{3,1},{4,6},{5,7},{6,4},{7,5},{8,10},{9,11},{10,... | collective-permute-start | bytes 737288 | tf_op jit(solution)/shard_map/ppermute | solution.py:34
  60.9 7.8 %copy-start.1 = (bf16[1,1280,1280]{2,1,0:T(8,128)(2,1)S(1)}, bf16[1,1280,1280]{2,1,0:T(8,128)(2,1)}, u32[]{:S(2)}) copy-start(bf16[1,1280,1280]{2,1,0:T(8,128)(2,1)} %param.11) | copy-start | bytes 9830404
  65.1 3.5 %copy-start = (bf16[1,1280,1280]{2,1,0:T(8,128)(2,1)S(1)}, bf16[1,1280,1280]{2,1,0:T(8,128)(2,1)}, u32[]{:S(2)}) copy-start(bf16[1,1280,1280]{2,1,0:T(8,128)(2,1)} %param.10) | copy-start | bytes 9830404
  65.1 2.2 %collective-permute-start.16 = (f32[128,1280]{1,0:T(8,128)S(1)}, f32[128,1280]{1,0:T(8,128)S(1)}, u32[]{:S(2)}, u32[]{:S(2)}) collective-permute-start(f32[128,1280]{1,0:T(8,128)S(1)} %get-tuple-element.35), channel_id=1, source_target_pairs={{0,8},{8,0},{16,24},{24,16},{1,9},{9,1},{17,25},{25,17},{2,10},{10... | collective-permute-start | bytes 1966088 | tf_op jit(solution)/shard_map/ppermute | solution.py:34
  65.2 3.4 %collective-permute-start.19 = (bf16[128,1280]{1,0:T(8,128)(2,1)S(1)}, bf16[128,1280]{1,0:T(8,128)(2,1)S(1)}, u32[]{:S(2)}, u32[]{:S(2)}) collective-permute-start(bf16[128,1280]{1,0:T(8,128)(2,1)S(1)} %shard_map.103.refs_1_), channel_id=1, source_target_pairs={{0,8},{8,0},{16,24},{24,16},{1,9},{9,1},{17,25},{25,17},{2,10},{10... | collective-permute-start | bytes 983048 | tf_op jit(solution)/shard_map/ppermute | solution.py:34
  67.8 10.5 %collective-permute-start.17 = (f16[128,1408]{1,0:T(8,128)(2,1)S(1)}, f16[128,1408]{1,0:T(8,128)(2,1)S(1)}, u32[]{:S(2)}, u32[]{:S(2)}) collective-permute-start(f16[128,1408]{1,0:T(8,128)(2,1)S(1)} %pad_maximum_fusion), channel_id=1, source_target_pairs={{0,16},{8,24},{16,0},{24,8},{1,17},{9,25},{17,1},{25,9},{2,18},{10... | collective-permute-start | bytes 1081352 | tf_op jit(solution)/shard_map/ppermute | solution.py:34
  71.8 7.2 %copy-start.6 = (bf16[256,1280]{1,0:T(8,128)(2,1)}, bf16[256,1280]{1,0:T(8,128)(2,1)S(1)}, u32[]{:S(2)}) copy-start(bf16[256,1280]{1,0:T(8,128)(2,1)S(1)} %get-tuple-element.56.left) | copy-start | bytes 1966084
  71.9 6.9 %collective-permute-start.22 = (f32[128,1280]{1,0:T(8,128)S(1)}, f32[128,1280]{1,0:T(8,128)S(1)}, u32[]{:S(2)}, u32[]{:S(2)}) collective-permute-start(f32[128,1280]{1,0:T(8,128)S(1)} %get-tuple-element.40), channel_id=1, source_target_pairs={{0,8},{8,0},{16,24},{24,16},{1,9},{9,1},{17,25},{25,17},{2,10},{10... | collective-permute-start | bytes 1966088 | tf_op jit(solution)/shard_map/ppermute | solution.py:34
  78.6 1.7 %collective-permute-start.18 = (bf16[128,1280]{1,0:T(8,128)(2,1)S(1)}, bf16[128,1280]{1,0:T(8,128)(2,1)S(1)}, u32[]{:S(2)}, u32[]{:S(2)}) collective-permute-start(bf16[128,1280]{1,0:T(8,128)(2,1)S(1)} %add_convert_fusion.1.refs_1_), channel_id=1, source_target_pairs={{0,8},{8,0},{16,24},{24,16},{1,9},{9,1},{17,25},{25,17},{2,10},{10... | collective-permute-start | bytes 983048 | tf_op jit(solution)/shard_map/ppermute | solution.py:34
  79.2 10.9 %collective-permute-start.23 = (f16[128,1408]{1,0:T(8,128)(2,1)S(1)}, f16[128,1408]{1,0:T(8,128)(2,1)S(1)}, u32[]{:S(2)}, u32[]{:S(2)}) collective-permute-start(f16[128,1408]{1,0:T(8,128)(2,1)S(1)} %pad_maximum_fusion.2), channel_id=1, source_target_pairs={{0,16},{8,24},{16,0},{24,8},{1,17},{9,25},{17,1},{25,9},{2,18},{10... | collective-permute-start | bytes 1081352 | tf_op jit(solution)/shard_map/ppermute | solution.py:34
  83.0 7.9 %copy-start.8 = (bf16[256,1280]{1,0:T(8,128)(2,1)}, bf16[256,1280]{1,0:T(8,128)(2,1)S(1)}, u32[]{:S(2)}) copy-start(bf16[256,1280]{1,0:T(8,128)(2,1)S(1)} %get-tuple-element.57.right) | copy-start | bytes 1966084
  83.0 7.9 %copy-start.10 = (bf16[256,1280]{1,0:T(8,128)(2,1)}, bf16[256,1280]{1,0:T(8,128)(2,1)S(1)}, u32[]{:S(2)}) copy-start(bf16[256,1280]{1,0:T(8,128)(2,1)S(1)} %get-tuple-element.55.right) | copy-start | bytes 1966084
  83.0 7.5 %collective-permute-start.20 = (f32[128,1280]{1,0:T(8,128)S(1)}, f32[128,1280]{1,0:T(8,128)S(1)}, u32[]{:S(2)}, u32[]{:S(2)}) collective-permute-start(f32[128,1280]{1,0:T(8,128)S(1)} %get-tuple-element.38), channel_id=1, source_target_pairs={{0,8},{8,0},{16,24},{24,16},{1,9},{9,1},{17,25},{25,17},{2,10},{10... | collective-permute-start | bytes 1966088 | tf_op jit(solution)/shard_map/ppermute | solution.py:34
  90.5 1.7 %collective-permute-start.24 = (bf16[128,1280]{1,0:T(8,128)(2,1)S(1)}, bf16[128,1280]{1,0:T(8,128)(2,1)S(1)}, u32[]{:S(2)}, u32[]{:S(2)}) collective-permute-start(bf16[128,1280]{1,0:T(8,128)(2,1)S(1)} %add_convert_fusion.refs_1_), channel_id=1, source_target_pairs={{0,8},{8,0},{16,24},{24,16},{1,9},{9,1},{17,25},{25,17},{2,10},{10... | collective-permute-start | bytes 983048 | tf_op jit(solution)/shard_map/ppermute | solution.py:34
  91.1 15.0 %collective-permute-start.21 = (f16[128,1408]{1,0:T(8,128)(2,1)S(1)}, f16[128,1408]{1,0:T(8,128)(2,1)S(1)}, u32[]{:S(2)}, u32[]{:S(2)}) collective-permute-start(f16[128,1408]{1,0:T(8,128)(2,1)S(1)} %pad_maximum_fusion.1), channel_id=1, source_target_pairs={{0,16},{8,24},{16,0},{24,8},{1,17},{9,25},{17,1},{25,9},{2,18},{10... | collective-permute-start | bytes 1081352 | tf_op jit(solution)/shard_map/ppermute | solution.py:34
  93.5 13.7 %copy-start.4 = (f32[256,768]{1,0:T(8,128)}, f32[256,768]{1,0:T(8,128)S(1)}, u32[]{:S(2)}) copy-start(f32[256,768]{1,0:T(8,128)S(1)} %get-tuple-element.44.refs_7_) | copy-start | bytes 2359300
  93.5 15.7 %copy-start.2 = (bf16[1280,768]{1,0:T(8,128)(2,1)S(1)}, bf16[1280,768]{1,0:T(8,128)(2,1)}, u32[]{:S(2)}) copy-start(bf16[1280,768]{1,0:T(8,128)(2,1)} %get-tuple-element.43.refs_3_) | copy-start | bytes 5898244
  93.5 3.7 %collective-permute-start.25 = (f32[1,768]{1,0:T(1,128)S(1)}, f32[1,768]{1,0:T(1,128)S(1)}, u32[]{:S(2)}, u32[]{:S(2)}) collective-permute-start(f32[1,768]{1,0:T(1,128)S(1)} %get-tuple-element.42), channel_id=1, source_target_pairs={{0,1},{1,0},{2,3},{3,2},{4,5},{5,4},{6,7},{7,6},{8,9},{9,8},{10,11... | collective-permute-start | bytes 9224 | tf_op jit(solution)/shard_map/ppermute | solution.py:34
  97.1 3.6 %collective-permute-start.26 = (f32[1,768]{1,0:T(1,128)S(1)}, f32[1,768]{1,0:T(1,128)S(1)}, u32[]{:S(2)}, u32[]{:S(2)}) collective-permute-start(f32[1,768]{1,0:T(1,128)S(1)} %add.85), channel_id=1, source_target_pairs={{0,2},{1,3},{2,0},{3,1},{4,6},{5,7},{6,4},{7,5},{8,10},{9,11},{10,... | collective-permute-start | bytes 9224 | tf_op jit(solution)/shard_map/ppermute | solution.py:34
  100.7 5.3 %collective-permute-start.27 = (f32[1,768]{1,0:T(1,128)S(1)}, f32[1,768]{1,0:T(1,128)S(1)}, u32[]{:S(2)}, u32[]{:S(2)}) collective-permute-start(f32[1,768]{1,0:T(1,128)S(1)} %add.86), channel_id=1, source_target_pairs={{0,4},{1,5},{2,6},{3,7},{4,0},{5,1},{6,2},{7,3},{8,12},{9,13},{10,... | collective-permute-start | bytes 9224 | tf_op jit(solution)/shard_map/ppermute | solution.py:34
  107.2 2.0 %collective-permute-start.28 = (bf16[128,1280]{1,0:T(8,128)(2,1)}, bf16[128,1280]{1,0:T(8,128)(2,1)}, u32[]{:S(2)}, u32[]{:S(2)}) collective-permute-start(bf16[128,1280]{1,0:T(8,128)(2,1)} %shard_map.108.refs_1_), channel_id=1, source_target_pairs={{0,8},{8,0},{16,24},{24,16},{1,9},{9,1},{17,25},{25,17},{2,10},{10... | collective-permute-start | bytes 983048 | tf_op jit(solution)/shard_map/ppermute | solution.py:34
  109.2 1.1 copy-start.5
  110.3 1.1 copy-start.13
  114.8 9.4 %collective-permute-start.30 = (bf16[160,768]{1,0:T(8,128)(2,1)S(1)}, bf16[160,768]{1,0:T(8,128)(2,1)S(1)}, u32[]{:S(2)}, u32[]{:S(2)}) collective-permute-start(bf16[160,768]{1,0:T(8,128)(2,1)S(1)} %get-tuple-element.49), channel_id=1, source_target_pairs={{0,1},{1,0},{2,3},{3,2},{4,5},{5,4},{6,7},{7,6},{8,9},{9,8},{10,11... | collective-permute-start | bytes 737288 | tf_op jit(solution)/shard_map/ppermute | solution.py:34
  116.4 3.4 %copy-start.11 = (bf16[256,1280]{1,0:T(8,128)(2,1)S(1)}, bf16[256,1280]{1,0:T(8,128)(2,1)}, u32[]{:S(2)}) copy-start(bf16[256,1280]{1,0:T(8,128)(2,1)} %copy-done.10) | copy-start | bytes 1966084
  117.1 24.5 %collective-permute-start.29 = (bf16[160,768]{1,0:T(8,128)(2,1)S(1)}, bf16[160,768]{1,0:T(8,128)(2,1)S(1)}, u32[]{:S(2)}, u32[]{:S(2)}) collective-permute-start(bf16[160,768]{1,0:T(8,128)(2,1)S(1)} %get-tuple-element.47), channel_id=1, source_target_pairs={{0,1},{1,0},{2,3},{3,2},{4,5},{5,4},{6,7},{7,6},{8,9},{9,8},{10,11... | collective-permute-start | bytes 737288 | tf_op jit(solution)/shard_map/ppermute | solution.py:34
  117.7 8.9 %collective-permute-start.32 = (bf16[160,768]{1,0:T(8,128)(2,1)S(1)}, bf16[160,768]{1,0:T(8,128)(2,1)S(1)}, u32[]{:S(2)}, u32[]{:S(2)}) collective-permute-start(bf16[160,768]{1,0:T(8,128)(2,1)S(1)} %get-tuple-element.52), channel_id=1, source_target_pairs={{0,2},{1,3},{2,0},{3,1},{4,6},{5,7},{6,4},{7,5},{8,10},{9,11},{10,... | collective-permute-start | bytes 737288 | tf_op jit(solution)/shard_map/ppermute | solution.py:34
  118.6 13.2 %collective-permute-start.34 = (bf16[160,768]{1,0:T(8,128)(2,1)S(1)}, bf16[160,768]{1,0:T(8,128)(2,1)S(1)}, u32[]{:S(2)}, u32[]{:S(2)}) collective-permute-start(bf16[160,768]{1,0:T(8,128)(2,1)S(1)} %get-tuple-element.53), channel_id=1, source_target_pairs={{0,2},{1,3},{2,0},{3,1},{4,6},{5,7},{6,4},{7,5},{8,10},{9,11},{10,... | collective-permute-start | bytes 737288 | tf_op jit(solution)/shard_map/ppermute | solution.py:34
  119.7 8.5 %collective-permute-start.36 = (bf16[2,320,256]{2,1,0:T(8,128)(2,1)S(1)}, bf16[2,320,256]{2,1,0:T(8,128)(2,1)S(1)}, u32[]{:S(2)}, u32[]{:S(2)}) collective-permute-start(bf16[2,320,256]{2,1,0:T(8,128)(2,1)S(1)} %fusion), channel_id=1, source_target_pairs={{0,8},{8,0},{16,24},{24,16},{1,9},{9,1},{17,25},{25,17},{2,10},{10... | collective-permute-start | bytes 983048 | tf_op jit(solution)/shard_map/ppermute | solution.py:34
  124.3 17.3 %collective-permute-start.31 = (bf16[160,768]{1,0:T(8,128)(2,1)S(1)}, bf16[160,768]{1,0:T(8,128)(2,1)S(1)}, u32[]{:S(2)}, u32[]{:S(2)}) collective-permute-start(bf16[160,768]{1,0:T(8,128)(2,1)S(1)} %add_convert_fusion.4), channel_id=1, source_target_pairs={{0,2},{1,3},{2,0},{3,1},{4,6},{5,7},{6,4},{7,5},{8,10},{9,11},{10,... | collective-permute-start | bytes 737288 | tf_op jit(solution)/shard_map/ppermute | solution.py:34
  126.5 9.9 %copy-start.7 = (bf16[256,1280]{1,0:T(8,128)(2,1)S(1)}, bf16[256,1280]{1,0:T(8,128)(2,1)}, u32[]{:S(2)}) copy-start(bf16[256,1280]{1,0:T(8,128)(2,1)} %copy-done.6) | copy-start | bytes 1966084
  126.6 9.9 %copy-start.9 = (bf16[256,1280]{1,0:T(8,128)(2,1)S(1)}, bf16[256,1280]{1,0:T(8,128)(2,1)}, u32[]{:S(2)}) copy-start(bf16[256,1280]{1,0:T(8,128)(2,1)} %copy-done.8) | copy-start | bytes 1966084
  126.6 6.8 %collective-permute-start.33 = (bf16[160,768]{1,0:T(8,128)(2,1)S(1)}, bf16[160,768]{1,0:T(8,128)(2,1)S(1)}, u32[]{:S(2)}, u32[]{:S(2)}) collective-permute-start(bf16[160,768]{1,0:T(8,128)(2,1)S(1)} %add_convert_fusion.3), channel_id=1, source_target_pairs={{0,1},{1,0},{2,3},{3,2},{4,5},{5,4},{6,7},{7,6},{8,9},{9,8},{10,11... | collective-permute-start | bytes 737288 | tf_op jit(solution)/shard_map/ppermute | solution.py:34
  128.3 12.5 %collective-permute-start.37 = (bf16[320,256]{1,0:T(8,128)(2,1)S(1)}, bf16[320,256]{1,0:T(8,128)(2,1)S(1)}, u32[]{:S(2)}, u32[]{:S(2)}) collective-permute-start(bf16[320,256]{1,0:T(8,128)(2,1)S(1)} %fusion.1), channel_id=1, source_target_pairs={{0,16},{8,24},{16,0},{24,8},{1,17},{9,25},{17,1},{25,9},{2,18},{10... | collective-permute-start | bytes 491528 | tf_op jit(solution)/shard_map/ppermute | solution.py:34
  133.5 12.3 %collective-permute-start.35 = (bf16[160,768]{1,0:T(8,128)(2,1)S(1)}, bf16[160,768]{1,0:T(8,128)(2,1)S(1)}, u32[]{:S(2)}, u32[]{:S(2)}) collective-permute-start(bf16[160,768]{1,0:T(8,128)(2,1)S(1)} %add_convert_fusion.2), channel_id=1, source_target_pairs={{0,4},{1,5},{2,6},{3,7},{4,0},{5,1},{6,2},{7,3},{8,12},{9,13},{10,... | collective-permute-start | bytes 737288 | tf_op jit(solution)/shard_map/ppermute | solution.py:34

commit v4 on v3

--- a/solution.py
+++ b/solution.py
@@ -306,10 +306,11 @@
         [pltpu.VMEM((slots, width), BF16)],
         vmem=24,
     )
-    k = 1
-    while k < n_exp:
-        row_stat = row_stat + swap(row_stat, "exp", k)
-        k *= 2
+    inner = 1 << ((n_exp.bit_length() - 1) // 2)
+    for peers in (range(1, inner), range(inner, n_exp, inner)):
+        row_part = row_stat
+        for k in peers:
+            row_stat = row_stat + swap(row_part, "exp", k)
     slot_grad, pre_grad, mine, other = call(
         backward_kernel,
         [sds((slots, width), BF16), sds((slots, hidden_units), BF16), *wide],

time: 147 us -> 146 us (level)
  starting transfers between devices: 42.7 us -> 40.7 us
    ppermute x38 -> x39, starting transfers between devices: 42.7 us -> 40.7 us  [swap(): return lax.ppermute(x, axis, [(i, i ^ k) for i in range(n)])]
    ppermute x38 -> x39, waiting for transfers between devices: 67.3 us -> 68.1 us  [swap(): return lax.ppermute(x, axis, [(i, i ^ k) for i in range(n)])]
  transfers between devices with their start and end apart: 38 -> 39, of which waited for: 23 -> 23; matrix products, arithmetic and copies ran while one was open for 4% -> 4% of each run, Pallas kernels for 11% -> 11%
where the time goes in v4:
time: 146 us; the launch traced here: 145 us
  waiting for transfers between devices  68.1 us (47%)
  starting transfers between devices  40.7 us (28%)
  Pallas kernels  24 us (16%)
  other arithmetic  6.43 us (4%)
  local copies, waits for them, and re-layouts  4.49 us (3%)
    ppermute x39, waiting for transfers between devices, swap(): return lax.ppermute(x, axis, [(i, i ^ k) for i in range(n)])  68.1 us
    ppermute x39, starting transfers between devices, swap(): return lax.ppermute(x, axis, [(i, i ^ k) for i in range(n)])  40.7 us
    pallas_call x6, Pallas kernels, call(): pl.pallas_call(kernel, out_shape=outs, in_specs=in_specs, out_specs=[pl.B...  14.4 us
    pallas_call x2, Pallas kernels, weight_grad(): pl.pallas_call(weight_grad_kernel, out_shape=sds((rows, columns), F32), g...  8.72 us
    unnamed x30, local copies, waits for them, and re-layouts  3.36 us
  transfers between devices with their start and end apart: 39, of which 23 were waited for; matrix products, arithmetic and copies ran while one was open for 4% of the time, Pallas kernels for 11%

profile of v4, /device:TPU:0, one launch (start us, length us, event | category | flops | bytes accessed | tf_op | source)
XLA Modules:
  0.0 145.5 jit_solution(3792071117240115590)
XLA Ops:
  0.6 1.1 convert_bitcast_fusion.refs_1_
  1.7 4.1 %collective-permute-start.10 = (bf16[160,768]{1,0:T(8,128)(2,1)S(1)}, bf16[160,768]{1,0:T(8,128)(2,1)S(1)}, u32[]{:S(2)}, u32[]{:S(2)}) collective-permute-start(bf16[160,768]{1,0:T(8,128)(2,1)S(1)} %convert_bitcast_fusion.refs_1_), channel_id=1, source_target_pairs={{0,4},{1,5},{2,6},{3,7},{4,0},{5,1},{6,2},{7,3},{8,12},{9,13},{10,... | collective-permute-start | bytes 737288 | tf_op jit(solution)/shard_map/ppermute | solution.py:34
  5.8 1.6 %collective-permute-start.8 = (bf16[160,768]{1,0:T(8,128)(2,1)S(1)}, bf16[160,768]{1,0:T(8,128)(2,1)S(1)}, u32[]{:S(2)}, u32[]{:S(2)}) collective-permute-start(bf16[160,768]{1,0:T(8,128)(2,1)S(1)} %convert_bitcast_fusion.refs_1_), channel_id=1, source_target_pairs={{0,2},{1,3},{2,0},{3,1},{4,6},{5,7},{6,4},{7,5},{8,10},{9,11},{10,... | collective-permute-start | bytes 737288 | tf_op jit(solution)/shard_map/ppermute | solution.py:34
  7.4 9.7 %collective-permute-done.10.refs_5_ = bf16[160,768]{1,0:T(8,128)(2,1)S(1)} collective-permute-done((bf16[160,768]{1,0:T(8,128)(2,1)S(1)}, bf16[160,768]{1,0:T(8,128)(2,1)S(1)}, u32[]{:S(2)}, u32[]{:S(2)}) %collective-permute-start.10) | collective-permute-done | bytes 245792 | tf_op jit(solution)/shard_map/ppermute | solution.py:34
  17.1 1.6 %collective-permute-start.11 = (bf16[160,768]{1,0:T(8,128)(2,1)S(1)}, bf16[160,768]{1,0:T(8,128)(2,1)S(1)}, u32[]{:S(2)}, u32[]{:S(2)}) collective-permute-start(bf16[160,768]{1,0:T(8,128)(2,1)S(1)} %collective-permute-done.10.refs_5_), channel_id=1, source_target_pairs={{0,1},{1,0},{2,3},{3,2},{4,5},{5,4},{6,7},{7,6},{8,9},{9,8},{10,11... | collective-permute-start | bytes 737288 | tf_op jit(solution)/shard_map/ppermute | solution.py:34
  19.1 1.1 convert_bitcast_fusion.1.refs_1_
  20.3 4.0 %collective-permute-start.12 = (bf16[160,768]{1,0:T(8,128)(2,1)S(1)}, bf16[160,768]{1,0:T(8,128)(2,1)S(1)}, u32[]{:S(2)}, u32[]{:S(2)}) collective-permute-start(bf16[160,768]{1,0:T(8,128)(2,1)S(1)} %collective-permute-done.10.refs_5_), channel_id=1, source_target_pairs={{0,2},{1,3},{2,0},{3,1},{4,6},{5,7},{6,4},{7,5},{8,10},{9,11},{10,... | collective-permute-start | bytes 737288 | tf_op jit(solution)/shard_map/ppermute | solution.py:34
  24.3 1.5 %collective-permute-start.9 = (bf16[160,768]{1,0:T(8,128)(2,1)S(1)}, bf16[160,768]{1,0:T(8,128)(2,1)S(1)}, u32[]{:S(2)}, u32[]{:S(2)}) collective-permute-start(bf16[160,768]{1,0:T(8,128)(2,1)S(1)} %collective-permute-done.8.refs_3_), channel_id=1, source_target_pairs={{0,1},{1,0},{2,3},{3,2},{4,5},{5,4},{6,7},{7,6},{8,9},{9,8},{10,11... | collective-permute-start | bytes 737288 | tf_op jit(solution)/shard_map/ppermute | solution.py:34
  26.0 0.5 collective-permute-start.13
  26.6 0.8 copy.15.refs_10_.refs_5_
  27.4 5.6 %collective-permute-done.3.refs_5_ = bf16[160,768]{1,0:T(8,128)(2,1)S(1)} collective-permute-done((bf16[160,768]{1,0:T(8,128)(2,1)S(1)}, bf16[160,768]{1,0:T(8,128)(2,1)S(1)}, u32[]{:S(2)}, u32[]{:S(2)}) %collective-permute-start.3) | collective-permute-done | bytes 245792 | tf_op jit(solution)/shard_map/ppermute | solution.py:34
  33.1 1.6 %collective-permute-done.12.refs_7_ = bf16[160,768]{1,0:T(8,128)(2,1)S(1)} collective-permute-done((bf16[160,768]{1,0:T(8,128)(2,1)S(1)}, bf16[160,768]{1,0:T(8,128)(2,1)S(1)}, u32[]{:S(2)}, u32[]{:S(2)}) %collective-permute-start.12) | collective-permute-done | bytes 245792 | tf_op jit(solution)/shard_map/ppermute | solution.py:34
  34.7 3.7 %collective-permute-done.13.refs_8_ = bf16[160,768]{1,0:T(8,128)(2,1)S(1)} collective-permute-done((bf16[160,768]{1,0:T(8,128)(2,1)S(1)}, bf16[160,768]{1,0:T(8,128)(2,1)S(1)}, u32[]{:S(2)}, u32[]{:S(2)}) %collective-permute-start.13) | collective-permute-done | bytes 245792 | tf_op jit(solution)/shard_map/ppermute | solution.py:34
  38.4 1.1 copy-done.12
  39.5 2.3 %shard_map.102 = (bf16[1280,768]{1,0:T(8,128)(2,1)}, f32[256,768]{1,0:T(8,128)}, f32[128,1280]{1,0:T(8,128)S(1)}, f32[128,1280]{1,0:T(8,128)S(1)}) custom-call(s32[2]{0:T(128)S(1)} %pad_add_fusion.refs_0_, bf16[160,768]{1,0:T(8,128)(2,1)S(1)} %convert_bitcast_fusion.refs_1_, bf16[160,768]{1,0:T(8,128)(2,1)S(1)} %collective-permute-done.7.refs_2_, ...), custom_call_target="tpu_custom_call" | custom-call | flops 1006632960 | bytes 6685704 | tf_op jit(solution)/shard_map/pallas_call | solution.py:86
  41.8 2.1 %collective-permute-done.14 = f32[128,1280]{1,0:T(8,128)S(1)} collective-permute-done((f32[128,1280]{1,0:T(8,128)S(1)}, f32[128,1280]{1,0:T(8,128)S(1)}, u32[]{:S(2)}, u32[]{:S(2)}) %collective-permute-start.14) | collective-permute-done | bytes 655392 | tf_op jit(solution)/shard_map/ppermute | solution.py:34
  44.0 1.3 collective-permute-start.15
  45.3 1.5 %collective-permute-start.4 = (bf16[160,768]{1,0:T(8,128)(2,1)S(1)}, bf16[160,768]{1,0:T(8,128)(2,1)S(1)}, u32[]{:S(2)}, u32[]{:S(2)}) collective-permute-start(bf16[160,768]{1,0:T(8,128)(2,1)S(1)} %collective-permute-done.3.refs_5_), channel_id=1, source_target_pairs={{0,1},{1,0},{2,3},{3,2},{4,5},{5,4},{6,7},{7,6},{8,9},{9,8},{10,11... | collective-permute-start | bytes 737288 | tf_op jit(solution)/shard_map/ppermute | solution.py:34
  46.9 0.5 collective-permute-start
  47.4 2.0 %collective-permute-start.5 = (bf16[160,768]{1,0:T(8,128)(2,1)S(1)}, bf16[160,768]{1,0:T(8,128)(2,1)S(1)}, u32[]{:S(2)}, u32[]{:S(2)}) collective-permute-start(bf16[160,768]{1,0:T(8,128)(2,1)S(1)} %collective-permute-done.3.refs_5_), channel_id=1, source_target_pairs={{0,2},{1,3},{2,0},{3,1},{4,6},{5,7},{6,4},{7,5},{8,10},{9,11},{10,... | collective-permute-start | bytes 737288 | tf_op jit(solution)/shard_map/ppermute | solution.py:34
  49.4 4.8 %collective-permute-done.1.refs_3_ = bf16[160,768]{1,0:T(8,128)(2,1)S(1)} collective-permute-done((bf16[160,768]{1,0:T(8,128)(2,1)S(1)}, bf16[160,768]{1,0:T(8,128)(2,1)S(1)}, u32[]{:S(2)}, u32[]{:S(2)}) %collective-permute-start.1) | collective-permute-done | bytes 245792 | tf_op jit(solution)/shard_map/ppermute | solution.py:34
  54.2 1.5 %collective-permute-start.2 = (bf16[160,768]{1,0:T(8,128)(2,1)S(1)}, bf16[160,768]{1,0:T(8,128)(2,1)S(1)}, u32[]{:S(2)}, u32[]{:S(2)}) collective-permute-start(bf16[160,768]{1,0:T(8,128)(2,1)S(1)} %collective-permute-done.1.refs_3_), channel_id=1, source_target_pairs={{0,1},{1,0},{2,3},{3,2},{4,5},{5,4},{6,7},{7,6},{8,9},{9,8},{10,11... | collective-permute-start | bytes 737288 | tf_op jit(solution)/shard_map/ppermute | solution.py:34
  55.7 0.5 collective-permute-start.6
  56.3 3.2 %collective-permute-done.refs_2_ = bf16[160,768]{1,0:T(8,128)(2,1)S(1)} collective-permute-done((bf16[160,768]{1,0:T(8,128)(2,1)S(1)}, bf16[160,768]{1,0:T(8,128)(2,1)S(1)}, u32[]{:S(2)}, u32[]{:S(2)}) %collective-permute-start) | collective-permute-done | bytes 245792 | tf_op jit(solution)/shard_map/ppermute | solution.py:34
  59.5 1.4 collective-permute-done.15.got
  61.0 2.6 %collective-permute-done.2.refs_4_ = bf16[160,768]{1,0:T(8,128)(2,1)S(1)} collective-permute-done((bf16[160,768]{1,0:T(8,128)(2,1)S(1)}, bf16[160,768]{1,0:T(8,128)(2,1)S(1)}, u32[]{:S(2)}, u32[]{:S(2)}) %collective-permute-start.2) | collective-permute-done | bytes 245792 | tf_op jit(solution)/shard_map/ppermute | solution.py:34
  63.6 1.5 %shard_map.104 = (bf16[1280,768]{1,0:T(8,128)(2,1)S(1)}, f32[128,1280]{1,0:T(8,128)S(1)}, f32[128,1280]{1,0:T(8,128)S(1)}) custom-call(s32[2]{0:T(128)S(1)} %pad_add_fusion.refs_0_, bf16[160,768]{1,0:T(8,128)(2,1)S(1)} %convert_bitcast_fusion.1.refs_1_, bf16[160,768]{1,0:T(8,128)(2,1)S(1)} %collective-permute-done.refs_2_, ...), custom_call_target="tpu_custom_call" | custom-call | flops 503316480 | bytes 6032392 | tf_op jit(solution)/shard_map/pallas_call | solution.py:86
  65.7 1.6 %collective-permute-done.16 = f32[128,1280]{1,0:T(8,128)S(1)} collective-permute-done((f32[128,1280]{1,0:T(8,128)S(1)}, f32[128,1280]{1,0:T(8,128)S(1)}, u32[]{:S(2)}, u32[]{:S(2)}) %collective-permute-start.16) | collective-permute-done | bytes 655392 | tf_op jit(solution)/shard_map/ppermute | solution.py:34
  67.8 0.8 collective-permute-start.17
  68.6 3.2 %shard_map.105 = (bf16[256,1280]{1,0:T(8,128)(2,1)S(1)}, bf16[256,1280]{1,0:T(8,128)(2,1)S(1)}, f32[256,1280]{1,0:T(8,128)S(1)}, f32[128,1280]{1,0:T(8,128)S(1)}, f32[128,1280]{1,0:T(8,128)S(1)}) custom-call(s32[2]{0:T(128)S(1)} %pad_add_fusion.refs_0_, bf16[128,1280]{1,0:T(8,128)(2,1)S(1)} %shard_map.103.refs_1_, ...), custom_call_target="tpu_custom_call" | custom-call | flops 1677721600 | bytes 11141128 | tf_op jit(solution)/shard_map/pallas_call | solution.py:86
  71.9 6.3 %collective-permute-done.17 = f16[128,1408]{1,0:T(8,128)(2,1)S(1)} collective-permute-done((f16[128,1408]{1,0:T(8,128)(2,1)S(1)}, f16[128,1408]{1,0:T(8,128)(2,1)S(1)}, u32[]{:S(2)}, u32[]{:S(2)}) %collective-permute-start.17) | collective-permute-done | bytes 360480 | tf_op jit(solution)/shard_map/ppermute | solution.py:34
  79.2 0.8 collective-permute-start.23
  80.3 2.7 %shard_map.106 = (bf16[256,1280]{1,0:T(8,128)(2,1)S(1)}, bf16[256,1280]{1,0:T(8,128)(2,1)S(1)}, f32[128,1280]{1,0:T(8,128)S(1)}, f32[128,1280]{1,0:T(8,128)S(1)}) custom-call(s32[2]{0:T(128)S(1)} %pad_add_fusion.refs_0_, bf16[128,1280]{1,0:T(8,128)(2,1)S(1)} %add_convert_fusion.1.refs_1_, bf16[128,1280]{1,0:T(8,128)(2,1)S(1)} %collective-permute-done.18.refs_2_, ...), custom_call_target="tpu_custom_call" | custom-call | flops 1677721600 | bytes 11141128 | tf_op jit(solution)/shard_map/pallas_call | solution.py:86
  83.2 6.9 %collective-permute-done.23 = f16[128,1408]{1,0:T(8,128)(2,1)S(1)} collective-permute-done((f16[128,1408]{1,0:T(8,128)(2,1)S(1)}, f16[128,1408]{1,0:T(8,128)(2,1)S(1)}, u32[]{:S(2)}, u32[]{:S(2)}) %collective-permute-start.23) | collective-permute-done | bytes 360480 | tf_op jit(solution)/shard_map/ppermute | solution.py:34
  91.1 0.8 collective-permute-start.21
  92.2 1.3 shard_map.107
  93.5 1.6 %collective-permute-start.25 = (f32[1,768]{1,0:T(1,128)S(1)}, f32[1,768]{1,0:T(1,128)S(1)}, u32[]{:S(2)}, u32[]{:S(2)}) collective-permute-start(f32[1,768]{1,0:T(1,128)S(1)} %get-tuple-element.42), channel_id=1, source_target_pairs={{0,1},{1,0},{2,3},{3,2},{4,5},{5,4},{6,7},{7,6},{8,9},{9,8},{10,11... | collective-permute-start | bytes 9224 | tf_op jit(solution)/shard_map/ppermute | solution.py:34
  95.1 2.1 %collective-permute-done.25 = f32[1,768]{1,0:T(1,128)S(1)} collective-permute-done((f32[1,768]{1,0:T(1,128)S(1)}, f32[1,768]{1,0:T(1,128)S(1)}, u32[]{:S(2)}, u32[]{:S(2)}) %collective-permute-start.25) | collective-permute-done | bytes 3104 | tf_op jit(solution)/shard_map/ppermute | solution.py:34
  97.1 3.5 %collective-permute-start.28 = (f32[1,768]{1,0:T(1,128)S(1)}, f32[1,768]{1,0:T(1,128)S(1)}, u32[]{:S(2)}, u32[]{:S(2)}) collective-permute-start(f32[1,768]{1,0:T(1,128)S(1)} %add.88), channel_id=1, source_target_pairs={{0,6},{1,7},{2,4},{3,5},{4,2},{5,3},{6,0},{7,1},{8,14},{9,15},{10,... | collective-permute-start | bytes 9224 | tf_op jit(solution)/shard_map/ppermute | solution.py:34
  101.0 0.6 collective-permute-start.26
  101.5 1.0 collective-permute-done.28
  102.5 2.6 %collective-permute-done.27 = f32[1,768]{1,0:T(1,128)S(1)} collective-permute-done((f32[1,768]{1,0:T(1,128)S(1)}, f32[1,768]{1,0:T(1,128)S(1)}, u32[]{:S(2)}, u32[]{:S(2)}) %collective-permute-start.27) | collective-permute-done | bytes 3104 | tf_op jit(solution)/shard_map/ppermute | solution.py:34
  105.5 0.8 shard_map.108.refs_1_
  106.3 2.0 %collective-permute-done.29.refs_2_ = bf16[128,1280]{1,0:T(8,128)(2,1)} collective-permute-done((bf16[128,1280]{1,0:T(8,128)(2,1)}, bf16[128,1280]{1,0:T(8,128)(2,1)}, u32[]{:S(2)}, u32[]{:S(2)}) %collective-permute-start.29) | collective-permute-done | bytes 327712 | tf_op jit(solution)/shard_map/ppermute | solution.py:34
  108.2 1.1 copy-done.5
  109.4 1.1 copy-done.13
  110.4 3.4 %shard_map.109 = (bf16[256,768]{1,0:T(8,128)(2,1)S(1)}, f32[160,768]{1,0:T(8,128)S(1)}, bf16[160,768]{1,0:T(8,128)(2,1)S(1)}, f32[160,768]{1,0:T(8,128)S(1)}, bf...) custom-call(s32[2]{0:T(128)S(1)} %pad_add_fusion.refs_0_, ...), custom_call_target="tpu_custom_call" | custom-call | flops 1509949440 | bytes 8854536 | tf_op jit(solution)/shard_map/pallas_call | solution.py:86
  113.8 1.6 %collective-permute-start.31 = (bf16[160,768]{1,0:T(8,128)(2,1)S(1)}, bf16[160,768]{1,0:T(8,128)(2,1)S(1)}, u32[]{:S(2)}, u32[]{:S(2)}) collective-permute-start(bf16[160,768]{1,0:T(8,128)(2,1)S(1)} %get-tuple-element.49), channel_id=1, source_target_pairs={{0,1},{1,0},{2,3},{3,2},{4,5},{5,4},{6,7},{7,6},{8,9},{9,8},{10,11... | collective-permute-start | bytes 737288 | tf_op jit(solution)/shard_map/ppermute | solution.py:34
  115.4 0.7 fusion.5
  116.1 0.6 collective-permute-start.30
  116.7 0.9 collective-permute-start.33
  117.6 1.2 collective-permute-start.35
  118.9 4.4 %shard_map.110 = f32[1280,1280]{1,0:T(8,128)} custom-call(bf16[256,1280]{1,0:T(8,128)(2,1)S(1)} %get-tuple-element.45.refs_9_.left, bf16[256,1280]{1,0:T(8,128)(2,1)S(1)} %copy-done.11, bf16[256,768]{1,0:T(8,128)(2,1)S(1)} %get-tuple-element.54._), custom_call_target="tpu_custom_call" | custom-call | flops 838860800 | bytes 6553600 | tf_op jit(solution)/shard_map/pallas_call | solution.py:228
  123.3 0.9 collective-permute-start.32
  124.2 1.4 collective-permute-done.33
  125.7 1.6 %collective-permute-start.34 = (bf16[160,768]{1,0:T(8,128)(2,1)S(1)}, bf16[160,768]{1,0:T(8,128)(2,1)S(1)}, u32[]{:S(2)}, u32[]{:S(2)}) collective-permute-start(bf16[160,768]{1,0:T(8,128)(2,1)S(1)} %add_convert_fusion.3), channel_id=1, source_target_pairs={{0,1},{1,0},{2,3},{3,2},{4,5},{5,4},{6,7},{7,6},{8,9},{9,8},{10,11... | collective-permute-start | bytes 737288 | tf_op jit(solution)/shard_map/ppermute | solution.py:34
  127.4 1.1 collective-permute-start.38
  128.5 2.4 %collective-permute-done.35 = bf16[160,768]{1,0:T(8,128)(2,1)S(1)} collective-permute-done((bf16[160,768]{1,0:T(8,128)(2,1)S(1)}, bf16[160,768]{1,0:T(8,128)(2,1)S(1)}, u32[]{:S(2)}, u32[]{:S(2)}) %collective-permute-start.35) | collective-permute-done | bytes 245792 | tf_op jit(solution)/shard_map/ppermute | solution.py:34
  130.9 1.6 %collective-permute-done.34 = bf16[160,768]{1,0:T(8,128)(2,1)S(1)} collective-permute-done((bf16[160,768]{1,0:T(8,128)(2,1)S(1)}, bf16[160,768]{1,0:T(8,128)(2,1)S(1)}, u32[]{:S(2)}, u32[]{:S(2)}) %collective-permute-start.34) | collective-permute-done | bytes 245792 | tf_op jit(solution)/shard_map/ppermute | solution.py:34
  132.5 2.1 %collective-permute-start.36 = (bf16[160,768]{1,0:T(8,128)(2,1)S(1)}, bf16[160,768]{1,0:T(8,128)(2,1)S(1)}, u32[]{:S(2)}, u32[]{:S(2)}) collective-permute-start(bf16[160,768]{1,0:T(8,128)(2,1)S(1)} %add_convert_fusion.2), channel_id=1, source_target_pairs={{0,4},{1,5},{2,6},{3,7},{4,0},{5,1},{6,2},{7,3},{8,12},{9,13},{10,... | collective-permute-start | bytes 737288 | tf_op jit(solution)/shard_map/ppermute | solution.py:34
  134.6 4.4 %shard_map.111 = f32[1280,1280]{1,0:T(8,128)} custom-call(bf16[256,1280]{1,0:T(8,128)(2,1)S(1)} %copy-done.7, bf16[256,1280]{1,0:T(8,128)(2,1)S(1)} %copy-done.9, bf16[256,768]{1,0:T(8,128)(2,1)S(1)} %get-tuple-element.54._), custom_call_target="tpu_custom_call" | custom-call | flops 838860800 | bytes 6553600 | tf_op jit(solution)/shard_map/pallas_call | solution.py:228
  139.0 0.8 bitcast_add_fusion.1
  139.7 4.8 %collective-permute-done.36 = bf16[160,768]{1,0:T(8,128)(2,1)S(1)} collective-permute-done((bf16[160,768]{1,0:T(8,128)(2,1)S(1)}, bf16[160,768]{1,0:T(8,128)(2,1)S(1)}, u32[]{:S(2)}, u32[]{:S(2)}) %collective-permute-start.36) | collective-permute-done | bytes 245792 | tf_op jit(solution)/shard_map/ppermute | solution.py:34
  144.6 0.9 add_bitcast_fusion
  (100 shorter events, 5.8 us)
Async XLA Ops:
  1.7 15.4 %collective-permute-start.10 = (bf16[160,768]{1,0:T(8,128)(2,1)S(1)}, bf16[160,768]{1,0:T(8,128)(2,1)S(1)}, u32[]{:S(2)}, u32[]{:S(2)}) collective-permute-start(bf16[160,768]{1,0:T(8,128)(2,1)S(1)} %convert_bitcast_fusion.refs_1_), channel_id=1, source_target_pairs={{0,4},{1,5},{2,6},{3,7},{4,0},{5,1},{6,2},{7,3},{8,12},{9,13},{10,... | collective-permute-start | bytes 737288 | tf_op jit(solution)/shard_map/ppermute | solution.py:34
  5.8 18.5 %collective-permute-start.8 = (bf16[160,768]{1,0:T(8,128)(2,1)S(1)}, bf16[160,768]{1,0:T(8,128)(2,1)S(1)}, u32[]{:S(2)}, u32[]{:S(2)}) collective-permute-start(bf16[160,768]{1,0:T(8,128)(2,1)S(1)} %convert_bitcast_fusion.refs_1_), channel_id=1, source_target_pairs={{0,2},{1,3},{2,0},{3,1},{4,6},{5,7},{6,4},{7,5},{8,10},{9,11},{10,... | collective-permute-start | bytes 737288 | tf_op jit(solution)/shard_map/ppermute | solution.py:34
  17.1 8.9 %collective-permute-start.11 = (bf16[160,768]{1,0:T(8,128)(2,1)S(1)}, bf16[160,768]{1,0:T(8,128)(2,1)S(1)}, u32[]{:S(2)}, u32[]{:S(2)}) collective-permute-start(bf16[160,768]{1,0:T(8,128)(2,1)S(1)} %collective-permute-done.10.refs_5_), channel_id=1, source_target_pairs={{0,1},{1,0},{2,3},{3,2},{4,5},{5,4},{6,7},{7,6},{8,9},{9,8},{10,11... | collective-permute-start | bytes 737288 | tf_op jit(solution)/shard_map/ppermute | solution.py:34
  18.7 14.4 %collective-permute-start.7 = (bf16[160,768]{1,0:T(8,128)(2,1)S(1)}, bf16[160,768]{1,0:T(8,128)(2,1)S(1)}, u32[]{:S(2)}, u32[]{:S(2)}) collective-permute-start(bf16[160,768]{1,0:T(8,128)(2,1)S(1)} %convert_bitcast_fusion.refs_1_), channel_id=1, source_target_pairs={{0,1},{1,0},{2,3},{3,2},{4,5},{5,4},{6,7},{7,6},{8,9},{9,8},{10,11... | collective-permute-start | bytes 737288 | tf_op jit(solution)/shard_map/ppermute | solution.py:34
  20.2 12.9 %collective-permute-start.3 = (bf16[160,768]{1,0:T(8,128)(2,1)S(1)}, bf16[160,768]{1,0:T(8,128)(2,1)S(1)}, u32[]{:S(2)}, u32[]{:S(2)}) collective-permute-start(bf16[160,768]{1,0:T(8,128)(2,1)S(1)} %convert_bitcast_fusion.1.refs_1_), channel_id=1, source_target_pairs={{0,4},{1,5},{2,6},{3,7},{4,0},{5,1},{6,2},{7,3},{8,12},{9,13},{10,... | collective-permute-start | bytes 737288 | tf_op jit(solution)/shard_map/ppermute | solution.py:34
  20.3 14.4 %collective-permute-start.12 = (bf16[160,768]{1,0:T(8,128)(2,1)S(1)}, bf16[160,768]{1,0:T(8,128)(2,1)S(1)}, u32[]{:S(2)}, u32[]{:S(2)}) collective-permute-start(bf16[160,768]{1,0:T(8,128)(2,1)S(1)} %collective-permute-done.10.refs_5_), channel_id=1, source_target_pairs={{0,2},{1,3},{2,0},{3,1},{4,6},{5,7},{6,4},{7,5},{8,10},{9,11},{10,... | collective-permute-start | bytes 737288 | tf_op jit(solution)/shard_map/ppermute | solution.py:34
  24.3 10.5 %collective-permute-start.9 = (bf16[160,768]{1,0:T(8,128)(2,1)S(1)}, bf16[160,768]{1,0:T(8,128)(2,1)S(1)}, u32[]{:S(2)}, u32[]{:S(2)}) collective-permute-start(bf16[160,768]{1,0:T(8,128)(2,1)S(1)} %collective-permute-done.8.refs_3_), channel_id=1, source_target_pairs={{0,1},{1,0},{2,3},{3,2},{4,5},{5,4},{6,7},{7,6},{8,9},{9,8},{10,11... | collective-permute-start | bytes 737288 | tf_op jit(solution)/shard_map/ppermute | solution.py:34
  26.0 12.4 %collective-permute-start.13 = (bf16[160,768]{1,0:T(8,128)(2,1)S(1)}, bf16[160,768]{1,0:T(8,128)(2,1)S(1)}, u32[]{:S(2)}, u32[]{:S(2)}) collective-permute-start(bf16[160,768]{1,0:T(8,128)(2,1)S(1)} %collective-permute-done.11.refs_6_), channel_id=1, source_target_pairs={{0,2},{1,3},{2,0},{3,1},{4,6},{5,7},{6,4},{7,5},{8,10},{9,11},{10,... | collective-permute-start | bytes 737288 | tf_op jit(solution)/shard_map/ppermute | solution.py:34
  33.1 23.2 %copy-start.14 = (f32[768]{0:T(1024)S(1)}, f32[768]{0:T(1024)}, u32[]{:S(2)}) copy-start(f32[768]{0:T(1024)} %param.13) | copy-start | bytes 9220
  38.4 1.1 copy-start.12
  41.8 21.8 %copy-start.3 = (f32[256,768]{1,0:T(8,128)S(1)}, f32[256,768]{1,0:T(8,128)}, u32[]{:S(2)}) copy-start(f32[256,768]{1,0:T(8,128)} %get-tuple-element.31.refs_9_.refs_4_) | copy-start | bytes 2359300
  41.8 2.1 %collective-permute-start.14 = (f32[128,1280]{1,0:T(8,128)S(1)}, f32[128,1280]{1,0:T(8,128)S(1)}, u32[]{:S(2)}, u32[]{:S(2)}) collective-permute-start(f32[128,1280]{1,0:T(8,128)S(1)} %get-tuple-element.33), channel_id=1, source_target_pairs={{0,8},{8,0},{16,24},{24,16},{1,9},{9,1},{17,25},{25,17},{2,10},{10... | collective-permute-start | bytes 1966088 | tf_op jit(solution)/shard_map/ppermute | solution.py:34
  44.0 16.8 %collective-permute-start.15 = (f32[128,1280]{1,0:T(8,128)S(1)}, f32[128,1280]{1,0:T(8,128)S(1)}, u32[]{:S(2)}, u32[]{:S(2)}) collective-permute-start(f32[128,1280]{1,0:T(8,128)S(1)} %add.82.ours), channel_id=1, source_target_pairs={{0,16},{8,24},{16,0},{24,8},{1,17},{9,25},{17,1},{25,9},{2,18},{10... | collective-permute-start | bytes 1966088 | tf_op jit(solution)/shard_map/ppermute | solution.py:34
  45.3 8.8 %collective-permute-start.1 = (bf16[160,768]{1,0:T(8,128)(2,1)S(1)}, bf16[160,768]{1,0:T(8,128)(2,1)S(1)}, u32[]{:S(2)}, u32[]{:S(2)}) collective-permute-start(bf16[160,768]{1,0:T(8,128)(2,1)S(1)} %convert_bitcast_fusion.1.refs_1_), channel_id=1, source_target_pairs={{0,2},{1,3},{2,0},{3,1},{4,6},{5,7},{6,4},{7,5},{8,10},{9,11},{10,... | collective-permute-start | bytes 737288 | tf_op jit(solution)/shard_map/ppermute | solution.py:34
  45.3 10.4 %collective-permute-start.4 = (bf16[160,768]{1,0:T(8,128)(2,1)S(1)}, bf16[160,768]{1,0:T(8,128)(2,1)S(1)}, u32[]{:S(2)}, u32[]{:S(2)}) collective-permute-start(bf16[160,768]{1,0:T(8,128)(2,1)S(1)} %collective-permute-done.3.refs_5_), channel_id=1, source_target_pairs={{0,1},{1,0},{2,3},{3,2},{4,5},{5,4},{6,7},{7,6},{8,9},{9,8},{10,11... | collective-permute-start | bytes 737288 | tf_op jit(solution)/shard_map/ppermute | solution.py:34
  46.9 12.6 %collective-permute-start = (bf16[160,768]{1,0:T(8,128)(2,1)S(1)}, bf16[160,768]{1,0:T(8,128)(2,1)S(1)}, u32[]{:S(2)}, u32[]{:S(2)}) collective-permute-start(bf16[160,768]{1,0:T(8,128)(2,1)S(1)} %convert_bitcast_fusion.1.refs_1_), channel_id=1, source_target_pairs={{0,1},{1,0},{2,3},{3,2},{4,5},{5,4},{6,7},{7,6},{8,9},{9,8},{10,11... | collective-permute-start | bytes 737288 | tf_op jit(solution)/shard_map/ppermute | solution.py:34
  47.4 12.1 %collective-permute-start.5 = (bf16[160,768]{1,0:T(8,128)(2,1)S(1)}, bf16[160,768]{1,0:T(8,128)(2,1)S(1)}, u32[]{:S(2)}, u32[]{:S(2)}) collective-permute-start(bf16[160,768]{1,0:T(8,128)(2,1)S(1)} %collective-permute-done.3.refs_5_), channel_id=1, source_target_pairs={{0,2},{1,3},{2,0},{3,1},{4,6},{5,7},{6,4},{7,5},{8,10},{9,11},{10,... | collective-permute-start | bytes 737288 | tf_op jit(solution)/shard_map/ppermute | solution.py:34
  54.2 9.4 %collective-permute-start.2 = (bf16[160,768]{1,0:T(8,128)(2,1)S(1)}, bf16[160,768]{1,0:T(8,128)(2,1)S(1)}, u32[]{:S(2)}, u32[]{:S(2)}) collective-permute-start(bf16[160,768]{1,0:T(8,128)(2,1)S(1)} %collective-permute-done.1.refs_3_), channel_id=1, source_target_pairs={{0,1},{1,0},{2,3},{3,2},{4,5},{5,4},{6,7},{7,6},{8,9},{9,8},{10,11... | collective-permute-start | bytes 737288 | tf_op jit(solution)/shard_map/ppermute | solution.py:34
  55.7 7.9 %collective-permute-start.6 = (bf16[160,768]{1,0:T(8,128)(2,1)S(1)}, bf16[160,768]{1,0:T(8,128)(2,1)S(1)}, u32[]{:S(2)}, u32[]{:S(2)}) collective-permute-start(bf16[160,768]{1,0:T(8,128)(2,1)S(1)} %collective-permute-done.4.refs_6_), channel_id=1, source_target_pairs={{0,2},{1,3},{2,0},{3,1},{4,6},{5,7},{6,4},{7,5},{8,10},{9,11},{10,... | collective-permute-start | bytes 737288 | tf_op jit(solution)/shard_map/ppermute | solution.py:34
  60.9 7.8 %copy-start.1 = (bf16[1,1280,1280]{2,1,0:T(8,128)(2,1)S(1)}, bf16[1,1280,1280]{2,1,0:T(8,128)(2,1)}, u32[]{:S(2)}) copy-start(bf16[1,1280,1280]{2,1,0:T(8,128)(2,1)} %param.11) | copy-start | bytes 9830404
  65.1 3.5 %copy-start = (bf16[1,1280,1280]{2,1,0:T(8,128)(2,1)S(1)}, bf16[1,1280,1280]{2,1,0:T(8,128)(2,1)}, u32[]{:S(2)}) copy-start(bf16[1,1280,1280]{2,1,0:T(8,128)(2,1)} %param.10) | copy-start | bytes 9830404
  65.1 2.2 %collective-permute-start.16 = (f32[128,1280]{1,0:T(8,128)S(1)}, f32[128,1280]{1,0:T(8,128)S(1)}, u32[]{:S(2)}, u32[]{:S(2)}) collective-permute-start(f32[128,1280]{1,0:T(8,128)S(1)} %get-tuple-element.35), channel_id=1, source_target_pairs={{0,8},{8,0},{16,24},{24,16},{1,9},{9,1},{17,25},{25,17},{2,10},{10... | collective-permute-start | bytes 1966088 | tf_op jit(solution)/shard_map/ppermute | solution.py:34
  65.2 3.4 %collective-permute-start.19 = (bf16[128,1280]{1,0:T(8,128)(2,1)S(1)}, bf16[128,1280]{1,0:T(8,128)(2,1)S(1)}, u32[]{:S(2)}, u32[]{:S(2)}) collective-permute-start(bf16[128,1280]{1,0:T(8,128)(2,1)S(1)} %shard_map.103.refs_1_), channel_id=1, source_target_pairs={{0,8},{8,0},{16,24},{24,16},{1,9},{9,1},{17,25},{25,17},{2,10},{10... | collective-permute-start | bytes 983048 | tf_op jit(solution)/shard_map/ppermute | solution.py:34
  67.8 10.5 %collective-permute-start.17 = (f16[128,1408]{1,0:T(8,128)(2,1)S(1)}, f16[128,1408]{1,0:T(8,128)(2,1)S(1)}, u32[]{:S(2)}, u32[]{:S(2)}) collective-permute-start(f16[128,1408]{1,0:T(8,128)(2,1)S(1)} %pad_maximum_fusion), channel_id=1, source_target_pairs={{0,16},{8,24},{16,0},{24,8},{1,17},{9,25},{17,1},{25,9},{2,18},{10... | collective-permute-start | bytes 1081352 | tf_op jit(solution)/shard_map/ppermute | solution.py:34
  71.8 7.2 %copy-start.6 = (bf16[256,1280]{1,0:T(8,128)(2,1)}, bf16[256,1280]{1,0:T(8,128)(2,1)S(1)}, u32[]{:S(2)}) copy-start(bf16[256,1280]{1,0:T(8,128)(2,1)S(1)} %get-tuple-element.56.left) | copy-start | bytes 1966084
  71.9 6.9 %collective-permute-start.22 = (f32[128,1280]{1,0:T(8,128)S(1)}, f32[128,1280]{1,0:T(8,128)S(1)}, u32[]{:S(2)}, u32[]{:S(2)}) collective-permute-start(f32[128,1280]{1,0:T(8,128)S(1)} %get-tuple-element.40), channel_id=1, source_target_pairs={{0,8},{8,0},{16,24},{24,16},{1,9},{9,1},{17,25},{25,17},{2,10},{10... | collective-permute-start | bytes 1966088 | tf_op jit(solution)/shard_map/ppermute | solution.py:34
  78.6 1.7 %collective-permute-start.18 = (bf16[128,1280]{1,0:T(8,128)(2,1)S(1)}, bf16[128,1280]{1,0:T(8,128)(2,1)S(1)}, u32[]{:S(2)}, u32[]{:S(2)}) collective-permute-start(bf16[128,1280]{1,0:T(8,128)(2,1)S(1)} %add_convert_fusion.1.refs_1_), channel_id=1, source_target_pairs={{0,8},{8,0},{16,24},{24,16},{1,9},{9,1},{17,25},{25,17},{2,10},{10... | collective-permute-start | bytes 983048 | tf_op jit(solution)/shard_map/ppermute | solution.py:34
  79.2 10.9 %collective-permute-start.23 = (f16[128,1408]{1,0:T(8,128)(2,1)S(1)}, f16[128,1408]{1,0:T(8,128)(2,1)S(1)}, u32[]{:S(2)}, u32[]{:S(2)}) collective-permute-start(f16[128,1408]{1,0:T(8,128)(2,1)S(1)} %pad_maximum_fusion.2), channel_id=1, source_target_pairs={{0,16},{8,24},{16,0},{24,8},{1,17},{9,25},{17,1},{25,9},{2,18},{10... | collective-permute-start | bytes 1081352 | tf_op jit(solution)/shard_map/ppermute | solution.py:34
  83.0 7.9 %copy-start.8 = (bf16[256,1280]{1,0:T(8,128)(2,1)}, bf16[256,1280]{1,0:T(8,128)(2,1)S(1)}, u32[]{:S(2)}) copy-start(bf16[256,1280]{1,0:T(8,128)(2,1)S(1)} %get-tuple-element.57.right) | copy-start | bytes 1966084
  83.0 7.9 %copy-start.10 = (bf16[256,1280]{1,0:T(8,128)(2,1)}, bf16[256,1280]{1,0:T(8,128)(2,1)S(1)}, u32[]{:S(2)}) copy-start(bf16[256,1280]{1,0:T(8,128)(2,1)S(1)} %get-tuple-element.55.right) | copy-start | bytes 1966084
  83.0 7.5 %collective-permute-start.20 = (f32[128,1280]{1,0:T(8,128)S(1)}, f32[128,1280]{1,0:T(8,128)S(1)}, u32[]{:S(2)}, u32[]{:S(2)}) collective-permute-start(f32[128,1280]{1,0:T(8,128)S(1)} %get-tuple-element.38), channel_id=1, source_target_pairs={{0,8},{8,0},{16,24},{24,16},{1,9},{9,1},{17,25},{25,17},{2,10},{10... | collective-permute-start | bytes 1966088 | tf_op jit(solution)/shard_map/ppermute | solution.py:34
  90.5 1.7 %collective-permute-start.24 = (bf16[128,1280]{1,0:T(8,128)(2,1)S(1)}, bf16[128,1280]{1,0:T(8,128)(2,1)S(1)}, u32[]{:S(2)}, u32[]{:S(2)}) collective-permute-start(bf16[128,1280]{1,0:T(8,128)(2,1)S(1)} %add_convert_fusion.refs_1_), channel_id=1, source_target_pairs={{0,8},{8,0},{16,24},{24,16},{1,9},{9,1},{17,25},{25,17},{2,10},{10... | collective-permute-start | bytes 983048 | tf_op jit(solution)/shard_map/ppermute | solution.py:34
  91.1 14.0 %collective-permute-start.21 = (f16[128,1408]{1,0:T(8,128)(2,1)S(1)}, f16[128,1408]{1,0:T(8,128)(2,1)S(1)}, u32[]{:S(2)}, u32[]{:S(2)}) collective-permute-start(f16[128,1408]{1,0:T(8,128)(2,1)S(1)} %pad_maximum_fusion.1), channel_id=1, source_target_pairs={{0,16},{8,24},{16,0},{24,8},{1,17},{9,25},{17,1},{25,9},{2,18},{10... | collective-permute-start | bytes 1081352 | tf_op jit(solution)/shard_map/ppermute | solution.py:34
  93.5 12.8 %copy-start.4 = (f32[256,768]{1,0:T(8,128)}, f32[256,768]{1,0:T(8,128)S(1)}, u32[]{:S(2)}) copy-start(f32[256,768]{1,0:T(8,128)S(1)} %get-tuple-element.44.refs_7_) | copy-start | bytes 2359300
  93.5 14.8 %copy-start.2 = (bf16[1280,768]{1,0:T(8,128)(2,1)S(1)}, bf16[1280,768]{1,0:T(8,128)(2,1)}, u32[]{:S(2)}) copy-start(bf16[1280,768]{1,0:T(8,128)(2,1)} %get-tuple-element.43.refs_3_) | copy-start | bytes 5898244
  93.5 3.7 %collective-permute-start.25 = (f32[1,768]{1,0:T(1,128)S(1)}, f32[1,768]{1,0:T(1,128)S(1)}, u32[]{:S(2)}, u32[]{:S(2)}) collective-permute-start(f32[1,768]{1,0:T(1,128)S(1)} %get-tuple-element.42), channel_id=1, source_target_pairs={{0,1},{1,0},{2,3},{3,2},{4,5},{5,4},{6,7},{7,6},{8,9},{9,8},{10,11... | collective-permute-start | bytes 9224 | tf_op jit(solution)/shard_map/ppermute | solution.py:34
  97.1 5.4 %collective-permute-start.28 = (f32[1,768]{1,0:T(1,128)S(1)}, f32[1,768]{1,0:T(1,128)S(1)}, u32[]{:S(2)}, u32[]{:S(2)}) collective-permute-start(f32[1,768]{1,0:T(1,128)S(1)} %add.88), channel_id=1, source_target_pairs={{0,6},{1,7},{2,4},{3,5},{4,2},{5,3},{6,0},{7,1},{8,14},{9,15},{10,... | collective-permute-start | bytes 9224 | tf_op jit(solution)/shard_map/ppermute | solution.py:34
  100.6 4.5 %collective-permute-start.27 = (f32[1,768]{1,0:T(1,128)S(1)}, f32[1,768]{1,0:T(1,128)S(1)}, u32[]{:S(2)}, u32[]{:S(2)}) collective-permute-start(f32[1,768]{1,0:T(1,128)S(1)} %add.88), channel_id=1, source_target_pairs={{0,4},{1,5},{2,6},{3,7},{4,0},{5,1},{6,2},{7,3},{8,12},{9,13},{10,... | collective-permute-start | bytes 9224 | tf_op jit(solution)/shard_map/ppermute | solution.py:34
  101.0 4.1 %collective-permute-start.26 = (f32[1,768]{1,0:T(1,128)S(1)}, f32[1,768]{1,0:T(1,128)S(1)}, u32[]{:S(2)}, u32[]{:S(2)}) collective-permute-start(f32[1,768]{1,0:T(1,128)S(1)} %add.88), channel_id=1, source_target_pairs={{0,2},{1,3},{2,0},{3,1},{4,6},{5,7},{6,4},{7,5},{8,10},{9,11},{10,... | collective-permute-start | bytes 9224 | tf_op jit(solution)/shard_map/ppermute | solution.py:34
  106.2 2.0 %collective-permute-start.29 = (bf16[128,1280]{1,0:T(8,128)(2,1)}, bf16[128,1280]{1,0:T(8,128)(2,1)}, u32[]{:S(2)}, u32[]{:S(2)}) collective-permute-start(bf16[128,1280]{1,0:T(8,128)(2,1)} %shard_map.108.refs_1_), channel_id=1, source_target_pairs={{0,8},{8,0},{16,24},{24,16},{1,9},{9,1},{17,25},{25,17},{2,10},{10... | collective-permute-start | bytes 983048 | tf_op jit(solution)/shard_map/ppermute | solution.py:34
  108.2 1.1 copy-start.5
  109.4 1.1 copy-start.13
  113.8 9.4 %collective-permute-start.31 = (bf16[160,768]{1,0:T(8,128)(2,1)S(1)}, bf16[160,768]{1,0:T(8,128)(2,1)S(1)}, u32[]{:S(2)}, u32[]{:S(2)}) collective-permute-start(bf16[160,768]{1,0:T(8,128)(2,1)S(1)} %get-tuple-element.49), channel_id=1, source_target_pairs={{0,1},{1,0},{2,3},{3,2},{4,5},{5,4},{6,7},{7,6},{8,9},{9,8},{10,11... | collective-permute-start | bytes 737288 | tf_op jit(solution)/shard_map/ppermute | solution.py:34
  115.4 3.4 %copy-start.11 = (bf16[256,1280]{1,0:T(8,128)(2,1)S(1)}, bf16[256,1280]{1,0:T(8,128)(2,1)}, u32[]{:S(2)}) copy-start(bf16[256,1280]{1,0:T(8,128)(2,1)} %copy-done.10) | copy-start | bytes 1966084
  116.1 23.6 %collective-permute-start.30 = (bf16[160,768]{1,0:T(8,128)(2,1)S(1)}, bf16[160,768]{1,0:T(8,128)(2,1)S(1)}, u32[]{:S(2)}, u32[]{:S(2)}) collective-permute-start(bf16[160,768]{1,0:T(8,128)(2,1)S(1)} %get-tuple-element.47), channel_id=1, source_target_pairs={{0,1},{1,0},{2,3},{3,2},{4,5},{5,4},{6,7},{7,6},{8,9},{9,8},{10,11... | collective-permute-start | bytes 737288 | tf_op jit(solution)/shard_map/ppermute | solution.py:34
  116.7 8.9 %collective-permute-start.33 = (bf16[160,768]{1,0:T(8,128)(2,1)S(1)}, bf16[160,768]{1,0:T(8,128)(2,1)S(1)}, u32[]{:S(2)}, u32[]{:S(2)}) collective-permute-start(bf16[160,768]{1,0:T(8,128)(2,1)S(1)} %get-tuple-element.52), channel_id=1, source_target_pairs={{0,2},{1,3},{2,0},{3,1},{4,6},{5,7},{6,4},{7,5},{8,10},{9,11},{10,... | collective-permute-start | bytes 737288 | tf_op jit(solution)/shard_map/ppermute | solution.py:34
  117.6 13.3 %collective-permute-start.35 = (bf16[160,768]{1,0:T(8,128)(2,1)S(1)}, bf16[160,768]{1,0:T(8,128)(2,1)S(1)}, u32[]{:S(2)}, u32[]{:S(2)}) collective-permute-start(bf16[160,768]{1,0:T(8,128)(2,1)S(1)} %get-tuple-element.53), channel_id=1, source_target_pairs={{0,2},{1,3},{2,0},{3,1},{4,6},{5,7},{6,4},{7,5},{8,10},{9,11},{10,... | collective-permute-start | bytes 737288 | tf_op jit(solution)/shard_map/ppermute | solution.py:34
  118.8 8.5 %collective-permute-start.37 = (bf16[2,320,256]{2,1,0:T(8,128)(2,1)S(1)}, bf16[2,320,256]{2,1,0:T(8,128)(2,1)S(1)}, u32[]{:S(2)}, u32[]{:S(2)}) collective-permute-start(bf16[2,320,256]{2,1,0:T(8,128)(2,1)S(1)} %fusion), channel_id=1, source_target_pairs={{0,8},{8,0},{16,24},{24,16},{1,9},{9,1},{17,25},{25,17},{2,10},{10... | collective-permute-start | bytes 983048 | tf_op jit(solution)/shard_map/ppermute | solution.py:34
  123.3 16.4 %collective-permute-start.32 = (bf16[160,768]{1,0:T(8,128)(2,1)S(1)}, bf16[160,768]{1,0:T(8,128)(2,1)S(1)}, u32[]{:S(2)}, u32[]{:S(2)}) collective-permute-start(bf16[160,768]{1,0:T(8,128)(2,1)S(1)} %add_convert_fusion.4), channel_id=1, source_target_pairs={{0,2},{1,3},{2,0},{3,1},{4,6},{5,7},{6,4},{7,5},{8,10},{9,11},{10,... | collective-permute-start | bytes 737288 | tf_op jit(solution)/shard_map/ppermute | solution.py:34
  125.6 9.0 %copy-start.7 = (bf16[256,1280]{1,0:T(8,128)(2,1)S(1)}, bf16[256,1280]{1,0:T(8,128)(2,1)}, u32[]{:S(2)}) copy-start(bf16[256,1280]{1,0:T(8,128)(2,1)} %copy-done.6) | copy-start | bytes 1966084
  125.6 9.0 %copy-start.9 = (bf16[256,1280]{1,0:T(8,128)(2,1)S(1)}, bf16[256,1280]{1,0:T(8,128)(2,1)}, u32[]{:S(2)}) copy-start(bf16[256,1280]{1,0:T(8,128)(2,1)} %copy-done.8) | copy-start | bytes 1966084
  125.7 6.8 %collective-permute-start.34 = (bf16[160,768]{1,0:T(8,128)(2,1)S(1)}, bf16[160,768]{1,0:T(8,128)(2,1)S(1)}, u32[]{:S(2)}, u32[]{:S(2)}) collective-permute-start(bf16[160,768]{1,0:T(8,128)(2,1)S(1)} %add_convert_fusion.3), channel_id=1, source_target_pairs={{0,1},{1,0},{2,3},{3,2},{4,5},{5,4},{6,7},{7,6},{8,9},{9,8},{10,11... | collective-permute-start | bytes 737288 | tf_op jit(solution)/shard_map/ppermute | solution.py:34
  127.4 11.6 %collective-permute-start.38 = (bf16[320,256]{1,0:T(8,128)(2,1)S(1)}, bf16[320,256]{1,0:T(8,128)(2,1)S(1)}, u32[]{:S(2)}, u32[]{:S(2)}) collective-permute-start(bf16[320,256]{1,0:T(8,128)(2,1)S(1)} %fusion.1), channel_id=1, source_target_pairs={{0,16},{8,24},{16,0},{24,8},{1,17},{9,25},{17,1},{25,9},{2,18},{10... | collective-permute-start | bytes 491528 | tf_op jit(solution)/shard_map/ppermute | solution.py:34
  132.5 12.0 %collective-permute-start.36 = (bf16[160,768]{1,0:T(8,128)(2,1)S(1)}, bf16[160,768]{1,0:T(8,128)(2,1)S(1)}, u32[]{:S(2)}, u32[]{:S(2)}) collective-permute-start(bf16[160,768]{1,0:T(8,128)(2,1)S(1)} %add_convert_fusion.2), channel_id=1, source_target_pairs={{0,4},{1,5},{2,6},{3,7},{4,0},{5,1},{6,2},{7,3},{8,12},{9,13},{10,... | collective-permute-start | bytes 737288 | tf_op jit(solution)/shard_map/ppermute | solution.py:34
